TPU v7x, 32 devices: a whole 2x2x4 slice. The times are simulated.
32 devices in a mesh: seq: 8 (over y, x, core), section: 4 (over z).
Axes of the slice: x: 2, y: 2, z: 4, core: 2. Of those that a mesh axis runs over, the one named last changes fastest.
Arguments:
- queries: bfloat16 [1024, 2048], P('seq', 'section'), may hold values from -10 to 10
- keys: bfloat16 [1024, 512], P('seq', 'section'), may hold values from -10 to 10
- values: bfloat16 [1024, 512], P('seq', 'section'), may hold values from -18 to 18
- residual: bfloat16 [1024, 8192], P(None, 'seq'), may hold values from -8 to 8
- out_weight: bfloat16 [2048, 8192], P('section', 'seq'), may hold values from -0.125 to 0.125
- norm_gain: float32 [8192], P('seq'), may hold values from 0.1 to 1.9
- in_weight: bfloat16 [8192, 2, 8, 256], P('seq', None, None, 'section'), may hold values from -0.09375 to 0.09375
- conv_weight: float32 [2048, 4], P(('seq', 'section')), may hold values from -3 to 3
- conv_bias: float32 [2048], P(('seq', 'section')), may hold values from -0.5 to 0.5
- proj_weight: bfloat16 [2048, 272], P(('seq', 'section')), may hold values from -0.125 to 0.125
- dt_weight: bfloat16 [256, 2048], P(None, ('seq', 'section')), may hold values from -0.375 to 0.375
- dt_bias: float32 [2048], P(('seq', 'section')), may hold values from -3 to 0
- a_log: float32 [2048, 8], P(('seq', 'section')), may hold values from -7 to 0
- skip_gain: float32 [2048], P(('seq', 'section')), may hold values from -2.5 to 2.5
Outputs:
- mixer_out: bfloat16 [2048, 1024], P(('seq', 'section'))
All inputs are finite; a program needn't handle non-finite values.
Results may differ from a plain program's by a relative error of at most 0.03.
Values may be sent and summed in bfloat16 or wider, within the bound.
No kernel may reach another device: no remote copies, remote signals or barrier semaphores. Data moves between devices by JAX's collectives and lax.ppermute only.
A program may use at most 128 MiB of HBM per device.

v0:
```python
import math

import jax
import jax.numpy as jnp
from jax import lax
from jax.sharding import PartitionSpec as P

D = 8192
HD = 128
GROUP = 4
NST = 8
DT_RANK = 256
CONV = 4
SCAN_BLOCK = 128


norm_eps = 1e-05


def fold_half(carried, query_part, query_first, key_part, value_part, first_row):
    half_rows = query_part.shape[0]
    key_count = key_part.shape[0]
    heads_kv = key_part.shape[1] // HD
    key_heads = key_part.reshape(key_count, heads_kv, HD)
    value_heads = value_part.reshape(key_count, heads_kv, HD)
    query_pos = query_first + jnp.arange(half_rows, dtype=jnp.int32)
    key_pos = jnp.arange(key_count, dtype=jnp.int32)

    def update(previous):
        running_max, weight_sum, accumulated = previous
        scores = jnp.einsum(
            "qhgd,khd->hgqk", query_part, key_heads, preferred_element_type=jnp.float32
        ) / math.sqrt(HD)
        allowed = query_pos[:, None] >= key_pos[None, :]
        scores = jnp.where(allowed, scores, -1e30)
        new_max = jnp.maximum(running_max, jnp.max(scores, axis=3))
        exponent_terms = jnp.where(allowed, jnp.exp(scores - new_max[..., None]), 0.0)
        weight_sum = jnp.sum(exponent_terms, axis=3)
        weights_bf = exponent_terms.astype(jnp.bfloat16)
        moved = jnp.einsum(
            "hgqk,khd->qhgd", weights_bf, value_heads, preferred_element_type=jnp.float32
        )
        accumulated = moved
        return (new_max, weight_sum, accumulated)

    def unchanged(previous):
        return previous

    return lax.cond(first_row <= query_first + half_rows - 1, update, unchanged, carried)


def finish_half(carried):
    running_max, weight_sum, accumulated = carried
    result = accumulated / jnp.transpose(weight_sum, (2, 0, 1))[..., None]
    return result.astype(jnp.bfloat16).reshape(result.shape[0], -1)


def body(
    queries,
    keys,
    values,
    residual,
    out_weight,
    norm_gain,
    in_weight,
    conv_weight,
    conv_bias,
    proj_weight,
    dt_weight,
    dt_bias,
    a_log,
    skip_gain,
):
    tok_rows = queries.shape[0]
    half_rows = tok_rows // 2
    heads_kv = keys.shape[1] // HD
    seq_rank = lax.axis_index("seq")
    query_halves = queries.reshape(2, half_rows, heads_kv, GROUP, HD)
    first_half = query_halves[0]
    second_half = query_halves[1]
    first_first = seq_rank * tok_rows
    second_first = seq_rank * tok_rows + half_rows
    start_state = (
        jnp.full((heads_kv, GROUP, half_rows), -1e30, jnp.float32),
        jnp.zeros((heads_kv, GROUP, half_rows), jnp.float32),
        jnp.zeros((half_rows, heads_kv, GROUP, HD), jnp.float32),
    )
    carried = (start_state, start_state)
    first_row = jnp.int32(0)
    key_part = lax.all_gather(keys, "seq", axis=0, tiled=True)
    value_part = lax.all_gather(values, "seq", axis=0, tiled=True)
    first_out = finish_half(
        fold_half(carried[0], first_half, first_first, key_part, value_part, first_row)
    )
    second_out = finish_half(
        fold_half(carried[1], second_half, second_first, key_part, value_part, first_row)
    )
    attended = jnp.concatenate([first_out, second_out], axis=0)
    branch_part = jnp.dot(
        lax.all_gather(attended, "seq", axis=0, tiled=True),
        out_weight,
        preferred_element_type=jnp.float32,
    )
    branch_total = lax.psum(branch_part.astype(jnp.bfloat16), "section").astype(jnp.float32)
    hidden = residual.astype(jnp.float32) + branch_total
    squares = lax.psum(jnp.sum(hidden * hidden, axis=1), "seq")
    inv_rms = lax.rsqrt(squares / D + norm_eps)
    normed = (hidden * inv_rms[:, None] * norm_gain[None, :]).astype(jnp.bfloat16)
    seq_len = normed.shape[0]
    channels = conv_weight.shape[0]
    columns = lax.all_to_all(in_weight, "seq", split_axis=2, concat_axis=0, tiled=True)
    column_rows = columns.reshape(columns.shape[0], 2, channels)
    feature_width = normed.shape[1]
    shard_piece = lax.all_gather(normed, "seq", axis=1, tiled=True)
    block_count = shard_piece.shape[1] // feature_width

    def add_one(block_index, inner):
        rows = lax.dynamic_slice_in_dim(shard_piece, block_index * feature_width, feature_width, 1)
        block_weight = lax.dynamic_slice_in_dim(
            column_rows, block_index * feature_width, feature_width, 0
        )
        partial_sum = jnp.einsum(
            "ld,dkc->kcl", rows, block_weight, preferred_element_type=jnp.float32
        )
        rounded = lax.optimization_barrier(partial_sum.astype(jnp.bfloat16))
        return inner + rounded.astype(jnp.float32)

    mixed_in = lax.fori_loop(
        0, block_count, add_one, jnp.zeros((2, channels, seq_len), jnp.float32)
    )
    x_path = mixed_in[0]
    z_gate = mixed_in[1]
    padded = jnp.pad(x_path, ((0, 0), (CONV - 1, 0)))
    conv_out = conv_bias[:, None] + jnp.zeros((channels, seq_len), jnp.float32)
    for offset in range(CONV):
        conv_out = (
            conv_out + conv_weight[:, offset : offset + 1] * padded[:, offset : offset + seq_len]
        )
    inputs = jax.nn.silu(conv_out).astype(jnp.bfloat16)
    local_proj = jnp.einsum("cr,cl->rl", proj_weight, inputs, preferred_element_type=jnp.float32)
    projected = lax.psum(local_proj, ("seq", "section"))
    low_rank = projected[:DT_RANK].astype(jnp.bfloat16)
    in_map = projected[DT_RANK : DT_RANK + NST]
    out_map = projected[DT_RANK + NST :]
    step_size = jax.nn.softplus(
        jnp.einsum("rc,rl->cl", dt_weight, low_rank, preferred_element_type=jnp.float32)
        + dt_bias[:, None]
    )
    decay = -jnp.exp(a_log)
    inputs_float = inputs.astype(jnp.float32)
    block_total = seq_len // SCAN_BLOCK

    def split_blocks(matrix):
        return jnp.moveaxis(matrix.reshape(matrix.shape[0], block_total, SCAN_BLOCK), 1, 0)

    def combine(earlier, later):
        return (earlier[0] * later[0], earlier[1] * later[0] + later[1])

    def scan_block(carried, block_inputs):
        step_block, input_block, in_block, out_block = block_inputs
        factor = jnp.exp(step_block[:, None, :] * decay[:, :, None])
        source = (step_block * input_block)[:, None, :] * in_block[None, :, :]
        cum_factor, cum_source = lax.associative_scan(combine, (factor, source), axis=2)
        states = cum_factor * carried[:, :, None] + cum_source
        readout = jnp.sum(states * out_block[None, :, :], axis=1)
        return (states[:, :, -1], readout)

    block_inputs = (
        split_blocks(step_size),
        split_blocks(inputs_float),
        split_blocks(in_map),
        split_blocks(out_map),
    )
    final_state, readouts = lax.scan(
        scan_block, jnp.zeros((channels, NST), jnp.float32), block_inputs
    )
    readout = jnp.moveaxis(readouts, 0, 1).reshape(channels, seq_len)
    return ((readout + skip_gain[:, None] * inputs_float) * jax.nn.silu(z_gate)).astype(
        jnp.bfloat16
    )


def solution(mesh):
    return jax.shard_map(
        body,
        mesh=mesh,
        in_specs=(
            P("seq", "section"),
            P("seq", "section"),
            P("seq", "section"),
            P(None, "seq"),
            P("section", "seq"),
            P("seq"),
            P("seq", None, None, "section"),
            P(("seq", "section"), None),
            P(("seq", "section")),
            P(("seq", "section"), None),
            P(None, ("seq", "section")),
            P(("seq", "section")),
            P(("seq", "section"), None),
            P(("seq", "section")),
        ),
        out_specs=P(("seq", "section"), None),
        check_vma=False,
    )
```

profile of v0, /device:TPU:0, one launch (start us, length us, event | category | flops | bytes accessed | tf_op | source)
XLA Modules:
  0.0 847.0 jit_solution(9445198959120966518)
XLA Ops:
  32.1 23.9 %all-gather.3.cloned.1.call-done = bf16[1024,512]{1,0:T(8,128)(2,1)} async-done(((bf16[128,512]{1,0:T(8,128)(2,1)}), bf16[1024,512]{1,0:T(8,128)(2,1)}) %all-gather.3.cloned.1.call-update) | async-done | bytes 1048592 | tf_op jit(solution)/shard_map/all_gather | solution.py:100
  59.8 86.6 %all-reduce.32.cloned.1.call-done = bf16[1024,1024]{1,0:T(8,128)(2,1)} async-done(((bf16[1024,1024]{1,0:T(8,128)(2,1)}), bf16[1024,1024]{1,0:T(8,128)(2,1)}) %all-reduce.32.cloned.1.call-update) | async-done | bytes 2097168 | tf_op jit(solution)/shard_map/psum | solution.py:104
  149.4 13.7 %psum.22 = f32[1024]{0:T(1024)S(1)} all-reduce(f32[1024]{0:T(1024)S(1)} %multiply_reduce_fusion.1), channel_id=1, replica_groups=mesh['seq'=8,'section'=4] {'seq'}, use_global_device_ids=true, to_apply=%region_10.11 | all-reduce | flops 1024 | bytes 8192 | tf_op jit(solution)/shard_map/psum | solution.py:106
  175.4 47.2 %all-to-all-done = bf16[1024,2,8,64]{0,3,1,2:T(8,128)(2,1)} async-done(((bf16[1024,2,8,64]{0,3,1,2:T(8,128)(2,1)}), bf16[1024,2,8,64]{0,3,1,2:T(8,128)(2,1)}, u32[]{:S(2)}, u32[]{:S(2)}) %all-to-all-start) | async-done | bytes 2097184 | tf_op jit(solution)/shard_map/all_to_all | solution.py:111
  231.2 45.4 %all-gather.5.cloned.1.call-done = bf16[1024,8192]{1,0:T(8,128)(2,1)} async-done(((bf16[1024,1024]{1,0:T(8,128)(2,1)}), bf16[1024,8192]{1,0:T(8,128)(2,1)}) %all-gather.5.cloned.1.call-update) | async-done | bytes 16777232 | tf_op jit(solution)/shard_map/all_gather | solution.py:114
  276.6 21.9 %while.27 = (s32[]{:T(128)}, f32[2,64,1024]{2,1,0:T(8,128)S(1)}, bf16[8192,2,64]{0,2,1:T(8,128)(2,1)}, bf16[1024,8192]{1,0:T(8,128)(2,1)}, s32[]{:T(128)}, /*index=5*/s32[]{:T(128)}, s32[]{:T(128)}, s32[]{:T(128)}) while((s32[]{:T(128)}, f32[2,64,1024]{2,1,0:T(8,128)S(1)}, bf16[8192,2,64]{0,2,1:T(8,128)(2,1)}, ...), condition=%wide.region_12.13_spmd.clone, body=%wide.region_11.12_spmd.clone.sunk | while | flops 268959744 | bytes 3933325 | solution.py:128
  301.0 129.6 %all-reduce.34.cloned.1.call-done = f32[272,1024]{1,0:T(8,128)} async-done(((f32[272,1024]{1,0:T(8,128)}), f32[272,1024]{1,0:T(8,128)}) %all-reduce.34.cloned.1.call-update) | async-done | bytes 1114128 | tf_op jit(solution)/shard_map/psum | solution.py:141
  434.3 403.1 %while.26 = (s32[]{:T(128)}, f32[64,8]{0,1:T(8,128)S(1)}, f32[8,64,128]{1,2,0:T(8,128)}, f32[8,64,128]{2,1,0:T(8,128)}, f32[64,8]{0,1:T(8,128)S(1)}, /*index=5*/...) while((s32[]{:T(128)}, f32[64,8]{0,1:T(8,128)S(1)}, ...), condition=%wide.region_16.17_spmd, body=%wide.region_14.16_spmd.sunk | while | flops 1284610 | bytes 13722377 | solution.py:174
  440.1 19.7 %pad.298 = f32[64,8,128]{0,1,2:T(8,128)} pad(f32[64,8,64]{0,1,2:T(8,128)S(1)} %add.446, f32[]{:T(128)} %constant.103.clone.1..sunk), padding=0_0_0x0_0_0x1_0_1 | pad | bytes 393220 | tf_op jit(solution)/shard_map/while/body/eval_jaxpr/pad | solution.py:163
  461.2 19.7 %pad.296 = f32[64,8,128]{0,1,2:T(8,128)} pad(f32[64,8,64]{0,1,2:T(8,128)S(1)} %add.445, f32[]{:T(128)} %constant.103.clone.1..sunk), padding=0_0_0x0_0_0x1_0_1 | pad | bytes 393220 | tf_op jit(solution)/shard_map/while/body/eval_jaxpr/pad | solution.py:163
  490.5 19.7 %pad.298 = f32[64,8,128]{0,1,2:T(8,128)} pad(f32[64,8,64]{0,1,2:T(8,128)S(1)} %add.446, f32[]{:T(128)} %constant.103.clone.1..sunk), padding=0_0_0x0_0_0x1_0_1 | pad | bytes 393220 | tf_op jit(solution)/shard_map/while/body/eval_jaxpr/pad | solution.py:163
  511.6 19.7 %pad.296 = f32[64,8,128]{0,1,2:T(8,128)} pad(f32[64,8,64]{0,1,2:T(8,128)S(1)} %add.445, f32[]{:T(128)} %constant.103.clone.1..sunk), padding=0_0_0x0_0_0x1_0_1 | pad | bytes 393220 | tf_op jit(solution)/shard_map/while/body/eval_jaxpr/pad | solution.py:163
  540.9 19.7 %pad.298 = f32[64,8,128]{0,1,2:T(8,128)} pad(f32[64,8,64]{0,1,2:T(8,128)S(1)} %add.446, f32[]{:T(128)} %constant.103.clone.1..sunk), padding=0_0_0x0_0_0x1_0_1 | pad | bytes 393220 | tf_op jit(solution)/shard_map/while/body/eval_jaxpr/pad | solution.py:163
  562.0 19.7 %pad.296 = f32[64,8,128]{0,1,2:T(8,128)} pad(f32[64,8,64]{0,1,2:T(8,128)S(1)} %add.445, f32[]{:T(128)} %constant.103.clone.1..sunk), padding=0_0_0x0_0_0x1_0_1 | pad | bytes 393220 | tf_op jit(solution)/shard_map/while/body/eval_jaxpr/pad | solution.py:163
  591.3 19.7 %pad.298 = f32[64,8,128]{0,1,2:T(8,128)} pad(f32[64,8,64]{0,1,2:T(8,128)S(1)} %add.446, f32[]{:T(128)} %constant.103.clone.1..sunk), padding=0_0_0x0_0_0x1_0_1 | pad | bytes 393220 | tf_op jit(solution)/shard_map/while/body/eval_jaxpr/pad | solution.py:163
  612.4 19.7 %pad.296 = f32[64,8,128]{0,1,2:T(8,128)} pad(f32[64,8,64]{0,1,2:T(8,128)S(1)} %add.445, f32[]{:T(128)} %constant.103.clone.1..sunk), padding=0_0_0x0_0_0x1_0_1 | pad | bytes 393220 | tf_op jit(solution)/shard_map/while/body/eval_jaxpr/pad | solution.py:163
  641.7 19.7 %pad.298 = f32[64,8,128]{0,1,2:T(8,128)} pad(f32[64,8,64]{0,1,2:T(8,128)S(1)} %add.446, f32[]{:T(128)} %constant.103.clone.1..sunk), padding=0_0_0x0_0_0x1_0_1 | pad | bytes 393220 | tf_op jit(solution)/shard_map/while/body/eval_jaxpr/pad | solution.py:163
  662.8 19.7 %pad.296 = f32[64,8,128]{0,1,2:T(8,128)} pad(f32[64,8,64]{0,1,2:T(8,128)S(1)} %add.445, f32[]{:T(128)} %constant.103.clone.1..sunk), padding=0_0_0x0_0_0x1_0_1 | pad | bytes 393220 | tf_op jit(solution)/shard_map/while/body/eval_jaxpr/pad | solution.py:163
  692.0 19.7 %pad.298 = f32[64,8,128]{0,1,2:T(8,128)} pad(f32[64,8,64]{0,1,2:T(8,128)S(1)} %add.446, f32[]{:T(128)} %constant.103.clone.1..sunk), padding=0_0_0x0_0_0x1_0_1 | pad | bytes 393220 | tf_op jit(solution)/shard_map/while/body/eval_jaxpr/pad | solution.py:163
  713.2 19.7 %pad.296 = f32[64,8,128]{0,1,2:T(8,128)} pad(f32[64,8,64]{0,1,2:T(8,128)S(1)} %add.445, f32[]{:T(128)} %constant.103.clone.1..sunk), padding=0_0_0x0_0_0x1_0_1 | pad | bytes 393220 | tf_op jit(solution)/shard_map/while/body/eval_jaxpr/pad | solution.py:163
  742.4 19.7 %pad.298 = f32[64,8,128]{0,1,2:T(8,128)} pad(f32[64,8,64]{0,1,2:T(8,128)S(1)} %add.446, f32[]{:T(128)} %constant.103.clone.1..sunk), padding=0_0_0x0_0_0x1_0_1 | pad | bytes 393220 | tf_op jit(solution)/shard_map/while/body/eval_jaxpr/pad | solution.py:163
  763.6 19.7 %pad.296 = f32[64,8,128]{0,1,2:T(8,128)} pad(f32[64,8,64]{0,1,2:T(8,128)S(1)} %add.445, f32[]{:T(128)} %constant.103.clone.1..sunk), padding=0_0_0x0_0_0x1_0_1 | pad | bytes 393220 | tf_op jit(solution)/shard_map/while/body/eval_jaxpr/pad | solution.py:163
  792.8 19.7 %pad.298 = f32[64,8,128]{0,1,2:T(8,128)} pad(f32[64,8,64]{0,1,2:T(8,128)S(1)} %add.446, f32[]{:T(128)} %constant.103.clone.1..sunk), padding=0_0_0x0_0_0x1_0_1 | pad | bytes 393220 | tf_op jit(solution)/shard_map/while/body/eval_jaxpr/pad | solution.py:163
  814.0 19.7 %pad.296 = f32[64,8,128]{0,1,2:T(8,128)} pad(f32[64,8,64]{0,1,2:T(8,128)S(1)} %add.445, f32[]{:T(128)} %constant.103.clone.1..sunk), padding=0_0_0x0_0_0x1_0_1 | pad | bytes 393220 | tf_op jit(solution)/shard_map/while/body/eval_jaxpr/pad | solution.py:163
  (772 shorter events, 172.2 us)
Async XLA Ops:
  6.5 49.4 %copy-start = (bf16[512,1024]{1,0:T(8,128)(2,1)S(1)}, bf16[512,1024]{1,0:T(8,128)(2,1)}, u32[]{:S(2)}) copy-start(bf16[512,1024]{1,0:T(8,128)(2,1)} %param.26) | copy-start | bytes 3145732
  6.5 49.4 %all-gather.3.cloned.1.call-start = ((), (), s32[]{:S(2)}) async-start(), calls=%async_computation.1 | async-start | bytes 1179648 | tf_op jit(solution)/shard_map/all_gather | solution.py:100
  32.0 114.4 %all-reduce.32.cloned.1.call-start = ((), (), s32[]{:S(2)}) async-start(), calls=%async_computation.2 | async-start | bytes 4194304 | tf_op jit(solution)/shard_map/psum | solution.py:104
  59.8 103.3 %copy-start.7 = (f32[1024]{0:T(1024)S(1)}, f32[1024]{0:T(1024)}, u32[]{:S(2)}) copy-start(f32[1024]{0:T(1024)} %param.27) | copy-start | bytes 12292
  59.8 216.8 %all-gather.5.cloned.1.call-start = ((), (), s32[]{:S(2)}) async-start(), calls=%async_computation.3 | async-start | bytes 18874368 | tf_op jit(solution)/shard_map/all_gather | solution.py:114
  170.6 4.8 copy-start.9
  170.6 52.0 %all-to-all-start = ((bf16[1024,2,8,64]{0,3,1,2:T(8,128)(2,1)}), bf16[1024,2,8,64]{0,3,1,2:T(8,128)(2,1)}, u32[]{:S(2)}, u32[]{:S(2)}) async-start(bf16[1024,2,8,64]{0,3,1,2:T(8,128)(2,1)} %copy.115), calls=%async_computation | async-start | bytes 4194304 | tf_op jit(solution)/shard_map/all_to_all | solution.py:111
  175.1 255.5 %all-reduce.34.cloned.1.call-start = ((), (), s32[]{:S(2)}) async-start(), calls=%async_computation.4 | async-start | bytes 2228224 | tf_op jit(solution)/shard_map/psum | solution.py:141
  276.6 21.9 %copy-start.11 = (f32[64]{0:T(128)S(1)}, f32[64]{0:T(128)}, u32[]{:S(2)}) copy-start(f32[64]{0:T(128)} %param.30) | copy-start | bytes 772
  276.6 22.3 %copy-start.5 = (bf16[64,272]{1,0:T(8,128)(2,1)S(1)}, bf16[64,272]{1,0:T(8,128)(2,1)}, u32[]{:S(2)}) copy-start(bf16[64,272]{1,0:T(8,128)(2,1)} %param.31) | copy-start | bytes 104452
  298.5 133.7 %copy-start.3 = (f32[2,64,1024]{2,1,0:T(8,128)}, f32[2,64,1024]{2,1,0:T(8,128)S(1)}, u32[]{:S(2)}) copy-start(f32[2,64,1024]{2,1,0:T(8,128)S(1)} %get-tuple-element.192) | copy-start | bytes 1572868
  298.5 132.2 %copy-start.6 = (bf16[256,64]{0,1:T(8,128)(2,1)S(1)}, bf16[256,64]{0,1:T(8,128)(2,1)}, u32[]{:S(2)}) copy-start(bf16[256,64]{0,1:T(8,128)(2,1)} %param.32) | copy-start | bytes 98308
  298.5 132.2 %copy-start.10 = (f32[64]{0:T(128)S(1)}, f32[64]{0:T(128)}, u32[]{:S(2)}) copy-start(f32[64]{0:T(128)} %param.33) | copy-start | bytes 772
  298.9 133.3 %copy-start.4 = (bf16[64,1024]{1,0:T(8,128)(2,1)}, bf16[64,1024]{1,0:T(8,128)(2,1)S(1)}, u32[]{:S(2)}) copy-start(bf16[64,1024]{1,0:T(8,128)(2,1)S(1)} %get-tuple-element.236) | copy-start | bytes 393220
  434.3 404.4 %copy-start.12 = (f32[64]{0:T(128)S(1)}, f32[64]{0:T(128)}, u32[]{:S(2)}) copy-start(f32[64]{0:T(128)} %param.35) | copy-start | bytes 772
  481.7 2.1 copy-start.1
  481.7 2.1 copy-start.2
  532.1 2.1 copy-start.2
  582.5 2.1 copy-start.2
  632.9 2.1 copy-start.2
  683.3 2.1 copy-start.2
  733.7 2.1 copy-start.2
  784.1 2.1 copy-start.2
  834.4 2.1 copy-start.2
  (8 other events, 16.4 us)
Sparse Core Ops, SparseCore 0:
  32.2 23.7 all-gather.2
  59.9 86.4 all-reduce.31
  167.5 109.0 all-gather.4
  300.4 130.2 all-reduce.33
where the time goes:
time: 850 us; the launch traced here: 847 us
  local copies, waits for them, and re-layouts  374 us (44%)
  waiting for transfers between devices  333 us (39%)
  other arithmetic  53.8 us (6%)
  blocking collectives  33.8 us (4%)
  matrix products  30.1 us (4%)
  between operations  13.4 us (2%)
    pad x192, local copies, waits for them, and re-layouts, scan_block(): lax.associative_scan(combine, (factor, source), axis=2)  338 us
    psum x1, waiting for transfers between devices, body(): projected = lax.psum(local_proj, ('seq', 'section'))  130 us
    psum x1, waiting for transfers between devices, body(): lax.psum(branch_part.astype(jnp.bfloat16), 'section').astype(jnp.float32)  86.6 us
    all_to_all x1, waiting for transfers between devices, body(): lax.all_to_all(in_weight, 'seq', split_axis=2, concat_axis=0, tiled=True)  47.2 us
    all_gather x1, waiting for transfers between devices, body(): shard_piece = lax.all_gather(normed, 'seq', axis=1, tiled=True)  45.4 us
    all_gather x1, waiting for transfers between devices, body(): lax.all_gather(attended, 'seq', axis=0, tiled=True)  23.9 us
    dot_general x8, matrix products, add_one(): jnp.einsum('ld,dkc->kcl', rows, block_weight, preferred_element_type=jnp....  20.2 us
  transfers between devices with their start and end apart: 5, of which 5 were waited for; matrix products, arithmetic and copies ran while one was open for 1% of the time, Pallas kernels for 0%

commit v1 on v0

v1 whole, which is shorter than its diff:
```python
import functools
import math

import jax
import jax.numpy as jnp
from jax import lax
from jax.experimental import pallas as pl
from jax.experimental.pallas import tpu as pltpu
from jax.sharding import PartitionSpec as P

D = 8192
HD = 128
GROUP = 4
NST = 8
DT_RANK = 256
CONV = 4
NORM_EPS = 1e-05
HALO = 16
VMEM_LIMIT = 56 * 1024 * 1024

F32 = jnp.float32
BF16 = jnp.bfloat16

NN = (((1,), (0,)), ((), ()))
NT = (((1,), (1,)), ((), ()))
TN = (((0,), (0,)), ((), ()))


def dot(lhs, rhs, dims=NN):
    return lax.dot_general(lhs, rhs, dims, preferred_element_type=F32)


def call(kernel, out_shape, n_in, scratch=(), flops=0, size=0, in_place=None, out_place=pltpu.VMEM):
    in_place = in_place or [pltpu.VMEM] * n_in
    return pl.pallas_call(
        kernel,
        out_shape=out_shape,
        in_specs=[pl.BlockSpec(memory_space=place) for place in [pltpu.SMEM] + in_place],
        out_specs=jax.tree.map(lambda _: pl.BlockSpec(memory_space=out_place), out_shape),
        scratch_shapes=list(scratch),
        compiler_params=pltpu.CompilerParams(vmem_limit_bytes=VMEM_LIMIT),
        cost_estimate=pl.CostEstimate(flops=flops, bytes_accessed=size, transcendentals=0),
    )


def swap(x, axis, count, bits):
    return lax.ppermute(x, axis, [(i, i ^ bits) for i in range(count)])


def after(x, *others):
    return lax.optimization_barrier((x, *others))[0]


def gather_seq(messages, count, *others):
    even = [messages[0]] + [swap(messages[k // 2], "seq", count, k) for k in range(2, count, 2)]
    even, others = lax.optimization_barrier((even, others))
    pieces = []
    for piece in even:
        pieces += [piece, swap(piece, "seq", count, 1)]
    return pieces, others


def attention_kernel(count, rank_ref, query_ref, *refs):
    kv_refs = refs[:count]
    out_ref, scores_ref, value_ref = refs[count:]
    rank = rank_ref[0]
    rows = query_ref.shape[0]
    stacked = jnp.concatenate(
        [query_ref[:, g * HD : (g + 1) * HD] for g in range(GROUP)], axis=0
    )
    maxima = None
    for k in range(count):
        part = dot(stacked, kv_refs[k][:, :HD], NT) * (1.0 / math.sqrt(HD))
        if k == 0:
            row = lax.broadcasted_iota(jnp.int32, part.shape, 0) % rows
            col = lax.broadcasted_iota(jnp.int32, part.shape, 1)
            part = jnp.where(row >= col, part, -1e30)
        else:
            earlier = jnp.bitwise_xor(rank, k) < rank
            part = jnp.where(earlier, part, -1e30)
        scores_ref[:, k * rows : (k + 1) * rows] = part
        value_ref[k * rows : (k + 1) * rows, :] = kv_refs[k][:, HD:]
        peak = jnp.max(part, axis=1, keepdims=True)
        maxima = peak if maxima is None else jnp.maximum(maxima, peak)
    terms = jnp.exp(scores_ref[...] - maxima)
    total = jnp.sum(terms, axis=1, keepdims=True)
    result = dot(terms.astype(BF16), value_ref[...]) / total
    result = result.astype(BF16)
    for g in range(GROUP):
        out_ref[:, g * HD : (g + 1) * HD] = result[g * rows : (g + 1) * rows, :]


class Copies:
    def __init__(self, semaphores):
        self.semaphores = semaphores
        self.count = 0

    def start(self, source, target):
        copy = pltpu.make_async_copy(source, target, self.semaphores.at[self.count])
        self.count += 1
        copy.start()
        return copy


def own_kernel(count, rank_ref, *refs):
    own_refs = refs[:count]
    weight_ref, residual_ref, acc_ref, left_ref = refs[count:]
    rank = rank_ref[0]
    rows = own_refs[0].shape[0]
    for k in range(count):
        left_ref[k * rows : (k + 1) * rows, :] = own_refs[k][...]
    tile = 2 * rows
    for t in range(count // 2):
        total = dot(left_ref[t * tile : (t + 1) * tile, :], weight_ref[...])
        for half in range(2):
            k = 2 * t + half
            first = pl.multiple_of(jnp.bitwise_xor(rank, k) * rows, rows)
            acc_ref[k * rows : (k + 1) * rows, :] = total[
                half * rows : (half + 1) * rows
            ] + residual_ref[pl.ds(first, rows), :].astype(F32)


def mix_kernel(count, used, rank_ref, *refs):
    far_refs = refs[:count]
    weight_refs = refs[count : count + used]
    refs = refs[count + used :]
    acc_ref, gain_ref, in_ref = refs[:3]
    out_refs = refs[3 : count + 3]
    left, weights, acc, columns, normed, mixed, halos, squares, semaphores = refs[count + 3 :]
    rank = rank_ref[0]
    rows = far_refs[0].shape[0]
    width = weight_refs[0].shape[0]
    channels = in_ref.shape[1]
    copies = Copies(semaphores)
    weight_copies = [
        copies.start(weight_refs[r], weights.at[pl.ds(r * width, width), :]) for r in range(used)
    ]
    tile = rows * count // 2
    left_copies, acc_copies, out_copies = [], [], []
    for t in range(2):
        left_copies.append(
            [
                copies.start(
                    far_refs[k],
                    left.at[pl.ds(k * rows, rows), :],
                )
                for k in range(t * count // 2, (t + 1) * count // 2)
            ]
        )
        span = pl.ds(t * tile, tile)
        acc_copies.append(copies.start(acc_ref.at[span, :], acc.at[span, :]))
    column_copy = copies.start(in_ref, columns)
    for copy in weight_copies:
        copy.wait()
    eye = lax.broadcasted_iota(jnp.int32, (rows, rows), 0) == lax.broadcasted_iota(
        jnp.int32, (rows, rows), 1
    )
    for t in range(2):
        span = pl.ds(t * tile, tile)
        for copy in left_copies[t]:
            copy.wait()
        total = dot(left[span, :], weights[...])
        acc_copies[t].wait()
        hidden = acc[span, :] + total
        normed[span, :] = (hidden * gain_ref[...]).astype(BF16)
        sums = jnp.sum(hidden * hidden, axis=1, keepdims=True)
        for part in range(count // 2):
            k = t * count // 2 + part
            squares[k : k + 1, :] = jnp.sum(
                jnp.where(eye, sums[part * rows : (part + 1) * rows], 0.0),
                axis=0,
                keepdims=True,
            )
    column_copy.wait()
    for t in range(2):
        result = dot(normed[pl.ds(t * tile, tile), :], columns[...]).astype(BF16)
        mixed[pl.ds(t * tile, tile), :] = result
        for part in range(count // 2):
            k = t * count // 2 + part
            out_copies.append(
                copies.start(
                    mixed.at[pl.ds(k * rows, rows), :], out_refs[k].at[pl.ds(HALO, rows), :]
                )
            )
    line = lax.broadcasted_iota(jnp.int32, (HALO, channels), 0)
    for k in range(count):
        block = jnp.bitwise_xor(rank, k)
        before = jnp.bitwise_xor(rank, jnp.maximum(block - 1, 0))
        last = pl.multiple_of(before * rows + (rows - HALO), HALO)
        halo = mixed[pl.ds(last, HALO), :].astype(F32)
        own = jnp.tile(squares[k : k + 1, :], (1, channels // rows))
        past = jnp.tile(squares[pl.ds(before, 1), :], (1, channels // rows))
        halo = jnp.where(line == 0, own, jnp.where(line == 1, past, halo))
        halos[k] = halo.astype(BF16)
        out_copies.append(copies.start(halos.at[k], out_refs[k].at[pl.ds(0, HALO), :]))
    for copy in out_copies:
        copy.wait()


def conv_kernel(n_pieces, count, rank_ref, *refs):
    piece_refs = refs[:n_pieces]
    param_refs = refs[n_pieces : n_pieces + count]
    out_ref, maps_ref, total_ref = refs[n_pieces + count :]
    rank = rank_ref[0]
    total = piece_refs[0][...].astype(F32)
    for piece in piece_refs[1:]:
        total += piece[...].astype(F32)
    rows = total.shape[0] - HALO
    eye = lax.broadcasted_iota(jnp.int32, (rows, rows), 0) == lax.broadcasted_iota(
        jnp.int32, (rows, rows), 1
    )
    scale_own = lax.rsqrt(total[0:1, :rows] / D + NORM_EPS)
    scale_past = lax.rsqrt(total[1:2, :rows] / D + NORM_EPS)
    scale_past = jnp.where(rank == 0, 0.0, scale_past)
    column_own = jnp.sum(jnp.where(eye, scale_own, 0.0), axis=1, keepdims=True)
    column_past = jnp.sum(jnp.where(eye, scale_past, 0.0), axis=1, keepdims=True)
    total_ref[0:8, :] = total[HALO - 8 : HALO] * column_past[rows - 8 :]
    total_ref[8:, :] = total[HALO:] * column_own
    group = out_ref.shape[2]
    middle = DT_RANK + 2 * NST
    projected = jnp.zeros((middle, rows), F32)
    for k in range(count):
        first = pl.multiple_of(jnp.bitwise_xor(rank, k) * group, group)
        path = total_ref[:, pl.ds(first, group)]
        params = param_refs[k][middle:, :].astype(F32)
        taps = params[0:5] + params[5:10] + params[10:15]
        conv = taps[CONV : CONV + 1] + jnp.zeros((rows, group), F32)
        for offset in range(CONV):
            begin = 8 - (CONV - 1) + offset
            conv += taps[offset : offset + 1] * path[begin : begin + rows]
        result = (conv / (1.0 + jnp.exp(-conv))).astype(BF16)
        out_ref[k] = result
        projected += dot(param_refs[k][0:middle, :], result, NT)
    low_rank = projected[:DT_RANK]
    maps = projected[DT_RANK:]
    high = maps.astype(BF16)
    maps_ref[0:DT_RANK, :] = low_rank.astype(BF16)
    maps_ref[DT_RANK:middle, :] = high
    maps_ref[middle:, :] = (maps - high.astype(F32)).astype(BF16)


def sum_kernel(n_pieces, rank_ref, *refs):
    del rank_ref
    pairs_ref = refs[n_pieces]
    out_refs = refs[n_pieces + 1 :]
    rows = pairs_ref.shape[1]
    total = refs[0][...].astype(F32)
    for piece in refs[1:n_pieces]:
        total += piece[...].astype(F32)
    middle = DT_RANK + 2 * NST
    maps = total[DT_RANK:middle] + total[middle:]
    high = maps.astype(BF16)
    low = (maps - high.astype(F32)).astype(BF16)
    low_rank = total[:DT_RANK].astype(BF16)
    for at, out_ref in enumerate(out_refs):
        out_ref[0:rows, :] = pairs_ref[2 * at]
        out_ref[rows : 2 * rows, :] = pairs_ref[2 * at + 1]
        out_ref[2 * rows : 2 * rows + DT_RANK, :] = low_rank
        out_ref[2 * rows + DT_RANK : 2 * rows + middle, :] = high
        out_ref[2 * rows + middle :, :] = low


def scan_kernel(count, rank_ref, *refs):
    rows = (refs[0].shape[0] - DT_RANK - 4 * NST) // 2
    pair_refs = [refs[k].at[pl.ds(k % 2 * rows, rows), :] for k in range(count)]
    maps_refs = [refs[k].at[pl.ds(2 * rows, DT_RANK + 4 * NST), :] for k in range(count)]
    (
        weight_ref, bias_ref, decay_ref, skip_ref, out_ref,
        factor_ref, source_ref, read_ref, value_ref, end_ref, product_ref, begin_ref,
    ) = refs[count:]
    rank = rank_ref[0]
    lanes = weight_ref.shape[1]
    half = lanes // 2
    groups = NST // 2
    wide = groups * lanes
    map_rows = maps_refs[0].shape[0] - DT_RANK
    map_row = lax.broadcasted_iota(jnp.int32, (map_rows, wide), 0) % (2 * NST)
    state_of = lax.broadcasted_iota(jnp.int32, (map_rows, wide), 1) // half
    spread_in = jnp.where(map_row == state_of, 1.0, 0.0).astype(BF16)
    spread_out = jnp.where(map_row == state_of + NST, 1.0, 0.0).astype(BF16)
    lane = lax.broadcasted_iota(jnp.int32, (rows, lanes), 1)
    for k in range(count):
        span = slice(k * rows, (k + 1) * rows)
        step = dot(maps_refs[k][:DT_RANK, :], weight_ref[...], TN) + bias_ref[...]
        step = jnp.maximum(step, 0.0) + jnp.log1p(jnp.exp(-jnp.abs(step)))
        pair = pair_refs[k][...].astype(F32)
        value = jnp.where(lane < half, pair, pltpu.roll(pair, half, 1))
        value_ref[span, :] = value
        maps = maps_refs[k][DT_RANK:, :]
        in_map = dot(maps, spread_in, TN)
        read_ref[span, :] = dot(maps, spread_out, TN)
        drive = step * value
        for g in range(groups):
            part = slice(g * lanes, (g + 1) * lanes)
            factor_ref[g, span, :] = jnp.exp(step * decay_ref[:, part])
            source_ref[g, span, :] = drive * in_map[:, part]

    def advance(t, carried):
        at = pl.ds(t, count, stride=rows)
        following = []
        for g in range(groups):
            state, product = carried[g]
            factor = factor_ref[g, at, :]
            state = factor * state + source_ref[g, at, :]
            product = factor * product
            source_ref[g, at, :] = state
            factor_ref[g, at, :] = product
            following.append((state, product))
        return following

    carried = lax.fori_loop(
        0,
        rows,
        advance,
        [(jnp.zeros((count, lanes), F32), jnp.ones((count, lanes), F32))] * groups,
        unroll=8,
    )
    state = jnp.concatenate([pair[0] for pair in carried], axis=1)
    product = jnp.concatenate([pair[1] for pair in carried], axis=1)
    end_ref[...] = state
    product_ref[...] = product
    carried = jnp.zeros((1, wide), F32)
    for j in range(count):
        at = pl.ds(jnp.bitwise_xor(rank, j), 1)
        begin_ref[at, :] = carried
        carried = product_ref[at, :] * carried + end_ref[at, :]
    for k in range(count):
        span = slice(k * rows, (k + 1) * rows)
        total = skip_ref[...] * value_ref[span, :]
        readout = jnp.zeros((rows, lanes), F32)
        for g in range(groups):
            part = slice(g * lanes, (g + 1) * lanes)
            state = source_ref[g, span, :] + factor_ref[g, span, :] * begin_ref[k : k + 1, part]
            readout += state * read_ref[span, part]
        total += readout + pltpu.roll(readout, half, 1)
        result = jnp.transpose(total * pair_refs[k][...].astype(F32))
        first = pl.multiple_of(jnp.bitwise_xor(rank, k) * rows, rows)
        out_ref[:, pl.ds(first, rows)] = result[half:].astype(BF16)


def body(
    n_seq,
    n_sec,
    queries,
    keys,
    values,
    residual,
    out_weight,
    norm_gain,
    in_weight,
    conv_weight,
    conv_bias,
    proj_weight,
    dt_weight,
    dt_bias,
    a_log,
    skip_gain,
):
    shape = jax.ShapeDtypeStruct
    rows = queries.shape[0]
    seq_len = residual.shape[0]
    features = residual.shape[1]
    own = conv_weight.shape[0]
    channels = n_seq * 2 * own
    rank = lax.axis_index("seq").astype(jnp.int32)
    rank_arg = rank.reshape(1)

    others_at = list(range(1, n_sec))
    far_at = list(range(3, n_sec, 2))
    weights = {r: swap(out_weight, "section", n_sec, r) for r in far_at}

    pairs, _ = gather_seq([jnp.concatenate([keys, values], axis=1)] * (n_seq // 2), n_seq)
    attended = call(
        functools.partial(attention_kernel, n_seq),
        shape((rows, GROUP * HD), BF16),
        1 + n_seq,
        [pltpu.VMEM((GROUP * rows, seq_len), F32), pltpu.VMEM((seq_len, HD), BF16)],
        flops=4 * GROUP * rows * seq_len * HD,
        size=4 * rows * 4 * HD * n_seq,
    )(rank_arg, queries, *pairs)

    far = jnp.concatenate(
        [swap(attended, "section", n_sec, r) for r in others_at], axis=1
    )
    own_pieces, _ = gather_seq([attended] * (n_seq // 2), n_seq)
    nearest = swap(after(out_weight, own_pieces[-1]), "section", n_sec, 1)
    for r in range(2, n_sec, 2):
        weights[r] = swap(after(weights[r + 1], far), "section", n_sec, 1)

    width = out_weight.shape[0]
    conv = jnp.concatenate([conv_weight, conv_bias[:, None]], axis=1).T
    identity = jnp.zeros_like(conv).at[CONV - 1].set(1.0)
    conv = jnp.concatenate([conv, identity], axis=1)
    terms = []
    for _ in range(3):
        high = lax.reduce_precision(conv, 8, 7)
        terms.append(high.astype(BF16))
        conv = conv - high
    proj = jnp.concatenate([proj_weight, jnp.zeros_like(proj_weight)], axis=0).reshape(
        2, own, -1
    )
    proj = jnp.transpose(proj, (2, 0, 1)).reshape(-1, 2 * own)
    params = jnp.concatenate([proj, *terms, jnp.zeros((1, 2 * own), BF16)], axis=0)
    params, _ = gather_seq([after(params, attended)] * (n_seq // 2), n_seq)
    in_columns = jnp.transpose(in_weight, (0, 2, 1, 3)).reshape(features, channels)
    far = after(far, in_columns)

    acc = call(
        functools.partial(own_kernel, n_seq),
        shape((seq_len, features), F32),
        n_seq + 2,
        [pltpu.VMEM((seq_len, width), BF16)],
        flops=2 * seq_len * features * width,
        size=seq_len * features * 8,
    )(rank_arg, *own_pieces, out_weight, residual)
    far_pieces, others = gather_seq(
        [far] * (n_seq // 2),
        n_seq,
        acc, nearest, *params,
    )
    acc, weights[1], *params = others
    used = n_sec - 1
    payloads = call(
        functools.partial(mix_kernel, n_seq, used),
        [shape((HALO + rows, channels), BF16)] * n_seq,
        n_seq + used + 3,
        [
            pltpu.VMEM((seq_len, width * used), BF16),
            pltpu.VMEM((used * width, features), BF16),
            pltpu.VMEM((seq_len, features), F32),
            pltpu.VMEM((features, channels), BF16),
            pltpu.VMEM((seq_len, features), BF16),
            pltpu.VMEM((seq_len, channels), BF16),
            pltpu.VMEM((n_seq, HALO, channels), BF16),
            pltpu.VMEM((n_seq, rows), F32),
            pltpu.SemaphoreType.DMA((3 * n_seq + 2 * used + 3,)),
        ],
        flops=2 * seq_len * features * (width * used + channels),
        size=seq_len * features * 12,
        in_place=[pl.ANY] * (n_seq + used + 1) + [pltpu.VMEM, pl.ANY],
        out_place=pl.ANY,
    )(
        rank_arg,
        *far_pieces,
        *[weights[r] for r in others_at],
        acc,
        norm_gain.reshape(1, -1),
        in_columns,
    )

    arrived = {k: swap(payloads[k], "seq", n_seq, 1) for k in range(n_seq - 1, 0, -2)}
    summed = {
        k: (payloads[k].astype(F32) + arrived[k + 1].astype(F32)).astype(BF16)
        for k in range(0, n_seq, 2)
    }
    pieces = [summed[0]] + [swap(summed[k], "seq", n_seq, k) for k in range(2, n_seq, 2)]

    map_rows = DT_RANK + 4 * NST
    outgoing, maps = call(
        functools.partial(conv_kernel, len(pieces), n_seq),
        [shape((n_seq, rows, 2 * own), BF16), shape((map_rows, rows), BF16)],
        len(pieces) + n_seq,
        [pltpu.VMEM((rows + 8, channels), F32)],
        flops=2 * rows * channels * map_rows,
        size=rows * channels * 12,
    )(rank_arg, *pieces, *params)

    map_parts = [maps] + [swap(maps, "section", n_sec, r) for r in range(1, n_sec)]
    messages = call(
        functools.partial(sum_kernel, n_sec),
        [shape((2 * rows + map_rows, rows), BF16)] * (n_seq // 2),
        n_sec + 1,
        size=map_rows * rows * 2 * n_sec,
    )(rank_arg, *map_parts, outgoing)
    scan_pieces, _ = gather_seq(messages, n_seq)

    weight = jnp.concatenate([dt_weight, dt_weight], axis=1)
    bias = jnp.concatenate([dt_bias, dt_bias]).reshape(1, -1)
    skip = jnp.concatenate([skip_gain, skip_gain]).reshape(1, -1)
    decay = (-jnp.exp(a_log)).T.reshape(1, -1)
    wide = NST * own
    return call(
        functools.partial(scan_kernel, n_seq),
        shape((own, seq_len), BF16),
        n_seq + 4,
        [pltpu.VMEM((NST // 2, seq_len, 2 * own), F32)] * 2
        + [pltpu.VMEM((seq_len, wide), F32)]
        + [pltpu.VMEM((seq_len, 2 * own), F32)]
        + [pltpu.VMEM((n_seq, wide), F32)] * 3,
        flops=2 * seq_len * DT_RANK * own,
        size=seq_len * wide * 8,
    )(rank_arg, *scan_pieces, weight, bias, decay, skip)


def solution(mesh):
    return jax.shard_map(
        functools.partial(body, mesh.shape["seq"], mesh.shape["section"]),
        mesh=mesh,
        in_specs=(
            P("seq", "section"),
            P("seq", "section"),
            P("seq", "section"),
            P(None, "seq"),
            P("section", "seq"),
            P("seq"),
            P("seq", None, None, "section"),
            P(("seq", "section"), None),
            P(("seq", "section")),
            P(("seq", "section"), None),
            P(None, ("seq", "section")),
            P(("seq", "section")),
            P(("seq", "section"), None),
            P(("seq", "section")),
        ),
        out_specs=P(("seq", "section"), None),
        check_vma=False,
    )
```

time: 850 us -> 167 us (0.20)
  local copies, waits for them, and re-layouts: 374 us -> 13.3 us
  waiting for transfers between devices: 333 us -> 71.1 us
  other arithmetic: 53.8 us -> 6.79 us
  Pallas kernels: 0 us -> 35.5 us
  starting transfers between devices: 4.83 us -> 38.9 us
  blocking collectives: 33.8 us -> 0 us
  matrix products: 30.1 us -> 0 us
  between operations: 13.4 us -> 0.44 us
    pad x192 -> x0, local copies, waits for them, and re-layouts: 338 us -> none  [scan_block(): lax.associative_scan(combine, (factor, source), axis=2)]
    psum x2 -> x0, waiting for transfers between devices: 216 us -> none  [the longest x1 130 us: body(): projected = lax.psum(local_proj, ('seq', 'section'))]
    ppermute x0 -> x51, waiting for transfers between devices: none -> 71.1 us  [swap(): return lax.ppermute(x, axis, [(i, i ^ bits) for i in range(count)])]
    all_gather x2 -> x0, waiting for transfers between devices: 69.3 us -> none  [the longest x1 45.4 us: body(): shard_piece = lax.all_gather(normed, 'seq', axis=1, tiled=True)]
    all_to_all x1 -> x0, waiting for transfers between devices: 47.2 us -> none  [body(): lax.all_to_all(in_weight, 'seq', split_axis=2, concat_axis=0, tiled=True)]
    ppermute x0 -> x51, starting transfers between devices: none -> 38.9 us  [swap(): return lax.ppermute(x, axis, [(i, i ^ bits) for i in range(count)])]
    pallas_call x0 -> x6, Pallas kernels: none -> 35.5 us  [the longest x1 11.1 us: body(): call(functools.partial(mix_kernel, n_seq, used), [shape((HALO + rows, cha...]
    dot_general x15 -> x0, matrix products: 30.1 us -> none  [the longest x8 20.2 us: add_one(): jnp.einsum('ld,dkc->kcl', rows, block_weight, preferred_element_type=jnp....]
  transfers between devices with their start and end apart: 5 -> 51, of which waited for: 5 -> 23; matrix products, arithmetic and copies ran while one was open for 1% -> 10% of each run, Pallas kernels for 0% -> 5%
where the time goes in v1:
time: 167 us; the launch traced here: 166 us
  waiting for transfers between devices  71.1 us (43%)
  starting transfers between devices  38.9 us (23%)
  Pallas kernels  35.5 us (21%)
  local copies, waits for them, and re-layouts  13.3 us (8%)
  other arithmetic  6.79 us (4%)
    ppermute x51, waiting for transfers between devices, swap(): return lax.ppermute(x, axis, [(i, i ^ bits) for i in range(count)])  71.1 us
    ppermute x51, starting transfers between devices, swap(): return lax.ppermute(x, axis, [(i, i ^ bits) for i in range(count)])  38.9 us
    pallas_call x1, Pallas kernels, body(): call(functools.partial(mix_kernel, n_seq, used), [shape((HALO + rows, cha...  11.1 us
    pallas_call x1, Pallas kernels, body(): call(functools.partial(scan_kernel, n_seq), shape((own, seq_len), BF16),...  10.6 us
    unnamed x91, local copies, waits for them, and re-layouts  7.52 us
    pallas_call x1, Pallas kernels, body(): call(functools.partial(own_kernel, n_seq), shape((seq_len, features), F32...  5.64 us
    convert_element_type x4, other arithmetic, body(): (payloads[k].astype(F32) + arrived[k + 1].astype(F32)).astype(BF16)  3.91 us
  transfers between devices with their start and end apart: 51, of which 23 were waited for; matrix products, arithmetic and copies ran while one was open for 10% of the time, Pallas kernels for 5%

profile of v1, /device:TPU:0, one launch (start us, length us, event | category | flops | bytes accessed | tf_op | source)
XLA Modules:
  0.0 166.0 jit_solution(9157150174780379552)
XLA Ops:
  0.0 5.0 %collective-permute-start.32 = (bf16[512,1024]{1,0:T(8,128)(2,1)}, bf16[512,1024]{1,0:T(8,128)(2,1)}, u32[]{:S(2)}, u32[]{:S(2)}) collective-permute-start(bf16[512,1024]{1,0:T(8,128)(2,1)} %refs_8_.1), channel_id=1, source_target_pairs={{0,3},{1,2},{2,1},{3,0},{4,7},{5,6},{6,5},{7,4},{8,11},{9,10},{10,... | collective-permute-start | bytes 3145736 | tf_op jit(solution)/shard_map/ppermute | solution.py:47
  10.9 2.2 %collective-permute-done.1.refs_4_ = bf16[128,256]{1,0:T(8,128)(2,1)S(1)} collective-permute-done((bf16[128,256]{1,0:T(8,128)(2,1)S(1)}, bf16[128,256]{1,0:T(8,128)(2,1)S(1)}, u32[]{:S(2)}, u32[]{:S(2)}) %collective-permute-start.1) | collective-permute-done | bytes 65568 | tf_op jit(solution)/shard_map/ppermute | solution.py:47
  17.4 3.1 %shard_map.136.refs_0_ = bf16[128,512]{1,0:T(8,128)(2,1)} custom-call(s32[1]{0:T(128)} %bitcast.rank_ref, bf16[128,512]{1,0:T(8,128)(2,1)} %query_ref.1, bf16[128,256]{1,0:T(8,128)(2,1)} %copy-done.30, bf16[128,256]{1,0:T(8,128)(2,1)} %copy-done.39, bf16[128,256]{1,0:T(8,128)(2,1)} %copy-done.36, bf16[128,256]{1,0:T(8,128)(2,1)} %copy-done.40, ...), custom_call_target="tpu_custom_call" | custom-call | flops 268435456 | bytes 2097152 | tf_op jit(solution)/shard_map/pallas_call | solution.py:373
  21.5 2.4 %collective-permute-start.15 = (bf16[128,512]{1,0:T(8,128)(2,1)}, bf16[128,512]{1,0:T(8,128)(2,1)S(1)}, u32[]{:S(2)}, u32[]{:S(2)}) collective-permute-start(bf16[128,512]{1,0:T(8,128)(2,1)} %shard_map.136.refs_0_), channel_id=1, source_target_pairs={{0,24},{4,28},{8,16},{12,20},{16,8},{20,12},{24,0},{28,4},{1,25},{... | collective-permute-start | bytes 393224 | tf_op jit(solution)/shard_map/ppermute | solution.py:47
  27.0 2.5 %collective-permute-done.14.refs_4_ = bf16[128,512]{1,0:T(8,128)(2,1)S(1)} collective-permute-done((bf16[128,512]{1,0:T(8,128)(2,1)}, bf16[128,512]{1,0:T(8,128)(2,1)S(1)}, u32[]{:S(2)}, u32[]{:S(2)}) %collective-permute-start.14) | collective-permute-done | bytes 131104 | tf_op jit(solution)/shard_map/ppermute | solution.py:47
  35.4 2.8 %collective-permute-done.22.refs_8_ = bf16[288,128]{1,0:T(8,128)(2,1)S(1)} collective-permute-done((bf16[288,128]{1,0:T(8,128)(2,1)S(1)}, bf16[288,128]{1,0:T(8,128)(2,1)S(1)}, u32[]{:S(2)}, u32[]{:S(2)}) %collective-permute-start.22) | collective-permute-done | bytes 73760 | tf_op jit(solution)/shard_map/ppermute | solution.py:47
  38.2 1.9 %collective-permute-start.9 = (bf16[128,512]{1,0:T(8,128)(2,1)}, bf16[128,512]{1,0:T(8,128)(2,1)S(1)}, u32[]{:S(2)}, u32[]{:S(2)}) collective-permute-start(bf16[128,512]{1,0:T(8,128)(2,1)} %shard_map.136.refs_0_), channel_id=1, source_target_pairs={{0,3},{1,2},{2,1},{3,0},{4,7},{5,6},{6,5},{7,4},{8,11},{9,10},{10,... | collective-permute-start | bytes 393224 | tf_op jit(solution)/shard_map/ppermute | solution.py:47
  40.8 21.3 %collective-permute-done.8 = bf16[128,512]{1,0:T(8,128)(2,1)S(1)} collective-permute-done((bf16[128,512]{1,0:T(8,128)(2,1)}, bf16[128,512]{1,0:T(8,128)(2,1)S(1)}, u32[]{:S(2)}, u32[]{:S(2)}) %collective-permute-start.8) | collective-permute-done | bytes 131104 | tf_op jit(solution)/shard_map/ppermute | solution.py:47
  62.7 2.3 %collective-permute-done.9 = bf16[128,512]{1,0:T(8,128)(2,1)S(1)} collective-permute-done((bf16[128,512]{1,0:T(8,128)(2,1)}, bf16[128,512]{1,0:T(8,128)(2,1)S(1)}, u32[]{:S(2)}, u32[]{:S(2)}) %collective-permute-start.9) | collective-permute-done | bytes 131104 | tf_op jit(solution)/shard_map/ppermute | solution.py:47
  67.6 1.8 %copy.19 = bf16[1024,2,8,64]{0,3,1,2:T(8,128)(2,1)S(1)} copy(bf16[1024,2,8,64]{0,3,2,1:T(8,128)(2,1)} %param.22) | data formatting | bytes 4194304 | tf_op args[6]
  73.1 5.6 %shard_map.137.refs_11_ = f32[1024,1024]{1,0:T(8,128)} custom-call(s32[1]{0:T(128)} %bitcast.rank_ref, bf16[128,512]{1,0:T(8,128)(2,1)} %shard_map.136.refs_0_, bf16[128,512]{1,0:T(8,128)(2,1)} %copy-done.16, bf16[128,512]{1,0:T(8,128)(2,1)} %copy-done.12, bf16[128,512]{1,0:T(8,128)(2,1)} %copy-done.17, bf16[128,512]{1,0:T(8,128)(2,1)} %copy-done.13, ...), custom_call_target="tpu_custom_call" | custom-call | flops 1073741824 | bytes 8388608 | tf_op jit(solution)/shard_map/pallas_call | solution.py:408
  78.8 3.0 %collective-permute-done.10.refs_2_ = bf16[128,1536]{1,0:T(8,128)(2,1)S(1)} collective-permute-done((bf16[128,1536]{1,0:T(8,128)(2,1)}, bf16[128,1536]{1,0:T(8,128)(2,1)S(1)}, u32[]{:S(2)}, u32[]{:S(2)}) %collective-permute-start.10) | collective-permute-done | bytes 393248 | tf_op jit(solution)/shard_map/ppermute | solution.py:47
  81.8 9.1 %collective-permute-done.11.refs_4_ = bf16[128,1536]{1,0:T(8,128)(2,1)S(1)} collective-permute-done((bf16[128,1536]{1,0:T(8,128)(2,1)}, bf16[128,1536]{1,0:T(8,128)(2,1)S(1)}, u32[]{:S(2)}, u32[]{:S(2)}) %collective-permute-start.11) | collective-permute-done | bytes 393248 | tf_op jit(solution)/shard_map/ppermute | solution.py:47
  91.9 2.6 %copy.21.refs_13_ = bf16[1024,1024]{1,0:T(8,128)(2,1)} copy(bf16[1024,1024]{0,1:T(8,128)(2,1)S(1)} %bitcast.20) | data formatting | bytes 4194304 | tf_op jit(solution)/shard_map/reshape | solution.py:405
  94.7 11.1 %shard_map.138 = (bf16[144,1024]{1,0:T(8,128)(2,1)}, bf16[144,1024]{1,0:T(8,128)(2,1)}, bf16[144,1024]{1,0:T(8,128)(2,1)}, bf16[144,1024]{1,0:T(8,128)(2,1)}, bf...) custom-call(s32[1]{0:T(128)} %bitcast.rank_ref, ...), custom_call_target="tpu_custom_call" | custom-call | flops 5368709120 | bytes 12582912 | tf_op jit(solution)/shard_map/pallas_call | solution.py:423
  115.3 4.2 %collective-permute-done.40.refs_3_ = bf16[144,1024]{1,0:T(8,128)(2,1)S(1)} collective-permute-done((bf16[144,1024]{1,0:T(8,128)(2,1)S(1)}, bf16[144,1024]{1,0:T(8,128)(2,1)S(1)}, u32[]{:S(2)}, u32[]{:S(2)}) %collective-permute-start.40) | collective-permute-done | bytes 294944 | tf_op jit(solution)/shard_map/ppermute | solution.py:47
  119.6 5.5 %collective-permute-done.38.refs_2_ = bf16[144,1024]{1,0:T(8,128)(2,1)S(1)} collective-permute-done((bf16[144,1024]{1,0:T(8,128)(2,1)S(1)}, bf16[144,1024]{1,0:T(8,128)(2,1)S(1)}, u32[]{:S(2)}, u32[]{:S(2)}) %collective-permute-start.38) | collective-permute-done | bytes 294944 | tf_op jit(solution)/shard_map/ppermute | solution.py:47
  126.5 3.1 %shard_map.139 = (bf16[8,128,128]{2,1,0:T(8,128)(2,1)}, bf16[288,128]{1,0:T(8,128)(2,1)}) custom-call(s32[1]{0:T(128)} %bitcast.rank_ref, bf16[144,1024]{1,0:T(8,128)(2,1)} %add_convert_fusion.3.refs_0_, bf16[144,1024]{1,0:T(8,128)(2,1)} %copy-done.3, bf16[144,1024]{1,0:T(8,128)(2,1)} %copy-done.2, bf16[144,1024]{1,0:T(8,128)(2,1)} %copy-done.1, ...), custom_call_target="tpu_custom_call" | custom-call | flops 75497472 | bytes 1572864 | tf_op jit(solution)/shard_map/pallas_call | solution.py:459
  129.6 2.0 %collective-permute-start.41 = (bf16[288,128]{1,0:T(8,128)(2,1)}, bf16[288,128]{1,0:T(8,128)(2,1)S(1)}, u32[]{:S(2)}, u32[]{:S(2)}) collective-permute-start(bf16[288,128]{1,0:T(8,128)(2,1)} %get-tuple-element.103.refs_0_), channel_id=1, source_target_pairs={{0,1},{1,0},{2,3},{3,2},{4,5},{5,4},{6,7},{7,6},{8,9},{9,8},{10,11... | collective-permute-start | bytes 221192 | tf_op jit(solution)/shard_map/ppermute | solution.py:47
  134.6 6.1 %collective-permute-done.42.refs_2_ = bf16[288,128]{1,0:T(8,128)(2,1)S(1)} collective-permute-done((bf16[288,128]{1,0:T(8,128)(2,1)}, bf16[288,128]{1,0:T(8,128)(2,1)S(1)}, u32[]{:S(2)}, u32[]{:S(2)}) %collective-permute-start.42) | collective-permute-done | bytes 73760 | tf_op jit(solution)/shard_map/ppermute | solution.py:47
  141.3 2.0 %shard_map.140 = (bf16[544,128]{1,0:T(8,128)(2,1)}, bf16[544,128]{1,0:T(8,128)(2,1)}, bf16[544,128]{1,0:T(8,128)(2,1)}, bf16[544,128]{1,0:T(8,128)(2,1)}) custom-call(s32[1]{0:T(128)} %bitcast.rank_ref, bf16[288,128]{1,0:T(8,128)(2,1)} %get-tuple-element.103.refs_0_, bf16[288,128]{1,0:T(8,128)(2,1)} %copy-done.19, bf16[288,128]{1,0:T(8,128)(2,1)} %copy-done.20, ...), custom_call_target="tpu_custom_call" | custom-call | bytes 294912 | tf_op jit(solution)/shard_map/pallas_call | solution.py:469
  146.8 2.1 %collective-permute-done.44.refs_2_ = bf16[544,128]{1,0:T(8,128)(2,1)S(1)} collective-permute-done((bf16[544,128]{1,0:T(8,128)(2,1)}, bf16[544,128]{1,0:T(8,128)(2,1)S(1)}, u32[]{:S(2)}, u32[]{:S(2)}) %collective-permute-start.44) | collective-permute-done | bytes 139296 | tf_op jit(solution)/shard_map/ppermute | solution.py:47
  148.9 2.4 %collective-permute-done.45.refs_4_ = bf16[544,128]{1,0:T(8,128)(2,1)S(1)} collective-permute-done((bf16[544,128]{1,0:T(8,128)(2,1)}, bf16[544,128]{1,0:T(8,128)(2,1)S(1)}, u32[]{:S(2)}, u32[]{:S(2)}) %collective-permute-start.45) | collective-permute-done | bytes 139296 | tf_op jit(solution)/shard_map/ppermute | solution.py:47
  155.4 10.6 %shard_map.141 = bf16[64,1024]{1,0:T(8,128)(2,1)} custom-call(s32[1]{0:T(128)} %bitcast.rank_ref, bf16[544,128]{1,0:T(8,128)(2,1)} %get-tuple-element.109.refs_0_, bf16[544,128]{1,0:T(8,128)(2,1)} %copy-done.8, bf16[544,128]{1,0:T(8,128)(2,1)} %copy-done.5, bf16[544,128]{1,0:T(8,128)(2,1)} %copy-done.9, bf16[544,128]{1,0:T(8,128)(2,1)} %copy-done.6, ...), custom_call_target="tpu_custom_call" | custom-call | flops 33554432 | bytes 4194304 | tf_op jit(solution)/shard_map/pallas_call | solution.py:482
  (192 shorter events, 50.9 us)
Async XLA Ops:
  0.0 65.7 %collective-permute-start.32 = (bf16[512,1024]{1,0:T(8,128)(2,1)}, bf16[512,1024]{1,0:T(8,128)(2,1)}, u32[]{:S(2)}, u32[]{:S(2)}) collective-permute-start(bf16[512,1024]{1,0:T(8,128)(2,1)} %refs_8_.1), channel_id=1, source_target_pairs={{0,3},{1,2},{2,1},{3,0},{4,7},{5,6},{6,5},{7,4},{8,11},{9,10},{10,... | collective-permute-start | bytes 3145736 | tf_op jit(solution)/shard_map/ppermute | solution.py:47
  20.5 6.5 %collective-permute-start.13 = (bf16[128,512]{1,0:T(8,128)(2,1)}, bf16[128,512]{1,0:T(8,128)(2,1)S(1)}, u32[]{:S(2)}, u32[]{:S(2)}) collective-permute-start(bf16[128,512]{1,0:T(8,128)(2,1)} %shard_map.136.refs_0_), channel_id=1, source_target_pairs={{0,8},{4,12},{8,0},{12,4},{16,24},{20,28},{24,16},{28,20},{1,9},{5... | collective-permute-start | bytes 393224 | tf_op jit(solution)/shard_map/ppermute | solution.py:47
  21.0 8.5 %collective-permute-start.14 = (bf16[128,512]{1,0:T(8,128)(2,1)}, bf16[128,512]{1,0:T(8,128)(2,1)S(1)}, u32[]{:S(2)}, u32[]{:S(2)}) collective-permute-start(bf16[128,512]{1,0:T(8,128)(2,1)} %shard_map.136.refs_0_), channel_id=1, source_target_pairs={{0,16},{4,20},{8,24},{12,28},{16,0},{20,4},{24,8},{28,12},{1,17},{... | collective-permute-start | bytes 393224 | tf_op jit(solution)/shard_map/ppermute | solution.py:47
  21.5 8.0 %collective-permute-start.15 = (bf16[128,512]{1,0:T(8,128)(2,1)}, bf16[128,512]{1,0:T(8,128)(2,1)S(1)}, u32[]{:S(2)}, u32[]{:S(2)}) collective-permute-start(bf16[128,512]{1,0:T(8,128)(2,1)} %shard_map.136.refs_0_), channel_id=1, source_target_pairs={{0,24},{4,28},{8,16},{12,20},{16,8},{20,12},{24,0},{28,4},{1,25},{... | collective-permute-start | bytes 393224 | tf_op jit(solution)/shard_map/ppermute | solution.py:47
  25.5 14.6 %collective-permute-start.7 = (bf16[128,512]{1,0:T(8,128)(2,1)}, bf16[128,512]{1,0:T(8,128)(2,1)S(1)}, u32[]{:S(2)}, u32[]{:S(2)}) collective-permute-start(bf16[128,512]{1,0:T(8,128)(2,1)} %shard_map.136.refs_0_), channel_id=1, source_target_pairs={{0,1},{1,0},{2,3},{3,2},{4,5},{5,4},{6,7},{7,6},{8,9},{9,8},{10,11... | collective-permute-start | bytes 393224 | tf_op jit(solution)/shard_map/ppermute | solution.py:47
  32.2 5.9 %collective-permute-start.22 = (bf16[288,128]{1,0:T(8,128)(2,1)S(1)}, bf16[288,128]{1,0:T(8,128)(2,1)S(1)}, u32[]{:S(2)}, u32[]{:S(2)}) collective-permute-start(bf16[288,128]{1,0:T(8,128)(2,1)S(1)} %concatenate.34.refs_4_), channel_id=1, source_target_pairs={{0,16},{4,20},{8,24},{12,28},{16,0},{20,4},{24,8},{28,12},{1,17},{... | collective-permute-start | bytes 221192 | tf_op jit(solution)/shard_map/ppermute | solution.py:47
  35.4 55.5 %collective-permute-start.20 = (bf16[512,1024]{1,0:T(8,128)(2,1)}, bf16[512,1024]{1,0:T(8,128)(2,1)}, u32[]{:S(2)}, u32[]{:S(2)}) collective-permute-start(bf16[512,1024]{1,0:T(8,128)(2,1)} %refs_8_.1), channel_id=1, source_target_pairs={{0,1},{1,0},{2,3},{3,2},{4,5},{5,4},{6,7},{7,6},{8,9},{9,8},{10,11... | collective-permute-start | bytes 3145736 | tf_op jit(solution)/shard_map/ppermute | solution.py:47
  38.1 23.9 %collective-permute-start.8 = (bf16[128,512]{1,0:T(8,128)(2,1)}, bf16[128,512]{1,0:T(8,128)(2,1)S(1)}, u32[]{:S(2)}, u32[]{:S(2)}) collective-permute-start(bf16[128,512]{1,0:T(8,128)(2,1)} %shard_map.136.refs_0_), channel_id=1, source_target_pairs={{0,2},{1,3},{2,0},{3,1},{4,6},{5,7},{6,4},{7,5},{8,10},{9,11},{10,... | collective-permute-start | bytes 393224 | tf_op jit(solution)/shard_map/ppermute | solution.py:47
  38.2 26.9 %collective-permute-start.9 = (bf16[128,512]{1,0:T(8,128)(2,1)}, bf16[128,512]{1,0:T(8,128)(2,1)S(1)}, u32[]{:S(2)}, u32[]{:S(2)}) collective-permute-start(bf16[128,512]{1,0:T(8,128)(2,1)} %shard_map.136.refs_0_), channel_id=1, source_target_pairs={{0,3},{1,2},{2,1},{3,0},{4,7},{5,6},{6,5},{7,4},{8,11},{9,10},{10,... | collective-permute-start | bytes 393224 | tf_op jit(solution)/shard_map/ppermute | solution.py:47
  40.1 26.1 %collective-permute-start.24 = (bf16[288,128]{1,0:T(8,128)(2,1)S(1)}, bf16[288,128]{1,0:T(8,128)(2,1)S(1)}, u32[]{:S(2)}, u32[]{:S(2)}) collective-permute-start(bf16[288,128]{1,0:T(8,128)(2,1)S(1)} %concatenate.34.refs_4_), channel_id=1, source_target_pairs={{0,4},{4,0},{8,12},{12,8},{16,20},{20,16},{24,28},{28,24},{1,5},{5... | collective-permute-start | bytes 221192 | tf_op jit(solution)/shard_map/ppermute | solution.py:47
  65.7 29.0 %collective-permute-start.33 = (bf16[512,1024]{1,0:T(8,128)(2,1)}, bf16[512,1024]{1,0:T(8,128)(2,1)}, u32[]{:S(2)}, u32[]{:S(2)}) collective-permute-start(bf16[512,1024]{1,0:T(8,128)(2,1)} %collective-permute-done.32.refs_10_), channel_id=1, source_target_pairs={{0,1},{1,0},{2,3},{3,2},{4,5},{5,4},{6,7},{7,6},{8,9},{9,8},{10,11... | collective-permute-start | bytes 3145736 | tf_op jit(solution)/shard_map/ppermute | solution.py:47
  69.6 12.2 %collective-permute-start.10 = (bf16[128,1536]{1,0:T(8,128)(2,1)}, bf16[128,1536]{1,0:T(8,128)(2,1)S(1)}, u32[]{:S(2)}, u32[]{:S(2)}) collective-permute-start(bf16[128,1536]{1,0:T(8,128)(2,1)} %constant_dynamic-update-slice_fusion.2.refs_0_), channel_id=1, source_target_pairs={{0,8},{4,12},{8,0},{12,4},{16,24},{20,28},{24,16},{28,20},{1,9},{5... | collective-permute-start | bytes 1179656 | tf_op jit(solution)/shard_map/ppermute | solution.py:47
  71.1 19.7 %collective-permute-start.11 = (bf16[128,1536]{1,0:T(8,128)(2,1)}, bf16[128,1536]{1,0:T(8,128)(2,1)S(1)}, u32[]{:S(2)}, u32[]{:S(2)}) collective-permute-start(bf16[128,1536]{1,0:T(8,128)(2,1)} %constant_dynamic-update-slice_fusion.2.refs_0_), channel_id=1, source_target_pairs={{0,16},{4,20},{8,24},{12,28},{16,0},{20,4},{24,8},{28,12},{1,17},{... | collective-permute-start | bytes 1179656 | tf_op jit(solution)/shard_map/ppermute | solution.py:47
  71.6 19.2 %collective-permute-start.12 = (bf16[128,1536]{1,0:T(8,128)(2,1)}, bf16[128,1536]{1,0:T(8,128)(2,1)}, u32[]{:S(2)}, u32[]{:S(2)}) collective-permute-start(bf16[128,1536]{1,0:T(8,128)(2,1)} %constant_dynamic-update-slice_fusion.2.refs_0_), channel_id=1, source_target_pairs={{0,24},{4,28},{8,16},{12,20},{16,8},{20,12},{24,0},{28,4},{1,25},{... | collective-permute-start | bytes 1179656 | tf_op jit(solution)/shard_map/ppermute | solution.py:47
  106.4 5.6 %collective-permute-start.35 = (bf16[144,1024]{1,0:T(8,128)(2,1)}, bf16[144,1024]{1,0:T(8,128)(2,1)S(1)}, u32[]{:S(2)}, u32[]{:S(2)}) collective-permute-start(bf16[144,1024]{1,0:T(8,128)(2,1)} %get-tuple-element.90), channel_id=1, source_target_pairs={{0,4},{4,0},{8,12},{12,8},{16,20},{20,16},{24,28},{28,24},{1,5},{5... | collective-permute-start | bytes 884744 | tf_op jit(solution)/shard_map/ppermute | solution.py:47
  106.5 8.0 %collective-permute-start.34 = (bf16[144,1024]{1,0:T(8,128)(2,1)}, bf16[144,1024]{1,0:T(8,128)(2,1)S(1)}, u32[]{:S(2)}, u32[]{:S(2)}) collective-permute-start(bf16[144,1024]{1,0:T(8,128)(2,1)} %get-tuple-element.88), channel_id=1, source_target_pairs={{0,4},{4,0},{8,12},{12,8},{16,20},{20,16},{24,28},{28,24},{1,5},{5... | collective-permute-start | bytes 884744 | tf_op jit(solution)/shard_map/ppermute | solution.py:47
  108.7 10.9 %collective-permute-start.40 = (bf16[144,1024]{1,0:T(8,128)(2,1)S(1)}, bf16[144,1024]{1,0:T(8,128)(2,1)S(1)}, u32[]{:S(2)}, u32[]{:S(2)}) collective-permute-start(bf16[144,1024]{1,0:T(8,128)(2,1)S(1)} %add_convert_fusion), channel_id=1, source_target_pairs={{0,24},{4,28},{8,16},{12,20},{16,8},{20,12},{24,0},{28,4},{1,25},{... | collective-permute-start | bytes 884744 | tf_op jit(solution)/shard_map/ppermute | solution.py:47
  111.0 14.0 %collective-permute-start.38 = (bf16[144,1024]{1,0:T(8,128)(2,1)S(1)}, bf16[144,1024]{1,0:T(8,128)(2,1)S(1)}, u32[]{:S(2)}, u32[]{:S(2)}) collective-permute-start(bf16[144,1024]{1,0:T(8,128)(2,1)S(1)} %add_convert_fusion.1), channel_id=1, source_target_pairs={{0,16},{4,20},{8,24},{12,28},{16,0},{20,4},{24,8},{28,12},{1,17},{... | collective-permute-start | bytes 884744 | tf_op jit(solution)/shard_map/ppermute | solution.py:47
  113.0 12.1 %collective-permute-start.36 = (bf16[144,1024]{1,0:T(8,128)(2,1)S(1)}, bf16[144,1024]{1,0:T(8,128)(2,1)S(1)}, u32[]{:S(2)}, u32[]{:S(2)}) collective-permute-start(bf16[144,1024]{1,0:T(8,128)(2,1)S(1)} %add_convert_fusion.2), channel_id=1, source_target_pairs={{0,8},{4,12},{8,0},{12,4},{16,24},{20,28},{24,16},{28,20},{1,9},{5... | collective-permute-start | bytes 884744 | tf_op jit(solution)/shard_map/ppermute | solution.py:47
  131.6 9.1 %collective-permute-start.42 = (bf16[288,128]{1,0:T(8,128)(2,1)}, bf16[288,128]{1,0:T(8,128)(2,1)S(1)}, u32[]{:S(2)}, u32[]{:S(2)}) collective-permute-start(bf16[288,128]{1,0:T(8,128)(2,1)} %get-tuple-element.103.refs_0_), channel_id=1, source_target_pairs={{0,2},{1,3},{2,0},{3,1},{4,6},{5,7},{6,4},{7,5},{8,10},{9,11},{10,... | collective-permute-start | bytes 221192 | tf_op jit(solution)/shard_map/ppermute | solution.py:47
  133.1 7.5 %collective-permute-start.43 = (bf16[288,128]{1,0:T(8,128)(2,1)}, bf16[288,128]{1,0:T(8,128)(2,1)S(1)}, u32[]{:S(2)}, u32[]{:S(2)}) collective-permute-start(bf16[288,128]{1,0:T(8,128)(2,1)} %get-tuple-element.103.refs_0_), channel_id=1, source_target_pairs={{0,3},{1,2},{2,1},{3,0},{4,7},{5,6},{6,5},{7,4},{8,11},{9,10},{10,... | collective-permute-start | bytes 221192 | tf_op jit(solution)/shard_map/ppermute | solution.py:47
  143.3 5.6 %collective-permute-start.44 = (bf16[544,128]{1,0:T(8,128)(2,1)}, bf16[544,128]{1,0:T(8,128)(2,1)S(1)}, u32[]{:S(2)}, u32[]{:S(2)}) collective-permute-start(bf16[544,128]{1,0:T(8,128)(2,1)} %get-tuple-element.106), channel_id=1, source_target_pairs={{0,8},{4,12},{8,0},{12,4},{16,24},{20,28},{24,16},{28,20},{1,9},{5... | collective-permute-start | bytes 417800 | tf_op jit(solution)/shard_map/ppermute | solution.py:47
  143.8 7.5 %collective-permute-start.45 = (bf16[544,128]{1,0:T(8,128)(2,1)}, bf16[544,128]{1,0:T(8,128)(2,1)S(1)}, u32[]{:S(2)}, u32[]{:S(2)}) collective-permute-start(bf16[544,128]{1,0:T(8,128)(2,1)} %get-tuple-element.107), channel_id=1, source_target_pairs={{0,16},{4,20},{8,24},{12,28},{16,0},{20,4},{24,8},{28,12},{1,17},{... | collective-permute-start | bytes 417800 | tf_op jit(solution)/shard_map/ppermute | solution.py:47
  145.0 6.3 %collective-permute-start.46 = (bf16[544,128]{1,0:T(8,128)(2,1)}, bf16[544,128]{1,0:T(8,128)(2,1)S(1)}, u32[]{:S(2)}, u32[]{:S(2)}) collective-permute-start(bf16[544,128]{1,0:T(8,128)(2,1)} %get-tuple-element.108), channel_id=1, source_target_pairs={{0,24},{4,28},{8,16},{12,20},{16,8},{20,12},{24,0},{28,4},{1,25},{... | collective-permute-start | bytes 417800 | tf_op jit(solution)/shard_map/ppermute | solution.py:47
  (70 other events, 635.6 us)

commit v2 on v1

--- a/solution.py
+++ b/solution.py
@@ -16,7 +16,9 @@
 CONV = 4
 NORM_EPS = 1e-05
 HALO = 16
-VMEM_LIMIT = 56 * 1024 * 1024
+PAD = 8
+MIB = 1024 * 1024
+VMEM_LIMIT = 56 * MIB
 
 F32 = jnp.float32
 BF16 = jnp.bfloat16
@@ -30,7 +32,7 @@
     return lax.dot_general(lhs, rhs, dims, preferred_element_type=F32)
 
 
-def call(kernel, out_shape, n_in, scratch=(), flops=0, size=0, in_place=None, out_place=pltpu.VMEM):
+def call(kernel, out_shape, n_in, scratch=(), flops=0, size=0, in_place=None, out_place=pltpu.VMEM, limit=16):
     in_place = in_place or [pltpu.VMEM] * n_in
     return pl.pallas_call(
         kernel,
@@ -38,7 +40,7 @@
         in_specs=[pl.BlockSpec(memory_space=place) for place in [pltpu.SMEM] + in_place],
         out_specs=jax.tree.map(lambda _: pl.BlockSpec(memory_space=out_place), out_shape),
         scratch_shapes=list(scratch),
-        compiler_params=pltpu.CompilerParams(vmem_limit_bytes=VMEM_LIMIT),
+        compiler_params=pltpu.CompilerParams(vmem_limit_bytes=min(limit * MIB, VMEM_LIMIT)),
         cost_estimate=pl.CostEstimate(flops=flops, bytes_accessed=size, transcendentals=0),
     )
 
@@ -130,7 +132,7 @@
     rank = rank_ref[0]
     rows = far_refs[0].shape[0]
     width = weight_refs[0].shape[0]
-    channels = in_ref.shape[1]
+    channels = in_ref.shape[0]
     copies = Copies(semaphores)
     weight_copies = [
         copies.start(weight_refs[r], weights.at[pl.ds(r * width, width), :]) for r in range(used)
@@ -173,7 +175,7 @@
             )
     column_copy.wait()
     for t in range(2):
-        result = dot(normed[pl.ds(t * tile, tile), :], columns[...]).astype(BF16)
+        result = dot(normed[pl.ds(t * tile, tile), :], columns[...], NT).astype(BF16)
         mixed[pl.ds(t * tile, tile), :] = result
         for part in range(count // 2):
             k = t * count // 2 + part
@@ -269,6 +271,7 @@
         factor_ref, source_ref, read_ref, value_ref, end_ref, product_ref, begin_ref,
     ) = refs[count:]
     rank = rank_ref[0]
+    pitch = rows + PAD
     lanes = weight_ref.shape[1]
     half = lanes // 2
     groups = NST // 2
@@ -281,6 +284,7 @@
     lane = lax.broadcasted_iota(jnp.int32, (rows, lanes), 1)
     for k in range(count):
         span = slice(k * rows, (k + 1) * rows)
+        padded = slice(k * pitch, k * pitch + rows)
         step = dot(maps_refs[k][:DT_RANK, :], weight_ref[...], TN) + bias_ref[...]
         step = jnp.maximum(step, 0.0) + jnp.log1p(jnp.exp(-jnp.abs(step)))
         pair = pair_refs[k][...].astype(F32)
@@ -292,11 +296,11 @@
         drive = step * value
         for g in range(groups):
             part = slice(g * lanes, (g + 1) * lanes)
-            factor_ref[g, span, :] = jnp.exp(step * decay_ref[:, part])
-            source_ref[g, span, :] = drive * in_map[:, part]
+            factor_ref[g, padded, :] = jnp.exp(step * decay_ref[:, part])
+            source_ref[g, padded, :] = drive * in_map[:, part]
 
     def advance(t, carried):
-        at = pl.ds(t, count, stride=rows)
+        at = pl.ds(t, count, stride=pitch)
         following = []
         for g in range(groups):
             state, product = carried[g]
@@ -326,16 +330,25 @@
         carried = product_ref[at, :] * carried + end_ref[at, :]
     for k in range(count):
         span = slice(k * rows, (k + 1) * rows)
+        padded = slice(k * pitch, k * pitch + rows)
         total = skip_ref[...] * value_ref[span, :]
         readout = jnp.zeros((rows, lanes), F32)
         for g in range(groups):
             part = slice(g * lanes, (g + 1) * lanes)
-            state = source_ref[g, span, :] + factor_ref[g, span, :] * begin_ref[k : k + 1, part]
+            state = source_ref[g, padded, :] + factor_ref[g, padded, :] * begin_ref[k : k + 1, part]
             readout += state * read_ref[span, part]
         total += readout + pltpu.roll(readout, half, 1)
         result = jnp.transpose(total * pair_refs[k][...].astype(F32))
         first = pl.multiple_of(jnp.bitwise_xor(rank, k) * rows, rows)
         out_ref[:, pl.ds(first, rows)] = result[half:].astype(BF16)
+
+
+def scan_arguments(dt_weight, dt_bias, a_log, skip_gain):
+    weight = jnp.concatenate([dt_weight, dt_weight], axis=1)
+    bias = jnp.concatenate([dt_bias, dt_bias]).reshape(1, -1)
+    skip = jnp.concatenate([skip_gain, skip_gain]).reshape(1, -1)
+    decay = (-jnp.exp(a_log)).T.reshape(1, -1)
+    return weight, bias, decay, skip
 
 
 def body(
@@ -360,6 +373,7 @@
     rows = queries.shape[0]
     seq_len = residual.shape[0]
     features = residual.shape[1]
+    scale = -(-seq_len // 1024)
     own = conv_weight.shape[0]
     channels = n_seq * 2 * own
     rank = lax.axis_index("seq").astype(jnp.int32)
@@ -377,6 +391,7 @@
         [pltpu.VMEM((GROUP * rows, seq_len), F32), pltpu.VMEM((seq_len, HD), BF16)],
         flops=4 * GROUP * rows * seq_len * HD,
         size=4 * rows * 4 * HD * n_seq,
+        limit=16 * scale,
     )(rank_arg, queries, *pairs)
 
     far = jnp.concatenate(
@@ -402,7 +417,8 @@
     proj = jnp.transpose(proj, (2, 0, 1)).reshape(-1, 2 * own)
     params = jnp.concatenate([proj, *terms, jnp.zeros((1, 2 * own), BF16)], axis=0)
     params, _ = gather_seq([after(params, attended)] * (n_seq // 2), n_seq)
-    in_columns = jnp.transpose(in_weight, (0, 2, 1, 3)).reshape(features, channels)
+    channel_args = scan_arguments(dt_weight, dt_bias, a_log, skip_gain)
+    in_columns = jnp.transpose(in_weight, (2, 1, 3, 0)).reshape(channels, features)
     far = after(far, in_columns)
 
     acc = call(
@@ -412,13 +428,14 @@
         [pltpu.VMEM((seq_len, width), BF16)],
         flops=2 * seq_len * features * width,
         size=seq_len * features * 8,
+        limit=56,
     )(rank_arg, *own_pieces, out_weight, residual)
     far_pieces, others = gather_seq(
         [far] * (n_seq // 2),
         n_seq,
-        acc, nearest, *params,
-    )
-    acc, weights[1], *params = others
+        acc, nearest, channel_args, *params,
+    )
+    acc, weights[1], channel_args, *params = others
     used = n_sec - 1
     payloads = call(
         functools.partial(mix_kernel, n_seq, used),
@@ -428,7 +445,7 @@
             pltpu.VMEM((seq_len, width * used), BF16),
             pltpu.VMEM((used * width, features), BF16),
             pltpu.VMEM((seq_len, features), F32),
-            pltpu.VMEM((features, channels), BF16),
+            pltpu.VMEM((channels, features), BF16),
             pltpu.VMEM((seq_len, features), BF16),
             pltpu.VMEM((seq_len, channels), BF16),
             pltpu.VMEM((n_seq, HALO, channels), BF16),
@@ -437,6 +454,7 @@
         ],
         flops=2 * seq_len * features * (width * used + channels),
         size=seq_len * features * 12,
+        limit=56,
         in_place=[pl.ANY] * (n_seq + used + 1) + [pltpu.VMEM, pl.ANY],
         out_place=pl.ANY,
     )(
@@ -463,6 +481,7 @@
         [pltpu.VMEM((rows + 8, channels), F32)],
         flops=2 * rows * channels * map_rows,
         size=rows * channels * 12,
+        limit=12 * scale,
     )(rank_arg, *pieces, *params)
 
     map_parts = [maps] + [swap(maps, "section", n_sec, r) for r in range(1, n_sec)]
@@ -471,25 +490,23 @@
         [shape((2 * rows + map_rows, rows), BF16)] * (n_seq // 2),
         n_sec + 1,
         size=map_rows * rows * 2 * n_sec,
+        limit=8 * scale,
     )(rank_arg, *map_parts, outgoing)
     scan_pieces, _ = gather_seq(messages, n_seq)
 
-    weight = jnp.concatenate([dt_weight, dt_weight], axis=1)
-    bias = jnp.concatenate([dt_bias, dt_bias]).reshape(1, -1)
-    skip = jnp.concatenate([skip_gain, skip_gain]).reshape(1, -1)
-    decay = (-jnp.exp(a_log)).T.reshape(1, -1)
     wide = NST * own
     return call(
         functools.partial(scan_kernel, n_seq),
         shape((own, seq_len), BF16),
         n_seq + 4,
-        [pltpu.VMEM((NST // 2, seq_len, 2 * own), F32)] * 2
+        [pltpu.VMEM((NST // 2, n_seq * (rows + PAD), 2 * own), F32)] * 2
         + [pltpu.VMEM((seq_len, wide), F32)]
         + [pltpu.VMEM((seq_len, 2 * own), F32)]
         + [pltpu.VMEM((n_seq, wide), F32)] * 3,
         flops=2 * seq_len * DT_RANK * own,
         size=seq_len * wide * 8,
-    )(rank_arg, *scan_pieces, weight, bias, decay, skip)
+        limit=16 * scale,
+    )(rank_arg, *scan_pieces, *channel_args)
 
 
 def solution(mesh):

time: 167 us -> 150 us (0.90)
  Pallas kernels: 35.5 us -> 22.8 us
  local copies, waits for them, and re-layouts: 13.3 us -> 8.29 us
  waiting for transfers between devices: 71.1 us -> 73.5 us
  other arithmetic: 6.79 us -> 4.81 us
    pallas_call x1, Pallas kernels: 10.6 us -> 3.6 us  [body(): call(functools.partial(scan_kernel, n_seq), shape((own, seq_len), BF16),...]
    unnamed x91 -> x48, local copies, waits for them, and re-layouts: 7.52 us -> 3.96 us
    reshape x2 -> x1, local copies, waits for them, and re-layouts: 3.23 us -> 0.08 us  [scan_arguments(): decay = (-jnp.exp(a_log)).T.reshape(1, -1)]
    ppermute x51, waiting for transfers between devices: 71.1 us -> 73.5 us  [swap(): return lax.ppermute(x, axis, [(i, i ^ bits) for i in range(count)])]
    pallas_call x1, Pallas kernels: 3.09 us -> 1.05 us  [body(): call(functools.partial(conv_kernel, len(pieces), n_seq), [shape((n_seq, r...]
    pallas_call x1, Pallas kernels: 1.97 us -> 0.05 us  [body(): call(functools.partial(sum_kernel, n_sec), [shape((2 * rows + map_rows, r...]
    pallas_call x1, Pallas kernels: 3.09 us -> 1.32 us  [body(): call(functools.partial(attention_kernel, n_seq), shape((rows, GROUP * HD)...]
  transfers between devices with their start and end apart: 51 -> 51, of which waited for: 23 -> 31; matrix products, arithmetic and copies ran while one was open for 10% -> 8% of each run, Pallas kernels for 5% -> 5%
where the time goes in v2:
time: 150 us
  waiting for transfers between devices  73.5 us (49%)
  starting transfers between devices  40.1 us (27%)
  Pallas kernels  22.8 us (15%)
  local copies, waits for them, and re-layouts  8.29 us (6%)
  other arithmetic  4.81 us (3%)
    ppermute x51, waiting for transfers between devices, swap(): return lax.ppermute(x, axis, [(i, i ^ bits) for i in range(count)])  73.5 us
    ppermute x51, starting transfers between devices, swap(): return lax.ppermute(x, axis, [(i, i ^ bits) for i in range(count)])  40.1 us
    pallas_call x1, Pallas kernels, body(): call(functools.partial(mix_kernel, n_seq, used), [shape((HALO + rows, cha...  11.1 us
    pallas_call x1, Pallas kernels, body(): call(functools.partial(own_kernel, n_seq), shape((seq_len, features), F32...  5.65 us
    unnamed x48, local copies, waits for them, and re-layouts  3.96 us
    pallas_call x1, Pallas kernels, body(): call(functools.partial(scan_kernel, n_seq), shape((own, seq_len), BF16),...  3.6 us
    convert_element_type x4, other arithmetic, body(): (payloads[k].astype(F32) + arrived[k + 1].astype(F32)).astype(BF16)  3.17 us
  transfers between devices with their start and end apart: 51, of which 31 were waited for; matrix products, arithmetic and copies ran while one was open for 8% of the time, Pallas kernels for 5%

profile of v2, /device:TPU:0, one launch (start us, length us, event | category | flops | bytes accessed | tf_op | source)
XLA Modules:
  0.0 149.7 jit_solution(4591656716049483579)
XLA Ops:
  0.0 5.0 %collective-permute-start.32 = (bf16[512,1024]{1,0:T(8,128)(2,1)}, bf16[512,1024]{1,0:T(8,128)(2,1)}, u32[]{:S(2)}, u32[]{:S(2)}) collective-permute-start(bf16[512,1024]{1,0:T(8,128)(2,1)} %refs_8_.1), channel_id=1, source_target_pairs={{0,3},{1,2},{2,1},{3,0},{4,7},{5,6},{6,5},{7,4},{8,11},{9,10},{10,... | collective-permute-start | bytes 3145736 | tf_op jit(solution)/shard_map/ppermute | solution.py:49
  6.6 2.5 %collective-permute-start.2 = (bf16[128,256]{1,0:T(8,128)(2,1)S(1)}, bf16[128,256]{1,0:T(8,128)(2,1)S(1)}, u32[]{:S(2)}, u32[]{:S(2)}) collective-permute-start(bf16[128,256]{1,0:T(8,128)(2,1)S(1)} %constant_dynamic-update-slice_fusion.refs_0_), channel_id=1, source_target_pairs={{0,24},{4,28},{8,16},{12,20},{16,8},{20,12},{24,0},{28,4},{1,25},{... | collective-permute-start | bytes 196616 | tf_op jit(solution)/shard_map/ppermute | solution.py:49
  10.1 1.8 %collective-permute-done.2.refs_6_ = bf16[128,256]{1,0:T(8,128)(2,1)S(1)} collective-permute-done((bf16[128,256]{1,0:T(8,128)(2,1)S(1)}, bf16[128,256]{1,0:T(8,128)(2,1)S(1)}, u32[]{:S(2)}, u32[]{:S(2)}) %collective-permute-start.2) | collective-permute-done | bytes 65568 | tf_op jit(solution)/shard_map/ppermute | solution.py:49
  23.2 2.2 %collective-permute-done.15.refs_6_ = bf16[128,512]{1,0:T(8,128)(2,1)S(1)} collective-permute-done((bf16[128,512]{1,0:T(8,128)(2,1)S(1)}, bf16[128,512]{1,0:T(8,128)(2,1)S(1)}, u32[]{:S(2)}, u32[]{:S(2)}) %collective-permute-start.15) | collective-permute-done | bytes 131104 | tf_op jit(solution)/shard_map/ppermute | solution.py:49
  25.4 2.2 %collective-permute-done.14.refs_4_ = bf16[128,512]{1,0:T(8,128)(2,1)S(1)} collective-permute-done((bf16[128,512]{1,0:T(8,128)(2,1)S(1)}, bf16[128,512]{1,0:T(8,128)(2,1)S(1)}, u32[]{:S(2)}, u32[]{:S(2)}) %collective-permute-start.14) | collective-permute-done | bytes 131104 | tf_op jit(solution)/shard_map/ppermute | solution.py:49
  29.0 1.6 %collective-permute-start.23 = (bf16[288,128]{1,0:T(8,128)(2,1)S(1)}, bf16[288,128]{1,0:T(8,128)(2,1)S(1)}, u32[]{:S(2)}, u32[]{:S(2)}) collective-permute-start(bf16[288,128]{1,0:T(8,128)(2,1)S(1)} %concatenate.37.refs_4_), channel_id=1, source_target_pairs={{0,24},{4,28},{8,16},{12,20},{16,8},{20,12},{24,0},{28,4},{1,25},{... | collective-permute-start | bytes 221192 | tf_op jit(solution)/shard_map/ppermute | solution.py:49
  32.5 2.1 %collective-permute-done.23.refs_10_ = bf16[288,128]{1,0:T(8,128)(2,1)S(1)} collective-permute-done((bf16[288,128]{1,0:T(8,128)(2,1)S(1)}, bf16[288,128]{1,0:T(8,128)(2,1)S(1)}, u32[]{:S(2)}, u32[]{:S(2)}) %collective-permute-start.23) | collective-permute-done | bytes 73760 | tf_op jit(solution)/shard_map/ppermute | solution.py:49
  36.3 1.8 %collective-permute-start.8 = (bf16[128,512]{1,0:T(8,128)(2,1)S(1)}, bf16[128,512]{1,0:T(8,128)(2,1)S(1)}, u32[]{:S(2)}, u32[]{:S(2)}) collective-permute-start(bf16[128,512]{1,0:T(8,128)(2,1)S(1)} %shard_map.136.refs_0_), channel_id=1, source_target_pairs={{0,2},{1,3},{2,0},{3,1},{4,6},{5,7},{6,4},{7,5},{8,10},{9,11},{10,... | collective-permute-start | bytes 393224 | tf_op jit(solution)/shard_map/ppermute | solution.py:49
  38.9 23.8 %collective-permute-done.9 = bf16[128,512]{1,0:T(8,128)(2,1)S(1)} collective-permute-done((bf16[128,512]{1,0:T(8,128)(2,1)S(1)}, bf16[128,512]{1,0:T(8,128)(2,1)S(1)}, u32[]{:S(2)}, u32[]{:S(2)}) %collective-permute-start.9) | collective-permute-done | bytes 131104 | tf_op jit(solution)/shard_map/ppermute | solution.py:49
  67.0 1.6 %copy.19 = bf16[8,2,64,1024]{3,2,1,0:T(8,128)(2,1)} copy(bf16[8,2,64,1024]{3,2,0,1:T(8,128)(2,1)S(1)} %bitcast.19) | data formatting | bytes 4194304 | tf_op jit(solution)/shard_map/transpose | solution.py:421
  72.6 5.7 %shard_map.137.refs_11_ = f32[1024,1024]{1,0:T(8,128)} custom-call(s32[1]{0:T(128)} %bitcast.rank_ref, bf16[128,512]{1,0:T(8,128)(2,1)} %copy-done, bf16[128,512]{1,0:T(8,128)(2,1)} %copy-done.8, bf16[128,512]{1,0:T(8,128)(2,1)} %copy-done.6, bf16[128,512]{1,0:T(8,128)(2,1)} %copy-done.9, bf16[128,512]{1,0:T(8,128)(2,1)} %copy-done.5, ...), custom_call_target="tpu_custom_call" | custom-call | flops 1073741824 | bytes 8388608 | tf_op jit(solution)/shard_map/pallas_call | solution.py:424
  78.2 3.5 %collective-permute-done.12.refs_6_ = bf16[128,1536]{1,0:T(8,128)(2,1)S(1)} collective-permute-done((bf16[128,1536]{1,0:T(8,128)(2,1)}, bf16[128,1536]{1,0:T(8,128)(2,1)S(1)}, u32[]{:S(2)}, u32[]{:S(2)}) %collective-permute-start.12) | collective-permute-done | bytes 393248 | tf_op jit(solution)/shard_map/ppermute | solution.py:49
  81.8 7.6 %collective-permute-done.11.refs_4_ = bf16[128,1536]{1,0:T(8,128)(2,1)S(1)} collective-permute-done((bf16[128,1536]{1,0:T(8,128)(2,1)}, bf16[128,1536]{1,0:T(8,128)(2,1)S(1)}, u32[]{:S(2)}, u32[]{:S(2)}) %collective-permute-start.11) | collective-permute-done | bytes 393248 | tf_op jit(solution)/shard_map/ppermute | solution.py:49
  93.7 11.1 %shard_map.138 = (bf16[144,1024]{1,0:T(8,128)(2,1)}, bf16[144,1024]{1,0:T(8,128)(2,1)}, bf16[144,1024]{1,0:T(8,128)(2,1)}, bf16[144,1024]{1,0:T(8,128)(2,1)}, bf...) custom-call(s32[1]{0:T(128)} %bitcast.rank_ref, ...), custom_call_target="tpu_custom_call" | custom-call | flops 5368709120 | bytes 12582912 | tf_op jit(solution)/shard_map/pallas_call | solution.py:440
  111.8 1.6 %collective-permute-start.40 = (bf16[144,1024]{1,0:T(8,128)(2,1)S(1)}, bf16[144,1024]{1,0:T(8,128)(2,1)S(1)}, u32[]{:S(2)}, u32[]{:S(2)}) collective-permute-start(bf16[144,1024]{1,0:T(8,128)(2,1)S(1)} %add_convert_fusion), channel_id=1, source_target_pairs={{0,24},{4,28},{8,16},{12,20},{16,8},{20,12},{24,0},{28,4},{1,25},{... | collective-permute-start | bytes 884744 | tf_op jit(solution)/shard_map/ppermute | solution.py:49
  113.5 4.1 %collective-permute-done.36.refs_1_ = bf16[144,1024]{1,0:T(8,128)(2,1)S(1)} collective-permute-done((bf16[144,1024]{1,0:T(8,128)(2,1)S(1)}, bf16[144,1024]{1,0:T(8,128)(2,1)S(1)}, u32[]{:S(2)}, u32[]{:S(2)}) %collective-permute-start.36) | collective-permute-done | bytes 294944 | tf_op jit(solution)/shard_map/ppermute | solution.py:49
  117.6 6.9 %collective-permute-done.38.refs_2_ = bf16[144,1024]{1,0:T(8,128)(2,1)S(1)} collective-permute-done((bf16[144,1024]{1,0:T(8,128)(2,1)S(1)}, bf16[144,1024]{1,0:T(8,128)(2,1)S(1)}, u32[]{:S(2)}, u32[]{:S(2)}) %collective-permute-start.38) | collective-permute-done | bytes 294944 | tf_op jit(solution)/shard_map/ppermute | solution.py:49
  125.5 3.3 %collective-permute-start.43 = (bf16[288,128]{1,0:T(8,128)(2,1)S(1)}, bf16[288,128]{1,0:T(8,128)(2,1)S(1)}, u32[]{:S(2)}, u32[]{:S(2)}) collective-permute-start(bf16[288,128]{1,0:T(8,128)(2,1)S(1)} %get-tuple-element.107.refs_0_), channel_id=1, source_target_pairs={{0,3},{1,2},{2,1},{3,0},{4,7},{5,6},{6,5},{7,4},{8,11},{9,10},{10,... | collective-permute-start | bytes 221192 | tf_op jit(solution)/shard_map/ppermute | solution.py:49
  130.0 2.2 %collective-permute-done.43.refs_3_ = bf16[288,128]{1,0:T(8,128)(2,1)S(1)} collective-permute-done((bf16[288,128]{1,0:T(8,128)(2,1)S(1)}, bf16[288,128]{1,0:T(8,128)(2,1)S(1)}, u32[]{:S(2)}, u32[]{:S(2)}) %collective-permute-start.43) | collective-permute-done | bytes 73760 | tf_op jit(solution)/shard_map/ppermute | solution.py:49
  132.1 2.0 %collective-permute-done.42.refs_2_ = bf16[288,128]{1,0:T(8,128)(2,1)S(1)} collective-permute-done((bf16[288,128]{1,0:T(8,128)(2,1)S(1)}, bf16[288,128]{1,0:T(8,128)(2,1)S(1)}, u32[]{:S(2)}, u32[]{:S(2)}) %collective-permute-start.42) | collective-permute-done | bytes 73760 | tf_op jit(solution)/shard_map/ppermute | solution.py:49
  134.2 2.0 %collective-permute-start.44 = (bf16[544,128]{1,0:T(8,128)(2,1)S(1)}, bf16[544,128]{1,0:T(8,128)(2,1)S(1)}, u32[]{:S(2)}, u32[]{:S(2)}) collective-permute-start(bf16[544,128]{1,0:T(8,128)(2,1)S(1)} %get-tuple-element.110), channel_id=1, source_target_pairs={{0,8},{4,12},{8,0},{12,4},{16,24},{20,28},{24,16},{28,20},{1,9},{5... | collective-permute-start | bytes 417800 | tf_op jit(solution)/shard_map/ppermute | solution.py:49
  137.7 2.6 %collective-permute-done.44.refs_2_ = bf16[544,128]{1,0:T(8,128)(2,1)S(1)} collective-permute-done((bf16[544,128]{1,0:T(8,128)(2,1)S(1)}, bf16[544,128]{1,0:T(8,128)(2,1)S(1)}, u32[]{:S(2)}, u32[]{:S(2)}) %collective-permute-start.44) | collective-permute-done | bytes 139296 | tf_op jit(solution)/shard_map/ppermute | solution.py:49
  140.3 3.7 %collective-permute-done.45.refs_4_ = bf16[544,128]{1,0:T(8,128)(2,1)S(1)} collective-permute-done((bf16[544,128]{1,0:T(8,128)(2,1)S(1)}, bf16[544,128]{1,0:T(8,128)(2,1)S(1)}, u32[]{:S(2)}, u32[]{:S(2)}) %collective-permute-start.45) | collective-permute-done | bytes 139296 | tf_op jit(solution)/shard_map/ppermute | solution.py:49
  146.1 3.6 %shard_map.141 = bf16[64,1024]{1,0:T(8,128)(2,1)} custom-call(s32[1]{0:T(128)} %bitcast.rank_ref, bf16[544,128]{1,0:T(8,128)(2,1)S(1)} %get-tuple-element.113.refs_0_, bf16[544,128]{1,0:T(8,128)(2,1)S(1)} %collective-permute-done.47.refs_1_, bf16[544,128]{1,0:T(8,128)(2,1)S(1)} %collective-permute-done.44.refs_2_, ...), custom_call_target="tpu_custom_call" | custom-call | flops 33554432 | bytes 4194304 | tf_op jit(solution)/shard_map/pallas_call | solution.py:498
  (149 shorter events, 45.1 us)
Async XLA Ops:
  0.0 64.6 %collective-permute-start.32 = (bf16[512,1024]{1,0:T(8,128)(2,1)}, bf16[512,1024]{1,0:T(8,128)(2,1)}, u32[]{:S(2)}, u32[]{:S(2)}) collective-permute-start(bf16[512,1024]{1,0:T(8,128)(2,1)} %refs_8_.1), channel_id=1, source_target_pairs={{0,3},{1,2},{2,1},{3,0},{4,7},{5,6},{6,5},{7,4},{8,11},{9,10},{10,... | collective-permute-start | bytes 3145736 | tf_op jit(solution)/shard_map/ppermute | solution.py:49
  18.0 7.3 %collective-permute-start.15 = (bf16[128,512]{1,0:T(8,128)(2,1)S(1)}, bf16[128,512]{1,0:T(8,128)(2,1)S(1)}, u32[]{:S(2)}, u32[]{:S(2)}) collective-permute-start(bf16[128,512]{1,0:T(8,128)(2,1)S(1)} %shard_map.136.refs_0_), channel_id=1, source_target_pairs={{0,24},{4,28},{8,16},{12,20},{16,8},{20,12},{24,0},{28,4},{1,25},{... | collective-permute-start | bytes 393224 | tf_op jit(solution)/shard_map/ppermute | solution.py:49
  19.6 8.0 %collective-permute-start.14 = (bf16[128,512]{1,0:T(8,128)(2,1)S(1)}, bf16[128,512]{1,0:T(8,128)(2,1)S(1)}, u32[]{:S(2)}, u32[]{:S(2)}) collective-permute-start(bf16[128,512]{1,0:T(8,128)(2,1)S(1)} %shard_map.136.refs_0_), channel_id=1, source_target_pairs={{0,16},{4,20},{8,24},{12,28},{16,0},{20,4},{24,8},{28,12},{1,17},{... | collective-permute-start | bytes 393224 | tf_op jit(solution)/shard_map/ppermute | solution.py:49
  20.1 7.6 %collective-permute-start.13 = (bf16[128,512]{1,0:T(8,128)(2,1)S(1)}, bf16[128,512]{1,0:T(8,128)(2,1)S(1)}, u32[]{:S(2)}, u32[]{:S(2)}) collective-permute-start(bf16[128,512]{1,0:T(8,128)(2,1)S(1)} %shard_map.136.refs_0_), channel_id=1, source_target_pairs={{0,8},{4,12},{8,0},{12,4},{16,24},{20,28},{24,16},{28,20},{1,9},{5... | collective-permute-start | bytes 393224 | tf_op jit(solution)/shard_map/ppermute | solution.py:49
  23.1 15.1 %collective-permute-start.7 = (bf16[128,512]{1,0:T(8,128)(2,1)S(1)}, bf16[128,512]{1,0:T(8,128)(2,1)S(1)}, u32[]{:S(2)}, u32[]{:S(2)}) collective-permute-start(bf16[128,512]{1,0:T(8,128)(2,1)S(1)} %shard_map.136.refs_0_), channel_id=1, source_target_pairs={{0,1},{1,0},{2,3},{3,2},{4,5},{5,4},{6,7},{7,6},{8,9},{9,8},{10,11... | collective-permute-start | bytes 393224 | tf_op jit(solution)/shard_map/ppermute | solution.py:49
  29.0 5.7 %collective-permute-start.23 = (bf16[288,128]{1,0:T(8,128)(2,1)S(1)}, bf16[288,128]{1,0:T(8,128)(2,1)S(1)}, u32[]{:S(2)}, u32[]{:S(2)}) collective-permute-start(bf16[288,128]{1,0:T(8,128)(2,1)S(1)} %concatenate.37.refs_4_), channel_id=1, source_target_pairs={{0,24},{4,28},{8,16},{12,20},{16,8},{20,12},{24,0},{28,4},{1,25},{... | collective-permute-start | bytes 221192 | tf_op jit(solution)/shard_map/ppermute | solution.py:49
  34.7 54.7 %collective-permute-start.20 = (bf16[512,1024]{1,0:T(8,128)(2,1)}, bf16[512,1024]{1,0:T(8,128)(2,1)}, u32[]{:S(2)}, u32[]{:S(2)}) collective-permute-start(bf16[512,1024]{1,0:T(8,128)(2,1)} %refs_8_.1), channel_id=1, source_target_pairs={{0,1},{1,0},{2,3},{3,2},{4,5},{5,4},{6,7},{7,6},{8,9},{9,8},{10,11... | collective-permute-start | bytes 3145736 | tf_op jit(solution)/shard_map/ppermute | solution.py:49
  36.1 26.5 %collective-permute-start.9 = (bf16[128,512]{1,0:T(8,128)(2,1)S(1)}, bf16[128,512]{1,0:T(8,128)(2,1)S(1)}, u32[]{:S(2)}, u32[]{:S(2)}) collective-permute-start(bf16[128,512]{1,0:T(8,128)(2,1)S(1)} %shard_map.136.refs_0_), channel_id=1, source_target_pairs={{0,3},{1,2},{2,1},{3,0},{4,7},{5,6},{6,5},{7,4},{8,11},{9,10},{10,... | collective-permute-start | bytes 393224 | tf_op jit(solution)/shard_map/ppermute | solution.py:49
  36.3 26.5 %collective-permute-start.8 = (bf16[128,512]{1,0:T(8,128)(2,1)S(1)}, bf16[128,512]{1,0:T(8,128)(2,1)S(1)}, u32[]{:S(2)}, u32[]{:S(2)}) collective-permute-start(bf16[128,512]{1,0:T(8,128)(2,1)S(1)} %shard_map.136.refs_0_), channel_id=1, source_target_pairs={{0,2},{1,3},{2,0},{3,1},{4,6},{5,7},{6,4},{7,5},{8,10},{9,11},{10,... | collective-permute-start | bytes 393224 | tf_op jit(solution)/shard_map/ppermute | solution.py:49
  38.2 25.7 %collective-permute-start.24 = (bf16[288,128]{1,0:T(8,128)(2,1)S(1)}, bf16[288,128]{1,0:T(8,128)(2,1)S(1)}, u32[]{:S(2)}, u32[]{:S(2)}) collective-permute-start(bf16[288,128]{1,0:T(8,128)(2,1)S(1)} %concatenate.37.refs_4_), channel_id=1, source_target_pairs={{0,4},{4,0},{8,12},{12,8},{16,20},{20,16},{24,28},{28,24},{1,5},{5... | collective-permute-start | bytes 221192 | tf_op jit(solution)/shard_map/ppermute | solution.py:49
  64.4 5.7 %collective-permute-start.17 = (bf16[128,512]{1,0:T(8,128)(2,1)S(1)}, bf16[128,512]{1,0:T(8,128)(2,1)S(1)}, u32[]{:S(2)}, u32[]{:S(2)}) collective-permute-start(bf16[128,512]{1,0:T(8,128)(2,1)S(1)} %collective-permute-done.13.refs_2_), channel_id=1, source_target_pairs={{0,4},{4,0},{8,12},{12,8},{16,20},{20,16},{24,28},{28,24},{1,5},{5... | collective-permute-start | bytes 393224 | tf_op jit(solution)/shard_map/ppermute | solution.py:49
  64.6 6.1 %collective-permute-start.18 = (bf16[128,512]{1,0:T(8,128)(2,1)S(1)}, bf16[128,512]{1,0:T(8,128)(2,1)S(1)}, u32[]{:S(2)}, u32[]{:S(2)}) collective-permute-start(bf16[128,512]{1,0:T(8,128)(2,1)S(1)} %collective-permute-done.14.refs_4_), channel_id=1, source_target_pairs={{0,4},{4,0},{8,12},{12,8},{16,20},{20,16},{24,28},{28,24},{1,5},{5... | collective-permute-start | bytes 393224 | tf_op jit(solution)/shard_map/ppermute | solution.py:49
  65.5 27.4 %collective-permute-start.33 = (bf16[512,1024]{1,0:T(8,128)(2,1)}, bf16[512,1024]{1,0:T(8,128)(2,1)}, u32[]{:S(2)}, u32[]{:S(2)}) collective-permute-start(bf16[512,1024]{1,0:T(8,128)(2,1)} %collective-permute-done.32.refs_10_), channel_id=1, source_target_pairs={{0,1},{1,0},{2,3},{3,2},{4,5},{5,4},{6,7},{7,6},{8,9},{9,8},{10,11... | collective-permute-start | bytes 3145736 | tf_op jit(solution)/shard_map/ppermute | solution.py:49
  68.6 13.2 %collective-permute-start.12 = (bf16[128,1536]{1,0:T(8,128)(2,1)}, bf16[128,1536]{1,0:T(8,128)(2,1)S(1)}, u32[]{:S(2)}, u32[]{:S(2)}) collective-permute-start(bf16[128,1536]{1,0:T(8,128)(2,1)} %constant_dynamic-update-slice_fusion.2.refs_0_), channel_id=1, source_target_pairs={{0,24},{4,28},{8,16},{12,20},{16,8},{20,12},{24,0},{28,4},{1,25},{... | collective-permute-start | bytes 1179656 | tf_op jit(solution)/shard_map/ppermute | solution.py:49
  70.0 19.4 %collective-permute-start.11 = (bf16[128,1536]{1,0:T(8,128)(2,1)}, bf16[128,1536]{1,0:T(8,128)(2,1)S(1)}, u32[]{:S(2)}, u32[]{:S(2)}) collective-permute-start(bf16[128,1536]{1,0:T(8,128)(2,1)} %constant_dynamic-update-slice_fusion.2.refs_0_), channel_id=1, source_target_pairs={{0,16},{4,20},{8,24},{12,28},{16,0},{20,4},{24,8},{28,12},{1,17},{... | collective-permute-start | bytes 1179656 | tf_op jit(solution)/shard_map/ppermute | solution.py:49
  70.7 18.7 %collective-permute-start.10 = (bf16[128,1536]{1,0:T(8,128)(2,1)}, bf16[128,1536]{1,0:T(8,128)(2,1)S(1)}, u32[]{:S(2)}, u32[]{:S(2)}) collective-permute-start(bf16[128,1536]{1,0:T(8,128)(2,1)} %constant_dynamic-update-slice_fusion.2.refs_0_), channel_id=1, source_target_pairs={{0,8},{4,12},{8,0},{12,4},{16,24},{20,28},{24,16},{28,20},{1,9},{5... | collective-permute-start | bytes 1179656 | tf_op jit(solution)/shard_map/ppermute | solution.py:49
  105.4 8.1 %collective-permute-start.34 = (bf16[144,1024]{1,0:T(8,128)(2,1)}, bf16[144,1024]{1,0:T(8,128)(2,1)S(1)}, u32[]{:S(2)}, u32[]{:S(2)}) collective-permute-start(bf16[144,1024]{1,0:T(8,128)(2,1)} %get-tuple-element.92), channel_id=1, source_target_pairs={{0,4},{4,0},{8,12},{12,8},{16,20},{20,16},{24,28},{28,24},{1,5},{5... | collective-permute-start | bytes 884744 | tf_op jit(solution)/shard_map/ppermute | solution.py:49
  107.7 9.9 %collective-permute-start.36 = (bf16[144,1024]{1,0:T(8,128)(2,1)S(1)}, bf16[144,1024]{1,0:T(8,128)(2,1)S(1)}, u32[]{:S(2)}, u32[]{:S(2)}) collective-permute-start(bf16[144,1024]{1,0:T(8,128)(2,1)S(1)} %add_convert_fusion.2), channel_id=1, source_target_pairs={{0,8},{4,12},{8,0},{12,4},{16,24},{20,28},{24,16},{28,20},{1,9},{5... | collective-permute-start | bytes 884744 | tf_op jit(solution)/shard_map/ppermute | solution.py:49
  109.3 15.2 %collective-permute-start.38 = (bf16[144,1024]{1,0:T(8,128)(2,1)S(1)}, bf16[144,1024]{1,0:T(8,128)(2,1)S(1)}, u32[]{:S(2)}, u32[]{:S(2)}) collective-permute-start(bf16[144,1024]{1,0:T(8,128)(2,1)S(1)} %add_convert_fusion.1), channel_id=1, source_target_pairs={{0,16},{4,20},{8,24},{12,28},{16,0},{20,4},{24,8},{28,12},{1,17},{... | collective-permute-start | bytes 884744 | tf_op jit(solution)/shard_map/ppermute | solution.py:49
  111.8 12.7 %collective-permute-start.40 = (bf16[144,1024]{1,0:T(8,128)(2,1)S(1)}, bf16[144,1024]{1,0:T(8,128)(2,1)S(1)}, u32[]{:S(2)}, u32[]{:S(2)}) collective-permute-start(bf16[144,1024]{1,0:T(8,128)(2,1)S(1)} %add_convert_fusion), channel_id=1, source_target_pairs={{0,24},{4,28},{8,16},{12,20},{16,8},{20,12},{24,0},{28,4},{1,25},{... | collective-permute-start | bytes 884744 | tf_op jit(solution)/shard_map/ppermute | solution.py:49
  125.5 6.6 %collective-permute-start.43 = (bf16[288,128]{1,0:T(8,128)(2,1)S(1)}, bf16[288,128]{1,0:T(8,128)(2,1)S(1)}, u32[]{:S(2)}, u32[]{:S(2)}) collective-permute-start(bf16[288,128]{1,0:T(8,128)(2,1)S(1)} %get-tuple-element.107.refs_0_), channel_id=1, source_target_pairs={{0,3},{1,2},{2,1},{3,0},{4,7},{5,6},{6,5},{7,4},{8,11},{9,10},{10,... | collective-permute-start | bytes 221192 | tf_op jit(solution)/shard_map/ppermute | solution.py:49
  134.2 6.1 %collective-permute-start.44 = (bf16[544,128]{1,0:T(8,128)(2,1)S(1)}, bf16[544,128]{1,0:T(8,128)(2,1)S(1)}, u32[]{:S(2)}, u32[]{:S(2)}) collective-permute-start(bf16[544,128]{1,0:T(8,128)(2,1)S(1)} %get-tuple-element.110), channel_id=1, source_target_pairs={{0,8},{4,12},{8,0},{12,4},{16,24},{20,28},{24,16},{28,20},{1,9},{5... | collective-permute-start | bytes 417800 | tf_op jit(solution)/shard_map/ppermute | solution.py:49
  136.2 7.9 %collective-permute-start.45 = (bf16[544,128]{1,0:T(8,128)(2,1)S(1)}, bf16[544,128]{1,0:T(8,128)(2,1)S(1)}, u32[]{:S(2)}, u32[]{:S(2)}) collective-permute-start(bf16[544,128]{1,0:T(8,128)(2,1)S(1)} %get-tuple-element.111), channel_id=1, source_target_pairs={{0,16},{4,20},{8,24},{12,28},{16,0},{20,4},{24,8},{28,12},{1,17},{... | collective-permute-start | bytes 417800 | tf_op jit(solution)/shard_map/ppermute | solution.py:49
  137.0 7.1 %collective-permute-start.46 = (bf16[544,128]{1,0:T(8,128)(2,1)S(1)}, bf16[544,128]{1,0:T(8,128)(2,1)S(1)}, u32[]{:S(2)}, u32[]{:S(2)}) collective-permute-start(bf16[544,128]{1,0:T(8,128)(2,1)S(1)} %get-tuple-element.112), channel_id=1, source_target_pairs={{0,24},{4,28},{8,16},{12,20},{16,8},{20,12},{24,0},{28,4},{1,25},{... | collective-permute-start | bytes 417800 | tf_op jit(solution)/shard_map/ppermute | solution.py:49
  (49 other events, 403.1 us)

commit v3 on v2

--- a/solution.py
+++ b/solution.py
@@ -92,6 +92,18 @@
         out_ref[:, g * HD : (g + 1) * HD] = result[g * rows : (g + 1) * rows, :]
 
 
+def partner_sums(blocks, count):
+    arrived = [swap(blocks[k + 1], "seq", count, 1) for k in range(0, count, 2)]
+    return [
+        (blocks[k].astype(F32) + arrived[k // 2].astype(F32)).astype(BF16)
+        for k in range(0, count, 2)
+    ]
+
+
+def owner_pieces(sums, count):
+    return [sums[0]] + [swap(sums[k // 2], "seq", count, k) for k in range(2, count, 2)]
+
+
 class Copies:
     def __init__(self, semaphores):
         self.semaphores = semaphores
@@ -127,18 +139,18 @@
     weight_refs = refs[count : count + used]
     refs = refs[count + used :]
     acc_ref, gain_ref, in_ref = refs[:3]
-    out_refs = refs[3 : count + 3]
-    left, weights, acc, columns, normed, mixed, halos, squares, semaphores = refs[count + 3 :]
+    path_refs, gate_refs = refs[3 : count + 3], refs[count + 3 : 2 * count + 3]
+    left, weights, normed, mixed, halos, squares, semaphores = refs[2 * count + 3 :]
     rank = rank_ref[0]
     rows = far_refs[0].shape[0]
     width = weight_refs[0].shape[0]
-    channels = in_ref.shape[0]
+    channels = in_ref.shape[0] // 2
     copies = Copies(semaphores)
     weight_copies = [
         copies.start(weight_refs[r], weights.at[pl.ds(r * width, width), :]) for r in range(used)
     ]
     tile = rows * count // 2
-    left_copies, acc_copies, out_copies = [], [], []
+    left_copies, out_copies = [], []
     for t in range(2):
         left_copies.append(
             [
@@ -149,9 +161,6 @@
                 for k in range(t * count // 2, (t + 1) * count // 2)
             ]
         )
-        span = pl.ds(t * tile, tile)
-        acc_copies.append(copies.start(acc_ref.at[span, :], acc.at[span, :]))
-    column_copy = copies.start(in_ref, columns)
     for copy in weight_copies:
         copy.wait()
     eye = lax.broadcasted_iota(jnp.int32, (rows, rows), 0) == lax.broadcasted_iota(
@@ -162,8 +171,7 @@
         for copy in left_copies[t]:
             copy.wait()
         total = dot(left[span, :], weights[...])
-        acc_copies[t].wait()
-        hidden = acc[span, :] + total
+        hidden = acc_ref[span, :] + total
         normed[span, :] = (hidden * gain_ref[...]).astype(BF16)
         sums = jnp.sum(hidden * hidden, axis=1, keepdims=True)
         for part in range(count // 2):
@@ -173,28 +181,26 @@
                 axis=0,
                 keepdims=True,
             )
-    column_copy.wait()
     for t in range(2):
-        result = dot(normed[pl.ds(t * tile, tile), :], columns[...], NT).astype(BF16)
+        result = dot(normed[pl.ds(t * tile, tile), :], in_ref[...], NT).astype(BF16)
         mixed[pl.ds(t * tile, tile), :] = result
         for part in range(count // 2):
             k = t * count // 2 + part
-            out_copies.append(
-                copies.start(
-                    mixed.at[pl.ds(k * rows, rows), :], out_refs[k].at[pl.ds(HALO, rows), :]
-                )
-            )
+            block = mixed.at[pl.ds(k * rows, rows), :]
+            target = path_refs[k].at[pl.ds(HALO, rows), :]
+            out_copies.append(copies.start(block.at[:, pl.ds(0, channels)], target))
+            out_copies.append(copies.start(block.at[:, pl.ds(channels, channels)], gate_refs[k]))
     line = lax.broadcasted_iota(jnp.int32, (HALO, channels), 0)
     for k in range(count):
         block = jnp.bitwise_xor(rank, k)
         before = jnp.bitwise_xor(rank, jnp.maximum(block - 1, 0))
         last = pl.multiple_of(before * rows + (rows - HALO), HALO)
-        halo = mixed[pl.ds(last, HALO), :].astype(F32)
+        halo = mixed[pl.ds(last, HALO), :channels].astype(F32)
         own = jnp.tile(squares[k : k + 1, :], (1, channels // rows))
         past = jnp.tile(squares[pl.ds(before, 1), :], (1, channels // rows))
         halo = jnp.where(line == 0, own, jnp.where(line == 1, past, halo))
         halos[k] = halo.astype(BF16)
-        out_copies.append(copies.start(halos.at[k], out_refs[k].at[pl.ds(0, HALO), :]))
+        out_copies.append(copies.start(halos.at[k], path_refs[k].at[pl.ds(0, HALO), :]))
     for copy in out_copies:
         copy.wait()
 
@@ -202,7 +208,7 @@
 def conv_kernel(n_pieces, count, rank_ref, *refs):
     piece_refs = refs[:n_pieces]
     param_refs = refs[n_pieces : n_pieces + count]
-    out_ref, maps_ref, total_ref = refs[n_pieces + count :]
+    out_ref, maps_ref, scale_ref, total_ref = refs[n_pieces + count :]
     rank = rank_ref[0]
     total = piece_refs[0][...].astype(F32)
     for piece in piece_refs[1:]:
@@ -216,23 +222,29 @@
     scale_past = jnp.where(rank == 0, 0.0, scale_past)
     column_own = jnp.sum(jnp.where(eye, scale_own, 0.0), axis=1, keepdims=True)
     column_past = jnp.sum(jnp.where(eye, scale_past, 0.0), axis=1, keepdims=True)
+    scale_ref[...] = column_own + jnp.zeros(scale_ref.shape, F32)
     total_ref[0:8, :] = total[HALO - 8 : HALO] * column_past[rows - 8 :]
     total_ref[8:, :] = total[HALO:] * column_own
-    group = out_ref.shape[2]
+    param_rows, group = param_refs[0].shape
     middle = DT_RANK + 2 * NST
+    lane = lax.broadcasted_iota(jnp.int32, (param_rows, group), 1)
+    parity = lane // (group // 2) == rank % 2
     projected = jnp.zeros((middle, rows), F32)
-    for k in range(count):
-        first = pl.multiple_of(jnp.bitwise_xor(rank, k) * group, group)
+    for m in range(count // 2):
+        first = pl.multiple_of(jnp.bitwise_xor(rank, 2 * m) // 2 * group, group)
         path = total_ref[:, pl.ds(first, group)]
-        params = param_refs[k][middle:, :].astype(F32)
-        taps = params[0:5] + params[5:10] + params[10:15]
+        params = jnp.where(
+            parity, param_refs[2 * m][...].astype(F32), param_refs[2 * m + 1][...].astype(F32)
+        )
+        taps = params[middle : middle + 5] + params[middle + 5 : middle + 10]
+        taps += params[middle + 10 : middle + 15]
         conv = taps[CONV : CONV + 1] + jnp.zeros((rows, group), F32)
         for offset in range(CONV):
             begin = 8 - (CONV - 1) + offset
             conv += taps[offset : offset + 1] * path[begin : begin + rows]
         result = (conv / (1.0 + jnp.exp(-conv))).astype(BF16)
-        out_ref[k] = result
-        projected += dot(param_refs[k][0:middle, :], result, NT)
+        out_ref[:, pl.ds(first, group)] = result
+        projected += dot(params[0:middle].astype(BF16), result, NT)
     low_rank = projected[:DT_RANK]
     maps = projected[DT_RANK:]
     high = maps.astype(BF16)
@@ -241,22 +253,37 @@
     maps_ref[middle:, :] = (maps - high.astype(F32)).astype(BF16)
 
 
-def sum_kernel(n_pieces, rank_ref, *refs):
-    del rank_ref
-    pairs_ref = refs[n_pieces]
-    out_refs = refs[n_pieces + 1 :]
-    rows = pairs_ref.shape[1]
-    total = refs[0][...].astype(F32)
-    for piece in refs[1:n_pieces]:
+def sum_kernel(n_maps, n_gates, count, rank_ref, *refs):
+    map_refs = refs[:n_maps]
+    gate_refs = refs[n_maps : n_maps + n_gates]
+    refs = refs[n_maps + n_gates :]
+    inputs_ref, scale_ref = refs[:2]
+    out_refs = refs[2 : 2 + count // 2]
+    gate_scratch = refs[2 + count // 2]
+    rank = rank_ref[0]
+    total = map_refs[0][...].astype(F32)
+    for piece in map_refs[1:]:
         total += piece[...].astype(F32)
     middle = DT_RANK + 2 * NST
     maps = total[DT_RANK:middle] + total[middle:]
     high = maps.astype(BF16)
     low = (maps - high.astype(F32)).astype(BF16)
     low_rank = total[:DT_RANK].astype(BF16)
+    gate = gate_refs[0][...].astype(F32)
+    for piece in gate_refs[1:]:
+        gate += piece[...].astype(F32)
+    gate = gate * scale_ref[:, 0:1]
+    gate_scratch[...] = gate / (1.0 + jnp.exp(-gate))
+    rows, group = scale_ref.shape
+    lane = lax.broadcasted_iota(jnp.int32, (rows, group), 1)
     for at, out_ref in enumerate(out_refs):
-        out_ref[0:rows, :] = pairs_ref[2 * at]
-        out_ref[rows : 2 * rows, :] = pairs_ref[2 * at + 1]
+        first = pl.multiple_of(jnp.bitwise_xor(rank, 2 * at) // 2 * group, group)
+        inputs = inputs_ref[:, pl.ds(first, group)].astype(F32)
+        gate = gate_scratch[:, pl.ds(first, group)]
+        even = jnp.where(lane < group // 2, inputs, pltpu.roll(gate, group // 2, 1))
+        odd = jnp.where(lane < group // 2, pltpu.roll(inputs, group // 2, 1), gate)
+        out_ref[0:rows, :] = jnp.where(rank % 2 == 0, even, odd).astype(BF16)
+        out_ref[rows : 2 * rows, :] = jnp.where(rank % 2 == 0, odd, even).astype(BF16)
         out_ref[2 * rows : 2 * rows + DT_RANK, :] = low_rank
         out_ref[2 * rows + DT_RANK : 2 * rows + middle, :] = high
         out_ref[2 * rows + middle :, :] = low
@@ -404,21 +431,16 @@
 
     width = out_weight.shape[0]
     conv = jnp.concatenate([conv_weight, conv_bias[:, None]], axis=1).T
-    identity = jnp.zeros_like(conv).at[CONV - 1].set(1.0)
-    conv = jnp.concatenate([conv, identity], axis=1)
-    terms = []
+    terms = [proj_weight.T]
     for _ in range(3):
         high = lax.reduce_precision(conv, 8, 7)
         terms.append(high.astype(BF16))
         conv = conv - high
-    proj = jnp.concatenate([proj_weight, jnp.zeros_like(proj_weight)], axis=0).reshape(
-        2, own, -1
-    )
-    proj = jnp.transpose(proj, (2, 0, 1)).reshape(-1, 2 * own)
-    params = jnp.concatenate([proj, *terms, jnp.zeros((1, 2 * own), BF16)], axis=0)
+    params = jnp.concatenate([*terms, jnp.zeros((1, own), BF16)], axis=0)
+    params = jnp.concatenate([params, params], axis=1)
     params, _ = gather_seq([after(params, attended)] * (n_seq // 2), n_seq)
     channel_args = scan_arguments(dt_weight, dt_bias, a_log, skip_gain)
-    in_columns = jnp.transpose(in_weight, (2, 1, 3, 0)).reshape(channels, features)
+    in_columns = jnp.transpose(in_weight, (1, 2, 3, 0)).reshape(channels, features)
     far = after(far, in_columns)
 
     acc = call(
@@ -439,23 +461,22 @@
     used = n_sec - 1
     payloads = call(
         functools.partial(mix_kernel, n_seq, used),
-        [shape((HALO + rows, channels), BF16)] * n_seq,
+        [shape((HALO + rows, channels // 2), BF16)] * n_seq
+        + [shape((rows, channels // 2), BF16)] * n_seq,
         n_seq + used + 3,
         [
             pltpu.VMEM((seq_len, width * used), BF16),
             pltpu.VMEM((used * width, features), BF16),
-            pltpu.VMEM((seq_len, features), F32),
-            pltpu.VMEM((channels, features), BF16),
             pltpu.VMEM((seq_len, features), BF16),
             pltpu.VMEM((seq_len, channels), BF16),
-            pltpu.VMEM((n_seq, HALO, channels), BF16),
+            pltpu.VMEM((n_seq, HALO, channels // 2), BF16),
             pltpu.VMEM((n_seq, rows), F32),
-            pltpu.SemaphoreType.DMA((3 * n_seq + 2 * used + 3,)),
+            pltpu.SemaphoreType.DMA((4 * n_seq + used,)),
         ],
         flops=2 * seq_len * features * (width * used + channels),
         size=seq_len * features * 12,
-        limit=56,
-        in_place=[pl.ANY] * (n_seq + used + 1) + [pltpu.VMEM, pl.ANY],
+        limit=28 * scale,
+        in_place=[pl.ANY] * (n_seq + used) + [pltpu.VMEM] * 3,
         out_place=pl.ANY,
     )(
         rank_arg,
@@ -466,32 +487,35 @@
         in_columns,
     )
 
-    arrived = {k: swap(payloads[k], "seq", n_seq, 1) for k in range(n_seq - 1, 0, -2)}
-    summed = {
-        k: (payloads[k].astype(F32) + arrived[k + 1].astype(F32)).astype(BF16)
-        for k in range(0, n_seq, 2)
-    }
-    pieces = [summed[0]] + [swap(summed[k], "seq", n_seq, k) for k in range(2, n_seq, 2)]
+    path_sums = partner_sums(payloads[:n_seq], n_seq)
+    path_pieces = owner_pieces(path_sums, n_seq)
+    gates = [after(gate, *path_sums) for gate in payloads[n_seq:]]
+    gate_pieces = owner_pieces(partner_sums(gates, n_seq), n_seq)
 
     map_rows = DT_RANK + 4 * NST
-    outgoing, maps = call(
-        functools.partial(conv_kernel, len(pieces), n_seq),
-        [shape((n_seq, rows, 2 * own), BF16), shape((map_rows, rows), BF16)],
-        len(pieces) + n_seq,
-        [pltpu.VMEM((rows + 8, channels), F32)],
-        flops=2 * rows * channels * map_rows,
-        size=rows * channels * 12,
+    inputs, maps, scales = call(
+        functools.partial(conv_kernel, len(path_pieces), n_seq),
+        [
+            shape((rows, channels // 2), BF16),
+            shape((map_rows, rows), BF16),
+            shape((rows, 2 * own), F32),
+        ],
+        len(path_pieces) + n_seq,
+        [pltpu.VMEM((rows + 8, channels // 2), F32)],
+        flops=rows * channels * map_rows,
+        size=rows * channels * 6,
         limit=12 * scale,
-    )(rank_arg, *pieces, *params)
+    )(rank_arg, *path_pieces, *params)
 
     map_parts = [maps] + [swap(maps, "section", n_sec, r) for r in range(1, n_sec)]
     messages = call(
-        functools.partial(sum_kernel, n_sec),
+        functools.partial(sum_kernel, n_sec, len(gate_pieces), n_seq),
         [shape((2 * rows + map_rows, rows), BF16)] * (n_seq // 2),
-        n_sec + 1,
+        n_sec + len(gate_pieces) + 2,
+        [pltpu.VMEM((rows, channels // 2), F32)],
         size=map_rows * rows * 2 * n_sec,
         limit=8 * scale,
-    )(rank_arg, *map_parts, outgoing)
+    )(rank_arg, *map_parts, *gate_pieces, inputs, scales)
     scan_pieces, _ = gather_seq(messages, n_seq)
 
     wide = NST * own

time: 150 us -> 140 us (0.933)
  waiting for transfers between devices: 73.5 us -> 66.3 us
  starting transfers between devices: 40.1 us -> 45.5 us
  other arithmetic: 4.81 us -> 1.27 us
  local copies, waits for them, and re-layouts: 8.29 us -> 5.95 us
  Pallas kernels: 22.8 us -> 20.6 us
    ppermute x51 -> x58, waiting for transfers between devices: 73.5 us -> 66.3 us  [swap(): return lax.ppermute(x, axis, [(i, i ^ bits) for i in range(count)])]
    ppermute x51 -> x58, starting transfers between devices: 40.1 us -> 45.5 us  [swap(): return lax.ppermute(x, axis, [(i, i ^ bits) for i in range(count)])]
    convert_element_type x4 -> x8, other arithmetic: 3.17 us -> 0.28 us  [partner_sums(): (blocks[k].astype(F32) + arrived[k // 2].astype(F32)).astype(BF16)]
    pallas_call x1, Pallas kernels: 11.1 us -> 8.96 us  [body(): call(functools.partial(mix_kernel, n_seq, used), [shape((HALO + rows, cha...]
    transpose x1 -> x0, local copies, waits for them, and re-layouts: 1.59 us -> none  [body(): jnp.transpose(in_weight, (2, 1, 3, 0)).reshape(channels, features)]
    unnamed x48 -> x35, local copies, waits for them, and re-layouts: 3.96 us -> 4.95 us
  transfers between devices with their start and end apart: 51 -> 58, of which waited for: 31 -> 38; matrix products, arithmetic and copies ran while one was open for 8% -> 3% of each run, Pallas kernels for 5% -> 6%
where the time goes in v3:
time: 140 us
  waiting for transfers between devices  66.3 us (47%)
  starting transfers between devices  45.5 us (32%)
  Pallas kernels  20.6 us (15%)
  local copies, waits for them, and re-layouts  5.95 us (4%)
    ppermute x58, waiting for transfers between devices, swap(): return lax.ppermute(x, axis, [(i, i ^ bits) for i in range(count)])  66.3 us
    ppermute x58, starting transfers between devices, swap(): return lax.ppermute(x, axis, [(i, i ^ bits) for i in range(count)])  45.5 us
    pallas_call x1, Pallas kernels, body(): call(functools.partial(mix_kernel, n_seq, used), [shape((HALO + rows, cha...  8.96 us
    pallas_call x1, Pallas kernels, body(): call(functools.partial(own_kernel, n_seq), shape((seq_len, features), F32...  5.78 us
    unnamed x35, local copies, waits for them, and re-layouts  4.95 us
    pallas_call x1, Pallas kernels, body(): call(functools.partial(scan_kernel, n_seq), shape((own, seq_len), BF16),...  3.61 us
  transfers between devices with their start and end apart: 58, of which 38 were waited for; matrix products, arithmetic and copies ran while one was open for 3% of the time, Pallas kernels for 6%

profile of v3, /device:TPU:0, one launch (start us, length us, event | category | flops | bytes accessed | tf_op | source)
XLA Modules:
  0.0 139.9 jit_solution(5629013971989424821)
XLA Ops:
  0.0 5.1 %collective-permute-start.32 = (bf16[512,1024]{1,0:T(8,128)(2,1)}, bf16[512,1024]{1,0:T(8,128)(2,1)S(1)}, u32[]{:S(2)}, u32[]{:S(2)}) collective-permute-start(bf16[512,1024]{1,0:T(8,128)(2,1)} %refs_8_.1), channel_id=1, source_target_pairs={{0,3},{1,2},{2,1},{3,0},{4,7},{5,6},{6,5},{7,4},{8,11},{9,10},{10,... | collective-permute-start | bytes 3145736 | tf_op jit(solution)/shard_map/ppermute | solution.py:49
  6.7 2.5 %collective-permute-start.2 = (bf16[128,256]{1,0:T(8,128)(2,1)S(1)}, bf16[128,256]{1,0:T(8,128)(2,1)S(1)}, u32[]{:S(2)}, u32[]{:S(2)}) collective-permute-start(bf16[128,256]{1,0:T(8,128)(2,1)S(1)} %constant_dynamic-update-slice_fusion.refs_0_), channel_id=1, source_target_pairs={{0,24},{4,28},{8,16},{12,20},{16,8},{20,12},{24,0},{28,4},{1,25},{... | collective-permute-start | bytes 196616 | tf_op jit(solution)/shard_map/ppermute | solution.py:49
  10.2 1.8 %collective-permute-done.2.refs_6_ = bf16[128,256]{1,0:T(8,128)(2,1)S(1)} collective-permute-done((bf16[128,256]{1,0:T(8,128)(2,1)S(1)}, bf16[128,256]{1,0:T(8,128)(2,1)S(1)}, u32[]{:S(2)}, u32[]{:S(2)}) %collective-permute-start.2) | collective-permute-done | bytes 65568 | tf_op jit(solution)/shard_map/ppermute | solution.py:49
  18.1 1.6 %collective-permute-start.15 = (bf16[128,512]{1,0:T(8,128)(2,1)S(1)}, bf16[128,512]{1,0:T(8,128)(2,1)S(1)}, u32[]{:S(2)}, u32[]{:S(2)}) collective-permute-start(bf16[128,512]{1,0:T(8,128)(2,1)S(1)} %shard_map.136.refs_0_), channel_id=1, source_target_pairs={{0,24},{4,28},{8,16},{12,20},{16,8},{20,12},{24,0},{28,4},{1,25},{... | collective-permute-start | bytes 393224 | tf_op jit(solution)/shard_map/ppermute | solution.py:49
  23.5 1.9 %collective-permute-done.15.refs_6_ = bf16[128,512]{1,0:T(8,128)(2,1)S(1)} collective-permute-done((bf16[128,512]{1,0:T(8,128)(2,1)S(1)}, bf16[128,512]{1,0:T(8,128)(2,1)S(1)}, u32[]{:S(2)}, u32[]{:S(2)}) %collective-permute-start.15) | collective-permute-done | bytes 131104 | tf_op jit(solution)/shard_map/ppermute | solution.py:49
  25.4 2.2 %collective-permute-done.14.refs_4_ = bf16[128,512]{1,0:T(8,128)(2,1)S(1)} collective-permute-done((bf16[128,512]{1,0:T(8,128)(2,1)S(1)}, bf16[128,512]{1,0:T(8,128)(2,1)S(1)}, u32[]{:S(2)}, u32[]{:S(2)}) %collective-permute-start.14) | collective-permute-done | bytes 131104 | tf_op jit(solution)/shard_map/ppermute | solution.py:49
  31.4 2.2 %collective-permute-done.23.refs_10_ = bf16[288,128]{1,0:T(8,128)(2,1)S(1)} collective-permute-done((bf16[288,128]{1,0:T(8,128)(2,1)S(1)}, bf16[288,128]{1,0:T(8,128)(2,1)S(1)}, u32[]{:S(2)}, u32[]{:S(2)}) %collective-permute-start.23) | collective-permute-done | bytes 73760 | tf_op jit(solution)/shard_map/ppermute | solution.py:49
  35.3 1.8 %collective-permute-start.8 = (bf16[128,512]{1,0:T(8,128)(2,1)S(1)}, bf16[128,512]{1,0:T(8,128)(2,1)S(1)}, u32[]{:S(2)}, u32[]{:S(2)}) collective-permute-start(bf16[128,512]{1,0:T(8,128)(2,1)S(1)} %shard_map.136.refs_0_), channel_id=1, source_target_pairs={{0,2},{1,3},{2,0},{3,1},{4,6},{5,7},{6,4},{7,5},{8,10},{9,11},{10,... | collective-permute-start | bytes 393224 | tf_op jit(solution)/shard_map/ppermute | solution.py:49
  37.1 24.5 %collective-permute-done.9 = bf16[128,512]{1,0:T(8,128)(2,1)S(1)} collective-permute-done((bf16[128,512]{1,0:T(8,128)(2,1)S(1)}, bf16[128,512]{1,0:T(8,128)(2,1)S(1)}, u32[]{:S(2)}, u32[]{:S(2)}) %collective-permute-start.9) | collective-permute-done | bytes 131104 | tf_op jit(solution)/shard_map/ppermute | solution.py:49
  63.7 1.7 %collective-permute-start.33 = (bf16[512,1024]{1,0:T(8,128)(2,1)S(1)}, bf16[512,1024]{1,0:T(8,128)(2,1)}, u32[]{:S(2)}, u32[]{:S(2)}) collective-permute-start(bf16[512,1024]{1,0:T(8,128)(2,1)S(1)} %collective-permute-done.32.refs_10_), channel_id=1, source_target_pairs={{0,1},{1,0},{2,3},{3,2},{4,5},{5,4},{6,7},{7,6},{8,9},{9,8},{10,11... | collective-permute-start | bytes 3145736 | tf_op jit(solution)/shard_map/ppermute | solution.py:49
  69.4 5.8 %shard_map.137.refs_11_ = f32[1024,1024]{1,0:T(8,128)} custom-call(s32[1]{0:T(128)} %bitcast.rank_ref, bf16[128,512]{1,0:T(8,128)(2,1)} %copy-done.1, bf16[128,512]{1,0:T(8,128)(2,1)} %copy-done.8, bf16[128,512]{1,0:T(8,128)(2,1)} %copy-done.7, bf16[128,512]{1,0:T(8,128)(2,1)} %copy-done.9, bf16[128,512]{1,0:T(8,128)(2,1)} %copy-done.6, ...), custom_call_target="tpu_custom_call" | custom-call | flops 1073741824 | bytes 8388608 | tf_op jit(solution)/shard_map/pallas_call | solution.py:446
  75.2 3.3 %collective-permute-done.12.refs_6_ = bf16[128,1536]{1,0:T(8,128)(2,1)} collective-permute-done((bf16[128,1536]{1,0:T(8,128)(2,1)S(1)}, bf16[128,1536]{1,0:T(8,128)(2,1)}, u32[]{:S(2)}, u32[]{:S(2)}) %collective-permute-start.12) | collective-permute-done | bytes 393248 | tf_op jit(solution)/shard_map/ppermute | solution.py:49
  78.5 7.3 %collective-permute-done.11.refs_4_ = bf16[128,1536]{1,0:T(8,128)(2,1)} collective-permute-done((bf16[128,1536]{1,0:T(8,128)(2,1)S(1)}, bf16[128,1536]{1,0:T(8,128)(2,1)}, u32[]{:S(2)}, u32[]{:S(2)}) %collective-permute-start.11) | collective-permute-done | bytes 393248 | tf_op jit(solution)/shard_map/ppermute | solution.py:49
  89.4 2.2 %copy-done = f32[1024,1024]{1,0:T(8,128)S(1)} copy-done((f32[1024,1024]{1,0:T(8,128)S(1)}, f32[1024,1024]{1,0:T(8,128)}, u32[]{:S(2)}) %copy-start) | copy-done | bytes 4194328
  91.6 9.0 %shard_map.138 = (bf16[144,512]{1,0:T(8,128)(2,1)S(1)}, bf16[144,512]{1,0:T(8,128)(2,1)S(1)}, bf16[144,512]{1,0:T(8,128)(2,1)S(1)}, bf16[144,512]{1,0:T(8,128)(2...) custom-call(s32[1]{0:T(128)} %bitcast.rank_ref, ...), custom_call_target="tpu_custom_call" | custom-call | flops 5368709120 | bytes 12582912 | tf_op jit(solution)/shard_map/pallas_call | solution.py:462
  110.4 3.2 %collective-permute-start.48 = (bf16[128,512]{1,0:T(8,128)(2,1)S(1)}, bf16[128,512]{1,0:T(8,128)(2,1)S(1)}, u32[]{:S(2)}, u32[]{:S(2)}) collective-permute-start(bf16[128,512]{1,0:T(8,128)(2,1)S(1)} %add_convert_fusion.5), channel_id=1, source_target_pairs={{0,16},{4,20},{8,24},{12,28},{16,0},{20,4},{24,8},{28,12},{1,17},{... | collective-permute-start | bytes 393224 | tf_op jit(solution)/shard_map/ppermute | solution.py:49
  114.3 3.3 %collective-permute-start.43 = (bf16[288,128]{1,0:T(8,128)(2,1)S(1)}, bf16[288,128]{1,0:T(8,128)(2,1)S(1)}, u32[]{:S(2)}, u32[]{:S(2)}) collective-permute-start(bf16[288,128]{1,0:T(8,128)(2,1)S(1)} %get-tuple-element.112.refs_0_), channel_id=1, source_target_pairs={{0,3},{1,2},{2,1},{3,0},{4,7},{5,6},{6,5},{7,4},{8,11},{9,10},{10,... | collective-permute-start | bytes 221192 | tf_op jit(solution)/shard_map/ppermute | solution.py:49
  117.6 1.7 %collective-permute-start.50 = (bf16[128,512]{1,0:T(8,128)(2,1)S(1)}, bf16[128,512]{1,0:T(8,128)(2,1)S(1)}, u32[]{:S(2)}, u32[]{:S(2)}) collective-permute-start(bf16[128,512]{1,0:T(8,128)(2,1)S(1)} %add_convert_fusion.4), channel_id=1, source_target_pairs={{0,24},{4,28},{8,16},{12,20},{16,8},{20,12},{24,0},{28,4},{1,25},{... | collective-permute-start | bytes 393224 | tf_op jit(solution)/shard_map/ppermute | solution.py:49
  119.3 1.8 %collective-permute-done.43.refs_3_ = bf16[288,128]{1,0:T(8,128)(2,1)S(1)} collective-permute-done((bf16[288,128]{1,0:T(8,128)(2,1)S(1)}, bf16[288,128]{1,0:T(8,128)(2,1)S(1)}, u32[]{:S(2)}, u32[]{:S(2)}) %collective-permute-start.43) | collective-permute-done | bytes 73760 | tf_op jit(solution)/shard_map/ppermute | solution.py:49
  121.2 4.2 %collective-permute-done.42.refs_2_ = bf16[288,128]{1,0:T(8,128)(2,1)S(1)} collective-permute-done((bf16[288,128]{1,0:T(8,128)(2,1)S(1)}, bf16[288,128]{1,0:T(8,128)(2,1)S(1)}, u32[]{:S(2)}, u32[]{:S(2)}) %collective-permute-start.42) | collective-permute-done | bytes 73760 | tf_op jit(solution)/shard_map/ppermute | solution.py:49
  128.3 1.6 %collective-permute-start.53 = (bf16[544,128]{1,0:T(8,128)(2,1)S(1)}, bf16[544,128]{1,0:T(8,128)(2,1)S(1)}, u32[]{:S(2)}, u32[]{:S(2)}) collective-permute-start(bf16[544,128]{1,0:T(8,128)(2,1)S(1)} %get-tuple-element.134), channel_id=1, source_target_pairs={{0,24},{4,28},{8,16},{12,20},{16,8},{20,12},{24,0},{28,4},{1,25},{... | collective-permute-start | bytes 417800 | tf_op jit(solution)/shard_map/ppermute | solution.py:49
  129.9 1.6 %collective-permute-done.51.refs_2_ = bf16[544,128]{1,0:T(8,128)(2,1)S(1)} collective-permute-done((bf16[544,128]{1,0:T(8,128)(2,1)S(1)}, bf16[544,128]{1,0:T(8,128)(2,1)S(1)}, u32[]{:S(2)}, u32[]{:S(2)}) %collective-permute-start.51) | collective-permute-done | bytes 139296 | tf_op jit(solution)/shard_map/ppermute | solution.py:49
  132.2 2.1 %collective-permute-done.53.refs_6_ = bf16[544,128]{1,0:T(8,128)(2,1)S(1)} collective-permute-done((bf16[544,128]{1,0:T(8,128)(2,1)S(1)}, bf16[544,128]{1,0:T(8,128)(2,1)S(1)}, u32[]{:S(2)}, u32[]{:S(2)}) %collective-permute-start.53) | collective-permute-done | bytes 139296 | tf_op jit(solution)/shard_map/ppermute | solution.py:49
  136.3 3.6 %shard_map.141 = bf16[64,1024]{1,0:T(8,128)(2,1)} custom-call(s32[1]{0:T(128)} %bitcast.rank_ref, bf16[544,128]{1,0:T(8,128)(2,1)S(1)} %get-tuple-element.135.refs_0_, bf16[544,128]{1,0:T(8,128)(2,1)S(1)} %collective-permute-done.54.refs_1_, bf16[544,128]{1,0:T(8,128)(2,1)S(1)} %collective-permute-done.51.refs_2_, ...), custom_call_target="tpu_custom_call" | custom-call | flops 33554432 | bytes 4194304 | tf_op jit(solution)/shard_map/pallas_call | solution.py:522
  (151 shorter events, 43.8 us)
Async XLA Ops:
  0.0 63.3 %collective-permute-start.32 = (bf16[512,1024]{1,0:T(8,128)(2,1)}, bf16[512,1024]{1,0:T(8,128)(2,1)S(1)}, u32[]{:S(2)}, u32[]{:S(2)}) collective-permute-start(bf16[512,1024]{1,0:T(8,128)(2,1)} %refs_8_.1), channel_id=1, source_target_pairs={{0,3},{1,2},{2,1},{3,0},{4,7},{5,6},{6,5},{7,4},{8,11},{9,10},{10,... | collective-permute-start | bytes 3145736 | tf_op jit(solution)/shard_map/ppermute | solution.py:49
  18.1 7.3 %collective-permute-start.15 = (bf16[128,512]{1,0:T(8,128)(2,1)S(1)}, bf16[128,512]{1,0:T(8,128)(2,1)S(1)}, u32[]{:S(2)}, u32[]{:S(2)}) collective-permute-start(bf16[128,512]{1,0:T(8,128)(2,1)S(1)} %shard_map.136.refs_0_), channel_id=1, source_target_pairs={{0,24},{4,28},{8,16},{12,20},{16,8},{20,12},{24,0},{28,4},{1,25},{... | collective-permute-start | bytes 393224 | tf_op jit(solution)/shard_map/ppermute | solution.py:49
  19.7 8.0 %collective-permute-start.14 = (bf16[128,512]{1,0:T(8,128)(2,1)S(1)}, bf16[128,512]{1,0:T(8,128)(2,1)S(1)}, u32[]{:S(2)}, u32[]{:S(2)}) collective-permute-start(bf16[128,512]{1,0:T(8,128)(2,1)S(1)} %shard_map.136.refs_0_), channel_id=1, source_target_pairs={{0,16},{4,20},{8,24},{12,28},{16,0},{20,4},{24,8},{28,12},{1,17},{... | collective-permute-start | bytes 393224 | tf_op jit(solution)/shard_map/ppermute | solution.py:49
  20.2 7.6 %collective-permute-start.13 = (bf16[128,512]{1,0:T(8,128)(2,1)S(1)}, bf16[128,512]{1,0:T(8,128)(2,1)S(1)}, u32[]{:S(2)}, u32[]{:S(2)}) collective-permute-start(bf16[128,512]{1,0:T(8,128)(2,1)S(1)} %shard_map.136.refs_0_), channel_id=1, source_target_pairs={{0,8},{4,12},{8,0},{12,4},{16,24},{20,28},{24,16},{28,20},{1,9},{5... | collective-permute-start | bytes 393224 | tf_op jit(solution)/shard_map/ppermute | solution.py:49
  23.5 13.6 %collective-permute-start.7 = (bf16[128,512]{1,0:T(8,128)(2,1)S(1)}, bf16[128,512]{1,0:T(8,128)(2,1)S(1)}, u32[]{:S(2)}, u32[]{:S(2)}) collective-permute-start(bf16[128,512]{1,0:T(8,128)(2,1)S(1)} %shard_map.136.refs_0_), channel_id=1, source_target_pairs={{0,1},{1,0},{2,3},{3,2},{4,5},{5,4},{6,7},{7,6},{8,9},{9,8},{10,11... | collective-permute-start | bytes 393224 | tf_op jit(solution)/shard_map/ppermute | solution.py:49
  33.6 52.2 %collective-permute-start.20 = (bf16[512,1024]{1,0:T(8,128)(2,1)}, bf16[512,1024]{1,0:T(8,128)(2,1)S(1)}, u32[]{:S(2)}, u32[]{:S(2)}) collective-permute-start(bf16[512,1024]{1,0:T(8,128)(2,1)} %refs_8_.1), channel_id=1, source_target_pairs={{0,1},{1,0},{2,3},{3,2},{4,5},{5,4},{6,7},{7,6},{8,9},{9,8},{10,11... | collective-permute-start | bytes 3145736 | tf_op jit(solution)/shard_map/ppermute | solution.py:49
  35.1 26.5 %collective-permute-start.9 = (bf16[128,512]{1,0:T(8,128)(2,1)S(1)}, bf16[128,512]{1,0:T(8,128)(2,1)S(1)}, u32[]{:S(2)}, u32[]{:S(2)}) collective-permute-start(bf16[128,512]{1,0:T(8,128)(2,1)S(1)} %shard_map.136.refs_0_), channel_id=1, source_target_pairs={{0,3},{1,2},{2,1},{3,0},{4,7},{5,6},{6,5},{7,4},{8,11},{9,10},{10,... | collective-permute-start | bytes 393224 | tf_op jit(solution)/shard_map/ppermute | solution.py:49
  35.3 26.6 %collective-permute-start.8 = (bf16[128,512]{1,0:T(8,128)(2,1)S(1)}, bf16[128,512]{1,0:T(8,128)(2,1)S(1)}, u32[]{:S(2)}, u32[]{:S(2)}) collective-permute-start(bf16[128,512]{1,0:T(8,128)(2,1)S(1)} %shard_map.136.refs_0_), channel_id=1, source_target_pairs={{0,2},{1,3},{2,0},{3,1},{4,6},{5,7},{6,4},{7,5},{8,10},{9,11},{10,... | collective-permute-start | bytes 393224 | tf_op jit(solution)/shard_map/ppermute | solution.py:49
  37.1 25.0 %collective-permute-start.24 = (bf16[288,128]{1,0:T(8,128)(2,1)S(1)}, bf16[288,128]{1,0:T(8,128)(2,1)S(1)}, u32[]{:S(2)}, u32[]{:S(2)}) collective-permute-start(bf16[288,128]{1,0:T(8,128)(2,1)S(1)} %pad_maximum_fusion.refs_4_), channel_id=1, source_target_pairs={{0,4},{4,0},{8,12},{12,8},{16,20},{20,16},{24,28},{28,24},{1,5},{5... | collective-permute-start | bytes 221192 | tf_op jit(solution)/shard_map/ppermute | solution.py:49
  63.7 25.7 %collective-permute-start.33 = (bf16[512,1024]{1,0:T(8,128)(2,1)S(1)}, bf16[512,1024]{1,0:T(8,128)(2,1)}, u32[]{:S(2)}, u32[]{:S(2)}) collective-permute-start(bf16[512,1024]{1,0:T(8,128)(2,1)S(1)} %collective-permute-done.32.refs_10_), channel_id=1, source_target_pairs={{0,1},{1,0},{2,3},{3,2},{4,5},{5,4},{6,7},{7,6},{8,9},{9,8},{10,11... | collective-permute-start | bytes 3145736 | tf_op jit(solution)/shard_map/ppermute | solution.py:49
  65.4 13.0 %collective-permute-start.12 = (bf16[128,1536]{1,0:T(8,128)(2,1)S(1)}, bf16[128,1536]{1,0:T(8,128)(2,1)}, u32[]{:S(2)}, u32[]{:S(2)}) collective-permute-start(bf16[128,1536]{1,0:T(8,128)(2,1)S(1)} %constant_dynamic-update-slice_fusion.2.refs_0_), channel_id=1, source_target_pairs={{0,24},{4,28},{8,16},{12,20},{16,8},{20,12},{24,0},{28,4},{1,25},{... | collective-permute-start | bytes 1179656 | tf_op jit(solution)/shard_map/ppermute | solution.py:49
  66.9 18.9 %collective-permute-start.11 = (bf16[128,1536]{1,0:T(8,128)(2,1)S(1)}, bf16[128,1536]{1,0:T(8,128)(2,1)}, u32[]{:S(2)}, u32[]{:S(2)}) collective-permute-start(bf16[128,1536]{1,0:T(8,128)(2,1)S(1)} %constant_dynamic-update-slice_fusion.2.refs_0_), channel_id=1, source_target_pairs={{0,16},{4,20},{8,24},{12,28},{16,0},{20,4},{24,8},{28,12},{1,17},{... | collective-permute-start | bytes 1179656 | tf_op jit(solution)/shard_map/ppermute | solution.py:49
  67.4 18.3 %collective-permute-start.10 = (bf16[128,1536]{1,0:T(8,128)(2,1)S(1)}, bf16[128,1536]{1,0:T(8,128)(2,1)}, u32[]{:S(2)}, u32[]{:S(2)}) collective-permute-start(bf16[128,1536]{1,0:T(8,128)(2,1)S(1)} %constant_dynamic-update-slice_fusion.2.refs_0_), channel_id=1, source_target_pairs={{0,8},{4,12},{8,0},{12,4},{16,24},{20,28},{24,16},{28,20},{1,9},{5... | collective-permute-start | bytes 1179656 | tf_op jit(solution)/shard_map/ppermute | solution.py:49
  103.1 6.7 %collective-permute-start.36 = (bf16[144,512]{1,0:T(8,128)(2,1)S(1)}, bf16[144,512]{1,0:T(8,128)(2,1)S(1)}, u32[]{:S(2)}, u32[]{:S(2)}) collective-permute-start(bf16[144,512]{1,0:T(8,128)(2,1)S(1)} %add_convert_fusion.2), channel_id=1, source_target_pairs={{0,8},{4,12},{8,0},{12,4},{16,24},{20,28},{24,16},{28,20},{1,9},{5... | collective-permute-start | bytes 442376 | tf_op jit(solution)/shard_map/ppermute | solution.py:49
  103.7 6.7 %collective-permute-start.38 = (bf16[144,512]{1,0:T(8,128)(2,1)S(1)}, bf16[144,512]{1,0:T(8,128)(2,1)S(1)}, u32[]{:S(2)}, u32[]{:S(2)}) collective-permute-start(bf16[144,512]{1,0:T(8,128)(2,1)S(1)} %add_convert_fusion.1), channel_id=1, source_target_pairs={{0,16},{4,20},{8,24},{12,28},{16,0},{20,4},{24,8},{28,12},{1,17},{... | collective-permute-start | bytes 442376 | tf_op jit(solution)/shard_map/ppermute | solution.py:49
  105.1 8.5 %collective-permute-start.40 = (bf16[144,512]{1,0:T(8,128)(2,1)S(1)}, bf16[144,512]{1,0:T(8,128)(2,1)S(1)}, u32[]{:S(2)}, u32[]{:S(2)}) collective-permute-start(bf16[144,512]{1,0:T(8,128)(2,1)S(1)} %add_convert_fusion), channel_id=1, source_target_pairs={{0,24},{4,28},{8,16},{12,20},{16,8},{20,12},{24,0},{28,4},{1,25},{... | collective-permute-start | bytes 442376 | tf_op jit(solution)/shard_map/ppermute | solution.py:49
  106.6 12.7 %collective-permute-start.44 = (bf16[128,512]{1,0:T(8,128)(2,1)S(1)}, bf16[128,512]{1,0:T(8,128)(2,1)S(1)}, u32[]{:S(2)}, u32[]{:S(2)}) collective-permute-start(bf16[128,512]{1,0:T(8,128)(2,1)S(1)} %get-tuple-element.116), channel_id=1, source_target_pairs={{0,4},{4,0},{8,12},{12,8},{16,20},{20,16},{24,28},{28,24},{1,5},{5... | collective-permute-start | bytes 393224 | tf_op jit(solution)/shard_map/ppermute | solution.py:49
  108.1 9.4 %collective-permute-start.49 = (bf16[128,512]{1,0:T(8,128)(2,1)S(1)}, bf16[128,512]{1,0:T(8,128)(2,1)S(1)}, u32[]{:S(2)}, u32[]{:S(2)}) collective-permute-start(bf16[128,512]{1,0:T(8,128)(2,1)S(1)} %get-tuple-element.128), channel_id=1, source_target_pairs={{0,4},{4,0},{8,12},{12,8},{16,20},{20,16},{24,28},{28,24},{1,5},{5... | collective-permute-start | bytes 393224 | tf_op jit(solution)/shard_map/ppermute | solution.py:49
  109.8 16.3 %collective-permute-start.46 = (bf16[128,512]{1,0:T(8,128)(2,1)S(1)}, bf16[128,512]{1,0:T(8,128)(2,1)S(1)}, u32[]{:S(2)}, u32[]{:S(2)}) collective-permute-start(bf16[128,512]{1,0:T(8,128)(2,1)S(1)} %add_convert_fusion.6), channel_id=1, source_target_pairs={{0,8},{4,12},{8,0},{12,4},{16,24},{20,28},{24,16},{28,20},{1,9},{5... | collective-permute-start | bytes 393224 | tf_op jit(solution)/shard_map/ppermute | solution.py:49
  110.4 15.7 %collective-permute-start.48 = (bf16[128,512]{1,0:T(8,128)(2,1)S(1)}, bf16[128,512]{1,0:T(8,128)(2,1)S(1)}, u32[]{:S(2)}, u32[]{:S(2)}) collective-permute-start(bf16[128,512]{1,0:T(8,128)(2,1)S(1)} %add_convert_fusion.5), channel_id=1, source_target_pairs={{0,16},{4,20},{8,24},{12,28},{16,0},{20,4},{24,8},{28,12},{1,17},{... | collective-permute-start | bytes 393224 | tf_op jit(solution)/shard_map/ppermute | solution.py:49
  114.3 6.8 %collective-permute-start.43 = (bf16[288,128]{1,0:T(8,128)(2,1)S(1)}, bf16[288,128]{1,0:T(8,128)(2,1)S(1)}, u32[]{:S(2)}, u32[]{:S(2)}) collective-permute-start(bf16[288,128]{1,0:T(8,128)(2,1)S(1)} %get-tuple-element.112.refs_0_), channel_id=1, source_target_pairs={{0,3},{1,2},{2,1},{3,0},{4,7},{5,6},{6,5},{7,4},{8,11},{9,10},{10,... | collective-permute-start | bytes 221192 | tf_op jit(solution)/shard_map/ppermute | solution.py:49
  117.6 8.5 %collective-permute-start.50 = (bf16[128,512]{1,0:T(8,128)(2,1)S(1)}, bf16[128,512]{1,0:T(8,128)(2,1)S(1)}, u32[]{:S(2)}, u32[]{:S(2)}) collective-permute-start(bf16[128,512]{1,0:T(8,128)(2,1)S(1)} %add_convert_fusion.4), channel_id=1, source_target_pairs={{0,24},{4,28},{8,16},{12,20},{16,8},{20,12},{24,0},{28,4},{1,25},{... | collective-permute-start | bytes 393224 | tf_op jit(solution)/shard_map/ppermute | solution.py:49
  119.3 6.0 %collective-permute-start.42 = (bf16[288,128]{1,0:T(8,128)(2,1)S(1)}, bf16[288,128]{1,0:T(8,128)(2,1)S(1)}, u32[]{:S(2)}, u32[]{:S(2)}) collective-permute-start(bf16[288,128]{1,0:T(8,128)(2,1)S(1)} %get-tuple-element.112.refs_0_), channel_id=1, source_target_pairs={{0,2},{1,3},{2,0},{3,1},{4,6},{5,7},{6,4},{7,5},{8,10},{9,11},{10,... | collective-permute-start | bytes 221192 | tf_op jit(solution)/shard_map/ppermute | solution.py:49
  128.3 6.0 %collective-permute-start.53 = (bf16[544,128]{1,0:T(8,128)(2,1)S(1)}, bf16[544,128]{1,0:T(8,128)(2,1)S(1)}, u32[]{:S(2)}, u32[]{:S(2)}) collective-permute-start(bf16[544,128]{1,0:T(8,128)(2,1)S(1)} %get-tuple-element.134), channel_id=1, source_target_pairs={{0,24},{4,28},{8,16},{12,20},{16,8},{20,12},{24,0},{28,4},{1,25},{... | collective-permute-start | bytes 417800 | tf_op jit(solution)/shard_map/ppermute | solution.py:49
  (49 other events, 566.8 us)

commit v4 on v3

--- a/solution.py
+++ b/solution.py
@@ -129,9 +129,10 @@
         for half in range(2):
             k = 2 * t + half
             first = pl.multiple_of(jnp.bitwise_xor(rank, k) * rows, rows)
-            acc_ref[k * rows : (k + 1) * rows, :] = total[
-                half * rows : (half + 1) * rows
-            ] + residual_ref[pl.ds(first, rows), :].astype(F32)
+            rest = residual_ref[pl.ds(first, rows), :].astype(F32)
+            acc_ref[k * rows : (k + 1) * rows, :] = (
+                total[half * rows : (half + 1) * rows] + rest
+            ).astype(BF16)
 
 
 def mix_kernel(count, used, rank_ref, *refs):
@@ -146,10 +147,9 @@
     width = weight_refs[0].shape[0]
     channels = in_ref.shape[0] // 2
     copies = Copies(semaphores)
-    weight_copies = [
-        copies.start(weight_refs[r], weights.at[pl.ds(r * width, width), :]) for r in range(used)
-    ]
     tile = rows * count // 2
+    spans = [pl.ds(r * width, width) for r in range(used)]
+    weight_copies = [copies.start(weight_refs[0], weights.at[spans[0], :])]
     left_copies, out_copies = [], []
     for t in range(2):
         left_copies.append(
@@ -161,8 +161,9 @@
                 for k in range(t * count // 2, (t + 1) * count // 2)
             ]
         )
-    for copy in weight_copies:
-        copy.wait()
+        if t == 0:
+            for r in range(1, used):
+                weight_copies.append(copies.start(weight_refs[r], weights.at[spans[r], :]))
     eye = lax.broadcasted_iota(jnp.int32, (rows, rows), 0) == lax.broadcasted_iota(
         jnp.int32, (rows, rows), 1
     )
@@ -170,8 +171,11 @@
         span = pl.ds(t * tile, tile)
         for copy in left_copies[t]:
             copy.wait()
-        total = dot(left[span, :], weights[...])
-        hidden = acc_ref[span, :] + total
+        hidden = acc_ref[span, :].astype(F32)
+        for r in range(used):
+            if t == 0:
+                weight_copies[r].wait()
+            hidden += dot(left[span, spans[r]], weights[spans[r], :])
         normed[span, :] = (hidden * gain_ref[...]).astype(BF16)
         sums = jnp.sum(hidden * hidden, axis=1, keepdims=True)
         for part in range(count // 2):
@@ -409,6 +413,7 @@
     others_at = list(range(1, n_sec))
     far_at = list(range(3, n_sec, 2))
     weights = {r: swap(out_weight, "section", n_sec, r) for r in far_at}
+    nearest = swap(out_weight, "section", n_sec, 1)
 
     pairs, _ = gather_seq([jnp.concatenate([keys, values], axis=1)] * (n_seq // 2), n_seq)
     attended = call(
@@ -425,7 +430,7 @@
         [swap(attended, "section", n_sec, r) for r in others_at], axis=1
     )
     own_pieces, _ = gather_seq([attended] * (n_seq // 2), n_seq)
-    nearest = swap(after(out_weight, own_pieces[-1]), "section", n_sec, 1)
+    far = after(far, nearest)
     for r in range(2, n_sec, 2):
         weights[r] = swap(after(weights[r + 1], far), "section", n_sec, 1)
 
@@ -445,7 +450,7 @@
 
     acc = call(
         functools.partial(own_kernel, n_seq),
-        shape((seq_len, features), F32),
+        shape((seq_len, features), BF16),
         n_seq + 2,
         [pltpu.VMEM((seq_len, width), BF16)],
         flops=2 * seq_len * features * width,

time: 140 us -> 139 us (level)
  waiting for transfers between devices: 66.3 us -> 63.2 us
    ppermute x58, waiting for transfers between devices: 66.3 us -> 63.2 us  [swap(): return lax.ppermute(x, axis, [(i, i ^ bits) for i in range(count)])]
    unnamed x35 -> x29, local copies, waits for them, and re-layouts: 4.95 us -> 6.22 us
  transfers between devices with their start and end apart: 58 -> 58, of which waited for: 38 -> 35; matrix products, arithmetic and copies ran while one was open for 3% -> 5% of each run, Pallas kernels for 6% -> 5%
where the time goes in v4:
time: 139 us
  waiting for transfers between devices  63.2 us (45%)
  starting transfers between devices  46 us (33%)
  Pallas kernels  19.9 us (14%)
  local copies, waits for them, and re-layouts  7.21 us (5%)
  other arithmetic  2.21 us (2%)
    ppermute x58, waiting for transfers between devices, swap(): return lax.ppermute(x, axis, [(i, i ^ bits) for i in range(count)])  63.2 us
    ppermute x58, starting transfers between devices, swap(): return lax.ppermute(x, axis, [(i, i ^ bits) for i in range(count)])  46 us
    pallas_call x1, Pallas kernels, body(): call(functools.partial(mix_kernel, n_seq, used), [shape((HALO + rows, cha...  9.02 us
    unnamed x29, local copies, waits for them, and re-layouts  6.22 us
    pallas_call x1, Pallas kernels, body(): call(functools.partial(own_kernel, n_seq), shape((seq_len, features), BF1...  5.02 us
    pallas_call x1, Pallas kernels, body(): call(functools.partial(scan_kernel, n_seq), shape((own, seq_len), BF16),...  3.6 us
  transfers between devices with their start and end apart: 58, of which 35 were waited for; matrix products, arithmetic and copies ran while one was open for 5% of the time, Pallas kernels for 5%

profile of v4, /device:TPU:0, one launch (start us, length us, event | category | flops | bytes accessed | tf_op | source)
XLA Modules:
  0.0 138.8 jit_solution(11280356951954880433)
XLA Ops:
  0.0 3.1 %collective-permute-start.10 = (bf16[512,1024]{1,0:T(8,128)(2,1)}, bf16[512,1024]{1,0:T(8,128)(2,1)S(1)}, u32[]{:S(2)}, u32[]{:S(2)}) collective-permute-start(bf16[512,1024]{1,0:T(8,128)(2,1)} %refs_8_.1), channel_id=1, source_target_pairs={{0,1},{1,0},{2,3},{3,2},{4,5},{5,4},{6,7},{7,6},{8,9},{9,8},{10,11... | collective-permute-start | bytes 3145736 | tf_op jit(solution)/shard_map/ppermute | solution.py:49
  3.1 2.5 %collective-permute-start.32 = (bf16[512,1024]{1,0:T(8,128)(2,1)}, bf16[512,1024]{1,0:T(8,128)(2,1)S(1)}, u32[]{:S(2)}, u32[]{:S(2)}) collective-permute-start(bf16[512,1024]{1,0:T(8,128)(2,1)} %refs_8_.1), channel_id=1, source_target_pairs={{0,3},{1,2},{2,1},{3,0},{4,7},{5,6},{6,5},{7,4},{8,11},{9,10},{10,... | collective-permute-start | bytes 3145736 | tf_op jit(solution)/shard_map/ppermute | solution.py:49
  7.1 2.5 %collective-permute-start.2 = (bf16[128,256]{1,0:T(8,128)(2,1)S(1)}, bf16[128,256]{1,0:T(8,128)(2,1)S(1)}, u32[]{:S(2)}, u32[]{:S(2)}) collective-permute-start(bf16[128,256]{1,0:T(8,128)(2,1)S(1)} %constant_dynamic-update-slice_fusion.refs_0_), channel_id=1, source_target_pairs={{0,24},{4,28},{8,16},{12,20},{16,8},{20,12},{24,0},{28,4},{1,25},{... | collective-permute-start | bytes 196616 | tf_op jit(solution)/shard_map/ppermute | solution.py:49
  19.5 1.6 %collective-permute-start.23 = (bf16[288,128]{1,0:T(8,128)(2,1)S(1)}, bf16[288,128]{1,0:T(8,128)(2,1)S(1)}, u32[]{:S(2)}, u32[]{:S(2)}) collective-permute-start(bf16[288,128]{1,0:T(8,128)(2,1)S(1)} %pad_maximum_fusion.1.refs_4_), channel_id=1, source_target_pairs={{0,24},{4,28},{8,16},{12,20},{16,8},{20,12},{24,0},{28,4},{1,25},{... | collective-permute-start | bytes 221192 | tf_op jit(solution)/shard_map/ppermute | solution.py:49
  23.0 2.0 %collective-permute-done.23.refs_10_ = bf16[288,128]{1,0:T(8,128)(2,1)S(1)} collective-permute-done((bf16[288,128]{1,0:T(8,128)(2,1)S(1)}, bf16[288,128]{1,0:T(8,128)(2,1)S(1)}, u32[]{:S(2)}, u32[]{:S(2)}) %collective-permute-start.23) | collective-permute-done | bytes 73760 | tf_op jit(solution)/shard_map/ppermute | solution.py:49
  25.1 1.5 %collective-permute-start.16 = (bf16[128,512]{1,0:T(8,128)(2,1)S(1)}, bf16[128,512]{1,0:T(8,128)(2,1)}, u32[]{:S(2)}, u32[]{:S(2)}) collective-permute-start(bf16[128,512]{1,0:T(8,128)(2,1)S(1)} %shard_map.136.refs_0_), channel_id=1, source_target_pairs={{0,24},{4,28},{8,16},{12,20},{16,8},{20,12},{24,0},{28,4},{1,25},{... | collective-permute-start | bytes 393224 | tf_op jit(solution)/shard_map/ppermute | solution.py:49
  28.6 3.0 %collective-permute-done.16.refs_6_ = bf16[128,512]{1,0:T(8,128)(2,1)} collective-permute-done((bf16[128,512]{1,0:T(8,128)(2,1)S(1)}, bf16[128,512]{1,0:T(8,128)(2,1)}, u32[]{:S(2)}, u32[]{:S(2)}) %collective-permute-start.16) | collective-permute-done | bytes 131104 | tf_op jit(solution)/shard_map/ppermute | solution.py:49
  33.8 2.3 %collective-permute-start.7 = (bf16[128,512]{1,0:T(8,128)(2,1)S(1)}, bf16[128,512]{1,0:T(8,128)(2,1)S(1)}, u32[]{:S(2)}, u32[]{:S(2)}) collective-permute-start(bf16[128,512]{1,0:T(8,128)(2,1)S(1)} %shard_map.136.refs_0_), channel_id=1, source_target_pairs={{0,1},{1,0},{2,3},{3,2},{4,5},{5,4},{6,7},{7,6},{8,9},{9,8},{10,11... | collective-permute-start | bytes 393224 | tf_op jit(solution)/shard_map/ppermute | solution.py:49
  36.1 19.2 %collective-permute-done.9 = bf16[128,512]{1,0:T(8,128)(2,1)S(1)} collective-permute-done((bf16[128,512]{1,0:T(8,128)(2,1)S(1)}, bf16[128,512]{1,0:T(8,128)(2,1)S(1)}, u32[]{:S(2)}, u32[]{:S(2)}) %collective-permute-start.9) | collective-permute-done | bytes 131104 | tf_op jit(solution)/shard_map/ppermute | solution.py:49
  55.2 7.3 %collective-permute-done.8 = bf16[128,512]{1,0:T(8,128)(2,1)S(1)} collective-permute-done((bf16[128,512]{1,0:T(8,128)(2,1)S(1)}, bf16[128,512]{1,0:T(8,128)(2,1)S(1)}, u32[]{:S(2)}, u32[]{:S(2)}) %collective-permute-start.8) | collective-permute-done | bytes 131104 | tf_op jit(solution)/shard_map/ppermute | solution.py:49
  64.6 2.4 %collective-permute-start.13 = (bf16[128,1536]{1,0:T(8,128)(2,1)S(1)}, bf16[128,1536]{1,0:T(8,128)(2,1)S(1)}, u32[]{:S(2)}, u32[]{:S(2)}) collective-permute-start(bf16[128,1536]{1,0:T(8,128)(2,1)S(1)} %pad_maximum_fusion.refs_0_), channel_id=1, source_target_pairs={{0,24},{4,28},{8,16},{12,20},{16,8},{20,12},{24,0},{28,4},{1,25},{... | collective-permute-start | bytes 1179656 | tf_op jit(solution)/shard_map/ppermute | solution.py:49
  71.6 5.0 %shard_map.137.refs_11_ = bf16[1024,1024]{1,0:T(8,128)(2,1)} custom-call(s32[1]{0:T(128)} %bitcast.rank_ref, bf16[128,512]{1,0:T(8,128)(2,1)} %copy-done.1, bf16[128,512]{1,0:T(8,128)(2,1)} %copy-done.7, bf16[128,512]{1,0:T(8,128)(2,1)} %copy-done.6, bf16[128,512]{1,0:T(8,128)(2,1)} %copy-done.8, bf16[128,512]{1,0:T(8,128)(2,1)} %copy-done.5, ...), custom_call_target="tpu_custom_call" | custom-call | flops 1073741824 | bytes 8388608 | tf_op jit(solution)/shard_map/pallas_call | solution.py:451
  77.5 7.9 %collective-permute-done.12.refs_4_ = bf16[128,1536]{1,0:T(8,128)(2,1)} collective-permute-done((bf16[128,1536]{1,0:T(8,128)(2,1)S(1)}, bf16[128,1536]{1,0:T(8,128)(2,1)}, u32[]{:S(2)}, u32[]{:S(2)}) %collective-permute-start.12) | collective-permute-done | bytes 393248 | tf_op jit(solution)/shard_map/ppermute | solution.py:49
  89.2 1.6 %copy-done = bf16[1024,1024]{1,0:T(8,128)(2,1)S(1)} copy-done((bf16[1024,1024]{1,0:T(8,128)(2,1)S(1)}, bf16[1024,1024]{1,0:T(8,128)(2,1)}, u32[]{:S(2)}) %copy-start) | copy-done | bytes 2097176
  90.8 9.0 %shard_map.138 = (bf16[144,512]{1,0:T(8,128)(2,1)S(1)}, bf16[144,512]{1,0:T(8,128)(2,1)S(1)}, bf16[144,512]{1,0:T(8,128)(2,1)S(1)}, bf16[144,512]{1,0:T(8,128)(2...) custom-call(s32[1]{0:T(128)} %bitcast.rank_ref, ...), custom_call_target="tpu_custom_call" | custom-call | flops 5368709120 | bytes 12582912 | tf_op jit(solution)/shard_map/pallas_call | solution.py:467
  110.6 2.1 %collective-permute-done.38.refs_2_ = bf16[144,512]{1,0:T(8,128)(2,1)S(1)} collective-permute-done((bf16[144,512]{1,0:T(8,128)(2,1)S(1)}, bf16[144,512]{1,0:T(8,128)(2,1)S(1)}, u32[]{:S(2)}, u32[]{:S(2)}) %collective-permute-start.38) | collective-permute-done | bytes 147488 | tf_op jit(solution)/shard_map/ppermute | solution.py:49
  114.4 2.6 %collective-permute-start.43 = (bf16[288,128]{1,0:T(8,128)(2,1)S(1)}, bf16[288,128]{1,0:T(8,128)(2,1)S(1)}, u32[]{:S(2)}, u32[]{:S(2)}) collective-permute-start(bf16[288,128]{1,0:T(8,128)(2,1)S(1)} %get-tuple-element.112.refs_0_), channel_id=1, source_target_pairs={{0,3},{1,2},{2,1},{3,0},{4,7},{5,6},{6,5},{7,4},{8,11},{9,10},{10,... | collective-permute-start | bytes 221192 | tf_op jit(solution)/shard_map/ppermute | solution.py:49
  118.9 2.2 %collective-permute-done.43.refs_3_ = bf16[288,128]{1,0:T(8,128)(2,1)S(1)} collective-permute-done((bf16[288,128]{1,0:T(8,128)(2,1)S(1)}, bf16[288,128]{1,0:T(8,128)(2,1)S(1)}, u32[]{:S(2)}, u32[]{:S(2)}) %collective-permute-start.43) | collective-permute-done | bytes 73760 | tf_op jit(solution)/shard_map/ppermute | solution.py:49
  121.1 1.5 %collective-permute-start.41 = (bf16[288,128]{1,0:T(8,128)(2,1)S(1)}, bf16[288,128]{1,0:T(8,128)(2,1)S(1)}, u32[]{:S(2)}, u32[]{:S(2)}) collective-permute-start(bf16[288,128]{1,0:T(8,128)(2,1)S(1)} %get-tuple-element.112.refs_0_), channel_id=1, source_target_pairs={{0,1},{1,0},{2,3},{3,2},{4,5},{5,4},{6,7},{7,6},{8,9},{9,8},{10,11... | collective-permute-start | bytes 221192 | tf_op jit(solution)/shard_map/ppermute | solution.py:49
  122.7 1.5 %collective-permute-done.42.refs_2_ = bf16[288,128]{1,0:T(8,128)(2,1)S(1)} collective-permute-done((bf16[288,128]{1,0:T(8,128)(2,1)S(1)}, bf16[288,128]{1,0:T(8,128)(2,1)S(1)}, u32[]{:S(2)}, u32[]{:S(2)}) %collective-permute-start.42) | collective-permute-done | bytes 73760 | tf_op jit(solution)/shard_map/ppermute | solution.py:49
  127.2 2.2 %collective-permute-start.53 = (bf16[544,128]{1,0:T(8,128)(2,1)S(1)}, bf16[544,128]{1,0:T(8,128)(2,1)S(1)}, u32[]{:S(2)}, u32[]{:S(2)}) collective-permute-start(bf16[544,128]{1,0:T(8,128)(2,1)S(1)} %get-tuple-element.134), channel_id=1, source_target_pairs={{0,24},{4,28},{8,16},{12,20},{16,8},{20,12},{24,0},{28,4},{1,25},{... | collective-permute-start | bytes 417800 | tf_op jit(solution)/shard_map/ppermute | solution.py:49
  129.4 1.6 %collective-permute-done.51.refs_2_ = bf16[544,128]{1,0:T(8,128)(2,1)S(1)} collective-permute-done((bf16[544,128]{1,0:T(8,128)(2,1)S(1)}, bf16[544,128]{1,0:T(8,128)(2,1)S(1)}, u32[]{:S(2)}, u32[]{:S(2)}) %collective-permute-start.51) | collective-permute-done | bytes 139296 | tf_op jit(solution)/shard_map/ppermute | solution.py:49
  131.6 1.5 %collective-permute-done.53.refs_6_ = bf16[544,128]{1,0:T(8,128)(2,1)S(1)} collective-permute-done((bf16[544,128]{1,0:T(8,128)(2,1)S(1)}, bf16[544,128]{1,0:T(8,128)(2,1)S(1)}, u32[]{:S(2)}, u32[]{:S(2)}) %collective-permute-start.53) | collective-permute-done | bytes 139296 | tf_op jit(solution)/shard_map/ppermute | solution.py:49
  135.2 3.6 %shard_map.141 = bf16[64,1024]{1,0:T(8,128)(2,1)} custom-call(s32[1]{0:T(128)} %bitcast.rank_ref, bf16[544,128]{1,0:T(8,128)(2,1)S(1)} %get-tuple-element.135.refs_0_, bf16[544,128]{1,0:T(8,128)(2,1)S(1)} %collective-permute-done.54.refs_1_, bf16[544,128]{1,0:T(8,128)(2,1)S(1)} %collective-permute-done.51.refs_2_, ...), custom_call_target="tpu_custom_call" | custom-call | flops 33554432 | bytes 4194304 | tf_op jit(solution)/shard_map/pallas_call | solution.py:527
  (145 shorter events, 48.8 us)
Async XLA Ops:
  0.0 63.0 %collective-permute-start.10 = (bf16[512,1024]{1,0:T(8,128)(2,1)}, bf16[512,1024]{1,0:T(8,128)(2,1)S(1)}, u32[]{:S(2)}, u32[]{:S(2)}) collective-permute-start(bf16[512,1024]{1,0:T(8,128)(2,1)} %refs_8_.1), channel_id=1, source_target_pairs={{0,1},{1,0},{2,3},{3,2},{4,5},{5,4},{6,7},{7,6},{8,9},{9,8},{10,11... | collective-permute-start | bytes 3145736 | tf_op jit(solution)/shard_map/ppermute | solution.py:49
  3.1 60.0 %collective-permute-start.32 = (bf16[512,1024]{1,0:T(8,128)(2,1)}, bf16[512,1024]{1,0:T(8,128)(2,1)S(1)}, u32[]{:S(2)}, u32[]{:S(2)}) collective-permute-start(bf16[512,1024]{1,0:T(8,128)(2,1)} %refs_8_.1), channel_id=1, source_target_pairs={{0,3},{1,2},{2,1},{3,0},{4,7},{5,6},{6,5},{7,4},{8,11},{9,10},{10,... | collective-permute-start | bytes 3145736 | tf_op jit(solution)/shard_map/ppermute | solution.py:49
  25.1 6.6 %collective-permute-start.16 = (bf16[128,512]{1,0:T(8,128)(2,1)S(1)}, bf16[128,512]{1,0:T(8,128)(2,1)}, u32[]{:S(2)}, u32[]{:S(2)}) collective-permute-start(bf16[128,512]{1,0:T(8,128)(2,1)S(1)} %shard_map.136.refs_0_), channel_id=1, source_target_pairs={{0,24},{4,28},{8,16},{12,20},{16,8},{20,12},{24,0},{28,4},{1,25},{... | collective-permute-start | bytes 393224 | tf_op jit(solution)/shard_map/ppermute | solution.py:49
  26.6 7.0 %collective-permute-start.15 = (bf16[128,512]{1,0:T(8,128)(2,1)S(1)}, bf16[128,512]{1,0:T(8,128)(2,1)S(1)}, u32[]{:S(2)}, u32[]{:S(2)}) collective-permute-start(bf16[128,512]{1,0:T(8,128)(2,1)S(1)} %shard_map.136.refs_0_), channel_id=1, source_target_pairs={{0,16},{4,20},{8,24},{12,28},{16,0},{20,4},{24,8},{28,12},{1,17},{... | collective-permute-start | bytes 393224 | tf_op jit(solution)/shard_map/ppermute | solution.py:49
  27.4 6.4 %collective-permute-start.14 = (bf16[128,512]{1,0:T(8,128)(2,1)S(1)}, bf16[128,512]{1,0:T(8,128)(2,1)S(1)}, u32[]{:S(2)}, u32[]{:S(2)}) collective-permute-start(bf16[128,512]{1,0:T(8,128)(2,1)S(1)} %shard_map.136.refs_0_), channel_id=1, source_target_pairs={{0,8},{4,12},{8,0},{12,4},{16,24},{20,28},{24,16},{28,20},{1,9},{5... | collective-permute-start | bytes 393224 | tf_op jit(solution)/shard_map/ppermute | solution.py:49
  31.7 23.6 %collective-permute-start.9 = (bf16[128,512]{1,0:T(8,128)(2,1)S(1)}, bf16[128,512]{1,0:T(8,128)(2,1)S(1)}, u32[]{:S(2)}, u32[]{:S(2)}) collective-permute-start(bf16[128,512]{1,0:T(8,128)(2,1)S(1)} %shard_map.136.refs_0_), channel_id=1, source_target_pairs={{0,3},{1,2},{2,1},{3,0},{4,7},{5,6},{6,5},{7,4},{8,11},{9,10},{10,... | collective-permute-start | bytes 393224 | tf_op jit(solution)/shard_map/ppermute | solution.py:49
  33.6 28.9 %collective-permute-start.8 = (bf16[128,512]{1,0:T(8,128)(2,1)S(1)}, bf16[128,512]{1,0:T(8,128)(2,1)S(1)}, u32[]{:S(2)}, u32[]{:S(2)}) collective-permute-start(bf16[128,512]{1,0:T(8,128)(2,1)S(1)} %shard_map.136.refs_0_), channel_id=1, source_target_pairs={{0,2},{1,3},{2,0},{3,1},{4,6},{5,7},{6,4},{7,5},{8,10},{9,11},{10,... | collective-permute-start | bytes 393224 | tf_op jit(solution)/shard_map/ppermute | solution.py:49
  33.8 28.8 %collective-permute-start.7 = (bf16[128,512]{1,0:T(8,128)(2,1)S(1)}, bf16[128,512]{1,0:T(8,128)(2,1)S(1)}, u32[]{:S(2)}, u32[]{:S(2)}) collective-permute-start(bf16[128,512]{1,0:T(8,128)(2,1)S(1)} %shard_map.136.refs_0_), channel_id=1, source_target_pairs={{0,1},{1,0},{2,3},{3,2},{4,5},{5,4},{6,7},{7,6},{8,9},{9,8},{10,11... | collective-permute-start | bytes 393224 | tf_op jit(solution)/shard_map/ppermute | solution.py:49
  55.2 8.1 %collective-permute-start.24 = (bf16[288,128]{1,0:T(8,128)(2,1)S(1)}, bf16[288,128]{1,0:T(8,128)(2,1)S(1)}, u32[]{:S(2)}, u32[]{:S(2)}) collective-permute-start(bf16[288,128]{1,0:T(8,128)(2,1)S(1)} %pad_maximum_fusion.1.refs_4_), channel_id=1, source_target_pairs={{0,4},{4,0},{8,12},{12,8},{16,20},{20,16},{24,28},{28,24},{1,5},{5... | collective-permute-start | bytes 221192 | tf_op jit(solution)/shard_map/ppermute | solution.py:49
  63.1 26.1 %collective-permute-start.33 = (bf16[512,1024]{1,0:T(8,128)(2,1)S(1)}, bf16[512,1024]{1,0:T(8,128)(2,1)}, u32[]{:S(2)}, u32[]{:S(2)}) collective-permute-start(bf16[512,1024]{1,0:T(8,128)(2,1)S(1)} %collective-permute-done.32.refs_10_), channel_id=1, source_target_pairs={{0,1},{1,0},{2,3},{3,2},{4,5},{5,4},{6,7},{7,6},{8,9},{9,8},{10,11... | collective-permute-start | bytes 3145736 | tf_op jit(solution)/shard_map/ppermute | solution.py:49
  64.6 12.9 %collective-permute-start.13 = (bf16[128,1536]{1,0:T(8,128)(2,1)S(1)}, bf16[128,1536]{1,0:T(8,128)(2,1)S(1)}, u32[]{:S(2)}, u32[]{:S(2)}) collective-permute-start(bf16[128,1536]{1,0:T(8,128)(2,1)S(1)} %pad_maximum_fusion.refs_0_), channel_id=1, source_target_pairs={{0,24},{4,28},{8,16},{12,20},{16,8},{20,12},{24,0},{28,4},{1,25},{... | collective-permute-start | bytes 1179656 | tf_op jit(solution)/shard_map/ppermute | solution.py:49
  67.1 18.4 %collective-permute-start.12 = (bf16[128,1536]{1,0:T(8,128)(2,1)S(1)}, bf16[128,1536]{1,0:T(8,128)(2,1)}, u32[]{:S(2)}, u32[]{:S(2)}) collective-permute-start(bf16[128,1536]{1,0:T(8,128)(2,1)S(1)} %pad_maximum_fusion.refs_0_), channel_id=1, source_target_pairs={{0,16},{4,20},{8,24},{12,28},{16,0},{20,4},{24,8},{28,12},{1,17},{... | collective-permute-start | bytes 1179656 | tf_op jit(solution)/shard_map/ppermute | solution.py:49
  67.6 17.9 %collective-permute-start.11 = (bf16[128,1536]{1,0:T(8,128)(2,1)S(1)}, bf16[128,1536]{1,0:T(8,128)(2,1)}, u32[]{:S(2)}, u32[]{:S(2)}) collective-permute-start(bf16[128,1536]{1,0:T(8,128)(2,1)S(1)} %pad_maximum_fusion.refs_0_), channel_id=1, source_target_pairs={{0,8},{4,12},{8,0},{12,4},{16,24},{20,28},{24,16},{28,20},{1,9},{5... | collective-permute-start | bytes 1179656 | tf_op jit(solution)/shard_map/ppermute | solution.py:49
  102.4 6.7 %collective-permute-start.36 = (bf16[144,512]{1,0:T(8,128)(2,1)S(1)}, bf16[144,512]{1,0:T(8,128)(2,1)S(1)}, u32[]{:S(2)}, u32[]{:S(2)}) collective-permute-start(bf16[144,512]{1,0:T(8,128)(2,1)S(1)} %add_convert_fusion.2), channel_id=1, source_target_pairs={{0,8},{4,12},{8,0},{12,4},{16,24},{20,28},{24,16},{28,20},{1,9},{5... | collective-permute-start | bytes 442376 | tf_op jit(solution)/shard_map/ppermute | solution.py:49
  103.9 8.8 %collective-permute-start.38 = (bf16[144,512]{1,0:T(8,128)(2,1)S(1)}, bf16[144,512]{1,0:T(8,128)(2,1)S(1)}, u32[]{:S(2)}, u32[]{:S(2)}) collective-permute-start(bf16[144,512]{1,0:T(8,128)(2,1)S(1)} %add_convert_fusion.1), channel_id=1, source_target_pairs={{0,16},{4,20},{8,24},{12,28},{16,0},{20,4},{24,8},{28,12},{1,17},{... | collective-permute-start | bytes 442376 | tf_op jit(solution)/shard_map/ppermute | solution.py:49
  104.6 9.1 %collective-permute-start.40 = (bf16[144,512]{1,0:T(8,128)(2,1)S(1)}, bf16[144,512]{1,0:T(8,128)(2,1)S(1)}, u32[]{:S(2)}, u32[]{:S(2)}) collective-permute-start(bf16[144,512]{1,0:T(8,128)(2,1)S(1)} %add_convert_fusion), channel_id=1, source_target_pairs={{0,24},{4,28},{8,16},{12,20},{16,8},{20,12},{24,0},{28,4},{1,25},{... | collective-permute-start | bytes 442376 | tf_op jit(solution)/shard_map/ppermute | solution.py:49
  105.9 12.3 %collective-permute-start.44 = (bf16[128,512]{1,0:T(8,128)(2,1)S(1)}, bf16[128,512]{1,0:T(8,128)(2,1)S(1)}, u32[]{:S(2)}, u32[]{:S(2)}) collective-permute-start(bf16[128,512]{1,0:T(8,128)(2,1)S(1)} %get-tuple-element.116), channel_id=1, source_target_pairs={{0,4},{4,0},{8,12},{12,8},{16,20},{20,16},{24,28},{28,24},{1,5},{5... | collective-permute-start | bytes 393224 | tf_op jit(solution)/shard_map/ppermute | solution.py:49
  107.4 9.6 %collective-permute-start.49 = (bf16[128,512]{1,0:T(8,128)(2,1)S(1)}, bf16[128,512]{1,0:T(8,128)(2,1)S(1)}, u32[]{:S(2)}, u32[]{:S(2)}) collective-permute-start(bf16[128,512]{1,0:T(8,128)(2,1)S(1)} %get-tuple-element.128), channel_id=1, source_target_pairs={{0,4},{4,0},{8,12},{12,8},{16,20},{20,16},{24,28},{28,24},{1,5},{5... | collective-permute-start | bytes 393224 | tf_op jit(solution)/shard_map/ppermute | solution.py:49
  109.1 16.4 %collective-permute-start.46 = (bf16[128,512]{1,0:T(8,128)(2,1)S(1)}, bf16[128,512]{1,0:T(8,128)(2,1)S(1)}, u32[]{:S(2)}, u32[]{:S(2)}) collective-permute-start(bf16[128,512]{1,0:T(8,128)(2,1)S(1)} %add_convert_fusion.6), channel_id=1, source_target_pairs={{0,8},{4,12},{8,0},{12,4},{16,24},{20,28},{24,16},{28,20},{1,9},{5... | collective-permute-start | bytes 393224 | tf_op jit(solution)/shard_map/ppermute | solution.py:49
  112.6 12.9 %collective-permute-start.48 = (bf16[128,512]{1,0:T(8,128)(2,1)S(1)}, bf16[128,512]{1,0:T(8,128)(2,1)S(1)}, u32[]{:S(2)}, u32[]{:S(2)}) collective-permute-start(bf16[128,512]{1,0:T(8,128)(2,1)S(1)} %add_convert_fusion.5), channel_id=1, source_target_pairs={{0,16},{4,20},{8,24},{12,28},{16,0},{20,4},{24,8},{28,12},{1,17},{... | collective-permute-start | bytes 393224 | tf_op jit(solution)/shard_map/ppermute | solution.py:49
  114.4 6.8 %collective-permute-start.43 = (bf16[288,128]{1,0:T(8,128)(2,1)S(1)}, bf16[288,128]{1,0:T(8,128)(2,1)S(1)}, u32[]{:S(2)}, u32[]{:S(2)}) collective-permute-start(bf16[288,128]{1,0:T(8,128)(2,1)S(1)} %get-tuple-element.112.refs_0_), channel_id=1, source_target_pairs={{0,3},{1,2},{2,1},{3,0},{4,7},{5,6},{6,5},{7,4},{8,11},{9,10},{10,... | collective-permute-start | bytes 221192 | tf_op jit(solution)/shard_map/ppermute | solution.py:49
  117.0 8.5 %collective-permute-start.50 = (bf16[128,512]{1,0:T(8,128)(2,1)S(1)}, bf16[128,512]{1,0:T(8,128)(2,1)S(1)}, u32[]{:S(2)}, u32[]{:S(2)}) collective-permute-start(bf16[128,512]{1,0:T(8,128)(2,1)S(1)} %add_convert_fusion.4), channel_id=1, source_target_pairs={{0,24},{4,28},{8,16},{12,20},{16,8},{20,12},{24,0},{28,4},{1,25},{... | collective-permute-start | bytes 393224 | tf_op jit(solution)/shard_map/ppermute | solution.py:49
  118.1 6.0 %collective-permute-start.42 = (bf16[288,128]{1,0:T(8,128)(2,1)S(1)}, bf16[288,128]{1,0:T(8,128)(2,1)S(1)}, u32[]{:S(2)}, u32[]{:S(2)}) collective-permute-start(bf16[288,128]{1,0:T(8,128)(2,1)S(1)} %get-tuple-element.112.refs_0_), channel_id=1, source_target_pairs={{0,2},{1,3},{2,0},{3,1},{4,6},{5,7},{6,4},{7,5},{8,10},{9,11},{10,... | collective-permute-start | bytes 221192 | tf_op jit(solution)/shard_map/ppermute | solution.py:49
  127.2 6.0 %collective-permute-start.53 = (bf16[544,128]{1,0:T(8,128)(2,1)S(1)}, bf16[544,128]{1,0:T(8,128)(2,1)S(1)}, u32[]{:S(2)}, u32[]{:S(2)}) collective-permute-start(bf16[544,128]{1,0:T(8,128)(2,1)S(1)} %get-tuple-element.134), channel_id=1, source_target_pairs={{0,24},{4,28},{8,16},{12,20},{16,8},{20,12},{24,0},{28,4},{1,25},{... | collective-permute-start | bytes 417800 | tf_op jit(solution)/shard_map/ppermute | solution.py:49
  (47 other events, 470.6 us)

commit v5 on v4

--- a/solution.py
+++ b/solution.py
@@ -521,7 +521,10 @@
         size=map_rows * rows * 2 * n_sec,
         limit=8 * scale,
     )(rank_arg, *map_parts, *gate_pieces, inputs, scales)
-    scan_pieces, _ = gather_seq(messages, n_seq)
+    scan_pieces = []
+    for k in range(0, n_seq, 2):
+        piece = swap(messages[k // 2], "seq", n_seq, k) if k else messages[0]
+        scan_pieces += [piece, swap(piece, "seq", n_seq, 1)]
 
     wide = NST * own
     return call(

time: 139 us -> 139 us (level)
  transfers between devices with their start and end apart: 58 -> 58, of which waited for: 35 -> 32; matrix products, arithmetic and copies ran while one was open for 5% -> 5% of each run, Pallas kernels for 5% -> 5%
where the time goes in v5:
time: 139 us; the launch traced here: 138 us
  waiting for transfers between devices  63.5 us (46%)
  starting transfers between devices  45 us (32%)
  Pallas kernels  19.9 us (14%)
  local copies, waits for them, and re-layouts  7.21 us (5%)
  other arithmetic  2.21 us (2%)
    ppermute x58, waiting for transfers between devices, swap(): return lax.ppermute(x, axis, [(i, i ^ bits) for i in range(count)])  63.5 us
    ppermute x58, starting transfers between devices, swap(): return lax.ppermute(x, axis, [(i, i ^ bits) for i in range(count)])  45 us
    pallas_call x1, Pallas kernels, body(): call(functools.partial(mix_kernel, n_seq, used), [shape((HALO + rows, cha...  9.02 us
    unnamed x29, local copies, waits for them, and re-layouts  6.22 us
    pallas_call x1, Pallas kernels, body(): call(functools.partial(own_kernel, n_seq), shape((seq_len, features), BF1...  5.02 us
    pallas_call x1, Pallas kernels, body(): call(functools.partial(scan_kernel, n_seq), shape((own, seq_len), BF16),...  3.61 us
  transfers between devices with their start and end apart: 58, of which 32 were waited for; matrix products, arithmetic and copies ran while one was open for 5% of the time, Pallas kernels for 5%

profile of v5, /device:TPU:0, one launch (start us, length us, event | category | flops | bytes accessed | tf_op | source)
XLA Modules:
  0.0 138.1 jit_solution(18244863585874837602)
XLA Ops:
  0.0 3.1 %collective-permute-start.10 = (bf16[512,1024]{1,0:T(8,128)(2,1)}, bf16[512,1024]{1,0:T(8,128)(2,1)S(1)}, u32[]{:S(2)}, u32[]{:S(2)}) collective-permute-start(bf16[512,1024]{1,0:T(8,128)(2,1)} %refs_8_.1), channel_id=1, source_target_pairs={{0,1},{1,0},{2,3},{3,2},{4,5},{5,4},{6,7},{7,6},{8,9},{9,8},{10,11... | collective-permute-start | bytes 3145736 | tf_op jit(solution)/shard_map/ppermute | solution.py:49
  3.1 2.5 %collective-permute-start.32 = (bf16[512,1024]{1,0:T(8,128)(2,1)}, bf16[512,1024]{1,0:T(8,128)(2,1)S(1)}, u32[]{:S(2)}, u32[]{:S(2)}) collective-permute-start(bf16[512,1024]{1,0:T(8,128)(2,1)} %refs_8_.1), channel_id=1, source_target_pairs={{0,3},{1,2},{2,1},{3,0},{4,7},{5,6},{6,5},{7,4},{8,11},{9,10},{10,... | collective-permute-start | bytes 3145736 | tf_op jit(solution)/shard_map/ppermute | solution.py:49
  7.1 2.5 %collective-permute-start.2 = (bf16[128,256]{1,0:T(8,128)(2,1)S(1)}, bf16[128,256]{1,0:T(8,128)(2,1)S(1)}, u32[]{:S(2)}, u32[]{:S(2)}) collective-permute-start(bf16[128,256]{1,0:T(8,128)(2,1)S(1)} %constant_dynamic-update-slice_fusion.refs_0_), channel_id=1, source_target_pairs={{0,24},{4,28},{8,16},{12,20},{16,8},{20,12},{24,0},{28,4},{1,25},{... | collective-permute-start | bytes 196616 | tf_op jit(solution)/shard_map/ppermute | solution.py:49
  19.5 1.6 %collective-permute-start.23 = (bf16[288,128]{1,0:T(8,128)(2,1)S(1)}, bf16[288,128]{1,0:T(8,128)(2,1)S(1)}, u32[]{:S(2)}, u32[]{:S(2)}) collective-permute-start(bf16[288,128]{1,0:T(8,128)(2,1)S(1)} %pad_maximum_fusion.1.refs_4_), channel_id=1, source_target_pairs={{0,24},{4,28},{8,16},{12,20},{16,8},{20,12},{24,0},{28,4},{1,25},{... | collective-permute-start | bytes 221192 | tf_op jit(solution)/shard_map/ppermute | solution.py:49
  21.5 1.5 %collective-permute-start.21 = (bf16[288,128]{1,0:T(8,128)(2,1)S(1)}, bf16[288,128]{1,0:T(8,128)(2,1)S(1)}, u32[]{:S(2)}, u32[]{:S(2)}) collective-permute-start(bf16[288,128]{1,0:T(8,128)(2,1)S(1)} %pad_maximum_fusion.1.refs_4_), channel_id=1, source_target_pairs={{0,8},{4,12},{8,0},{12,4},{16,24},{20,28},{24,16},{28,20},{1,9},{5... | collective-permute-start | bytes 221192 | tf_op jit(solution)/shard_map/ppermute | solution.py:49
  23.0 2.0 %collective-permute-done.23.refs_10_ = bf16[288,128]{1,0:T(8,128)(2,1)S(1)} collective-permute-done((bf16[288,128]{1,0:T(8,128)(2,1)S(1)}, bf16[288,128]{1,0:T(8,128)(2,1)S(1)}, u32[]{:S(2)}, u32[]{:S(2)}) %collective-permute-start.23) | collective-permute-done | bytes 73760 | tf_op jit(solution)/shard_map/ppermute | solution.py:49
  25.1 1.5 %collective-permute-start.16 = (bf16[128,512]{1,0:T(8,128)(2,1)S(1)}, bf16[128,512]{1,0:T(8,128)(2,1)}, u32[]{:S(2)}, u32[]{:S(2)}) collective-permute-start(bf16[128,512]{1,0:T(8,128)(2,1)S(1)} %shard_map.136.refs_0_), channel_id=1, source_target_pairs={{0,24},{4,28},{8,16},{12,20},{16,8},{20,12},{24,0},{28,4},{1,25},{... | collective-permute-start | bytes 393224 | tf_op jit(solution)/shard_map/ppermute | solution.py:49
  28.6 3.0 %collective-permute-done.16.refs_6_ = bf16[128,512]{1,0:T(8,128)(2,1)} collective-permute-done((bf16[128,512]{1,0:T(8,128)(2,1)S(1)}, bf16[128,512]{1,0:T(8,128)(2,1)}, u32[]{:S(2)}, u32[]{:S(2)}) %collective-permute-start.16) | collective-permute-done | bytes 131104 | tf_op jit(solution)/shard_map/ppermute | solution.py:49
  33.8 2.3 %collective-permute-start.7 = (bf16[128,512]{1,0:T(8,128)(2,1)S(1)}, bf16[128,512]{1,0:T(8,128)(2,1)S(1)}, u32[]{:S(2)}, u32[]{:S(2)}) collective-permute-start(bf16[128,512]{1,0:T(8,128)(2,1)S(1)} %shard_map.136.refs_0_), channel_id=1, source_target_pairs={{0,1},{1,0},{2,3},{3,2},{4,5},{5,4},{6,7},{7,6},{8,9},{9,8},{10,11... | collective-permute-start | bytes 393224 | tf_op jit(solution)/shard_map/ppermute | solution.py:49
  36.1 19.2 %collective-permute-done.9 = bf16[128,512]{1,0:T(8,128)(2,1)S(1)} collective-permute-done((bf16[128,512]{1,0:T(8,128)(2,1)S(1)}, bf16[128,512]{1,0:T(8,128)(2,1)S(1)}, u32[]{:S(2)}, u32[]{:S(2)}) %collective-permute-start.9) | collective-permute-done | bytes 131104 | tf_op jit(solution)/shard_map/ppermute | solution.py:49
  55.2 7.3 %collective-permute-done.8 = bf16[128,512]{1,0:T(8,128)(2,1)S(1)} collective-permute-done((bf16[128,512]{1,0:T(8,128)(2,1)S(1)}, bf16[128,512]{1,0:T(8,128)(2,1)S(1)}, u32[]{:S(2)}, u32[]{:S(2)}) %collective-permute-start.8) | collective-permute-done | bytes 131104 | tf_op jit(solution)/shard_map/ppermute | solution.py:49
  64.6 2.4 %collective-permute-start.13 = (bf16[128,1536]{1,0:T(8,128)(2,1)S(1)}, bf16[128,1536]{1,0:T(8,128)(2,1)S(1)}, u32[]{:S(2)}, u32[]{:S(2)}) collective-permute-start(bf16[128,1536]{1,0:T(8,128)(2,1)S(1)} %pad_maximum_fusion.refs_0_), channel_id=1, source_target_pairs={{0,24},{4,28},{8,16},{12,20},{16,8},{20,12},{24,0},{28,4},{1,25},{... | collective-permute-start | bytes 1179656 | tf_op jit(solution)/shard_map/ppermute | solution.py:49
  71.6 5.0 %shard_map.137.refs_11_ = bf16[1024,1024]{1,0:T(8,128)(2,1)} custom-call(s32[1]{0:T(128)} %bitcast.rank_ref, bf16[128,512]{1,0:T(8,128)(2,1)} %copy-done.1, bf16[128,512]{1,0:T(8,128)(2,1)} %copy-done.7, bf16[128,512]{1,0:T(8,128)(2,1)} %copy-done.6, bf16[128,512]{1,0:T(8,128)(2,1)} %copy-done.8, bf16[128,512]{1,0:T(8,128)(2,1)} %copy-done.5, ...), custom_call_target="tpu_custom_call" | custom-call | flops 1073741824 | bytes 8388608 | tf_op jit(solution)/shard_map/pallas_call | solution.py:451
  77.5 7.9 %collective-permute-done.12.refs_4_ = bf16[128,1536]{1,0:T(8,128)(2,1)} collective-permute-done((bf16[128,1536]{1,0:T(8,128)(2,1)S(1)}, bf16[128,1536]{1,0:T(8,128)(2,1)}, u32[]{:S(2)}, u32[]{:S(2)}) %collective-permute-start.12) | collective-permute-done | bytes 393248 | tf_op jit(solution)/shard_map/ppermute | solution.py:49
  89.2 1.6 %copy-done = bf16[1024,1024]{1,0:T(8,128)(2,1)S(1)} copy-done((bf16[1024,1024]{1,0:T(8,128)(2,1)S(1)}, bf16[1024,1024]{1,0:T(8,128)(2,1)}, u32[]{:S(2)}) %copy-start) | copy-done | bytes 2097176
  90.8 9.0 %shard_map.138 = (bf16[144,512]{1,0:T(8,128)(2,1)S(1)}, bf16[144,512]{1,0:T(8,128)(2,1)S(1)}, bf16[144,512]{1,0:T(8,128)(2,1)S(1)}, bf16[144,512]{1,0:T(8,128)(2...) custom-call(s32[1]{0:T(128)} %bitcast.rank_ref, ...), custom_call_target="tpu_custom_call" | custom-call | flops 5368709120 | bytes 12582912 | tf_op jit(solution)/shard_map/pallas_call | solution.py:467
  110.6 2.1 %collective-permute-done.38.refs_2_ = bf16[144,512]{1,0:T(8,128)(2,1)S(1)} collective-permute-done((bf16[144,512]{1,0:T(8,128)(2,1)S(1)}, bf16[144,512]{1,0:T(8,128)(2,1)S(1)}, u32[]{:S(2)}, u32[]{:S(2)}) %collective-permute-start.38) | collective-permute-done | bytes 147488 | tf_op jit(solution)/shard_map/ppermute | solution.py:49
  114.4 2.6 %collective-permute-start.43 = (bf16[288,128]{1,0:T(8,128)(2,1)S(1)}, bf16[288,128]{1,0:T(8,128)(2,1)S(1)}, u32[]{:S(2)}, u32[]{:S(2)}) collective-permute-start(bf16[288,128]{1,0:T(8,128)(2,1)S(1)} %get-tuple-element.108.refs_0_), channel_id=1, source_target_pairs={{0,3},{1,2},{2,1},{3,0},{4,7},{5,6},{6,5},{7,4},{8,11},{9,10},{10,... | collective-permute-start | bytes 221192 | tf_op jit(solution)/shard_map/ppermute | solution.py:49
  118.9 2.2 %collective-permute-done.43.refs_3_ = bf16[288,128]{1,0:T(8,128)(2,1)S(1)} collective-permute-done((bf16[288,128]{1,0:T(8,128)(2,1)S(1)}, bf16[288,128]{1,0:T(8,128)(2,1)S(1)}, u32[]{:S(2)}, u32[]{:S(2)}) %collective-permute-start.43) | collective-permute-done | bytes 73760 | tf_op jit(solution)/shard_map/ppermute | solution.py:49
  121.1 1.5 %collective-permute-start.41 = (bf16[288,128]{1,0:T(8,128)(2,1)S(1)}, bf16[288,128]{1,0:T(8,128)(2,1)S(1)}, u32[]{:S(2)}, u32[]{:S(2)}) collective-permute-start(bf16[288,128]{1,0:T(8,128)(2,1)S(1)} %get-tuple-element.108.refs_0_), channel_id=1, source_target_pairs={{0,1},{1,0},{2,3},{3,2},{4,5},{5,4},{6,7},{7,6},{8,9},{9,8},{10,11... | collective-permute-start | bytes 221192 | tf_op jit(solution)/shard_map/ppermute | solution.py:49
  122.7 1.5 %collective-permute-done.42.refs_2_ = bf16[288,128]{1,0:T(8,128)(2,1)S(1)} collective-permute-done((bf16[288,128]{1,0:T(8,128)(2,1)S(1)}, bf16[288,128]{1,0:T(8,128)(2,1)S(1)}, u32[]{:S(2)}, u32[]{:S(2)}) %collective-permute-start.42) | collective-permute-done | bytes 73760 | tf_op jit(solution)/shard_map/ppermute | solution.py:49
  127.2 2.2 %collective-permute-start.56 = (bf16[544,128]{1,0:T(8,128)(2,1)S(1)}, bf16[544,128]{1,0:T(8,128)(2,1)S(1)}, u32[]{:S(2)}, u32[]{:S(2)}) collective-permute-start(bf16[544,128]{1,0:T(8,128)(2,1)S(1)} %get-tuple-element.130), channel_id=1, source_target_pairs={{0,24},{4,28},{8,16},{12,20},{16,8},{20,12},{24,0},{28,4},{1,25},{... | collective-permute-start | bytes 417800 | tf_op jit(solution)/shard_map/ppermute | solution.py:49
  129.4 1.6 %collective-permute-done.52.refs_2_ = bf16[544,128]{1,0:T(8,128)(2,1)S(1)} collective-permute-done((bf16[544,128]{1,0:T(8,128)(2,1)S(1)}, bf16[544,128]{1,0:T(8,128)(2,1)S(1)}, u32[]{:S(2)}, u32[]{:S(2)}) %collective-permute-start.52) | collective-permute-done | bytes 139296 | tf_op jit(solution)/shard_map/ppermute | solution.py:49
  134.5 3.6 %shard_map.141 = bf16[64,1024]{1,0:T(8,128)(2,1)} custom-call(s32[1]{0:T(128)} %bitcast.rank_ref, bf16[544,128]{1,0:T(8,128)(2,1)S(1)} %get-tuple-element.127.refs_0_, bf16[544,128]{1,0:T(8,128)(2,1)S(1)} %collective-permute-done.51.refs_1_, bf16[544,128]{1,0:T(8,128)(2,1)S(1)} %collective-permute-done.52.refs_2_, ...), custom_call_target="tpu_custom_call" | custom-call | flops 33554432 | bytes 4194304 | tf_op jit(solution)/shard_map/pallas_call | solution.py:530
  (145 shorter events, 48.1 us)
Async XLA Ops:
  0.0 63.0 %collective-permute-start.10 = (bf16[512,1024]{1,0:T(8,128)(2,1)}, bf16[512,1024]{1,0:T(8,128)(2,1)S(1)}, u32[]{:S(2)}, u32[]{:S(2)}) collective-permute-start(bf16[512,1024]{1,0:T(8,128)(2,1)} %refs_8_.1), channel_id=1, source_target_pairs={{0,1},{1,0},{2,3},{3,2},{4,5},{5,4},{6,7},{7,6},{8,9},{9,8},{10,11... | collective-permute-start | bytes 3145736 | tf_op jit(solution)/shard_map/ppermute | solution.py:49
  3.1 60.0 %collective-permute-start.32 = (bf16[512,1024]{1,0:T(8,128)(2,1)}, bf16[512,1024]{1,0:T(8,128)(2,1)S(1)}, u32[]{:S(2)}, u32[]{:S(2)}) collective-permute-start(bf16[512,1024]{1,0:T(8,128)(2,1)} %refs_8_.1), channel_id=1, source_target_pairs={{0,3},{1,2},{2,1},{3,0},{4,7},{5,6},{6,5},{7,4},{8,11},{9,10},{10,... | collective-permute-start | bytes 3145736 | tf_op jit(solution)/shard_map/ppermute | solution.py:49
  25.1 6.6 %collective-permute-start.16 = (bf16[128,512]{1,0:T(8,128)(2,1)S(1)}, bf16[128,512]{1,0:T(8,128)(2,1)}, u32[]{:S(2)}, u32[]{:S(2)}) collective-permute-start(bf16[128,512]{1,0:T(8,128)(2,1)S(1)} %shard_map.136.refs_0_), channel_id=1, source_target_pairs={{0,24},{4,28},{8,16},{12,20},{16,8},{20,12},{24,0},{28,4},{1,25},{... | collective-permute-start | bytes 393224 | tf_op jit(solution)/shard_map/ppermute | solution.py:49
  26.6 7.0 %collective-permute-start.15 = (bf16[128,512]{1,0:T(8,128)(2,1)S(1)}, bf16[128,512]{1,0:T(8,128)(2,1)S(1)}, u32[]{:S(2)}, u32[]{:S(2)}) collective-permute-start(bf16[128,512]{1,0:T(8,128)(2,1)S(1)} %shard_map.136.refs_0_), channel_id=1, source_target_pairs={{0,16},{4,20},{8,24},{12,28},{16,0},{20,4},{24,8},{28,12},{1,17},{... | collective-permute-start | bytes 393224 | tf_op jit(solution)/shard_map/ppermute | solution.py:49
  27.4 6.4 %collective-permute-start.14 = (bf16[128,512]{1,0:T(8,128)(2,1)S(1)}, bf16[128,512]{1,0:T(8,128)(2,1)S(1)}, u32[]{:S(2)}, u32[]{:S(2)}) collective-permute-start(bf16[128,512]{1,0:T(8,128)(2,1)S(1)} %shard_map.136.refs_0_), channel_id=1, source_target_pairs={{0,8},{4,12},{8,0},{12,4},{16,24},{20,28},{24,16},{28,20},{1,9},{5... | collective-permute-start | bytes 393224 | tf_op jit(solution)/shard_map/ppermute | solution.py:49
  31.7 23.6 %collective-permute-start.9 = (bf16[128,512]{1,0:T(8,128)(2,1)S(1)}, bf16[128,512]{1,0:T(8,128)(2,1)S(1)}, u32[]{:S(2)}, u32[]{:S(2)}) collective-permute-start(bf16[128,512]{1,0:T(8,128)(2,1)S(1)} %shard_map.136.refs_0_), channel_id=1, source_target_pairs={{0,3},{1,2},{2,1},{3,0},{4,7},{5,6},{6,5},{7,4},{8,11},{9,10},{10,... | collective-permute-start | bytes 393224 | tf_op jit(solution)/shard_map/ppermute | solution.py:49
  33.6 28.9 %collective-permute-start.8 = (bf16[128,512]{1,0:T(8,128)(2,1)S(1)}, bf16[128,512]{1,0:T(8,128)(2,1)S(1)}, u32[]{:S(2)}, u32[]{:S(2)}) collective-permute-start(bf16[128,512]{1,0:T(8,128)(2,1)S(1)} %shard_map.136.refs_0_), channel_id=1, source_target_pairs={{0,2},{1,3},{2,0},{3,1},{4,6},{5,7},{6,4},{7,5},{8,10},{9,11},{10,... | collective-permute-start | bytes 393224 | tf_op jit(solution)/shard_map/ppermute | solution.py:49
  33.8 28.8 %collective-permute-start.7 = (bf16[128,512]{1,0:T(8,128)(2,1)S(1)}, bf16[128,512]{1,0:T(8,128)(2,1)S(1)}, u32[]{:S(2)}, u32[]{:S(2)}) collective-permute-start(bf16[128,512]{1,0:T(8,128)(2,1)S(1)} %shard_map.136.refs_0_), channel_id=1, source_target_pairs={{0,1},{1,0},{2,3},{3,2},{4,5},{5,4},{6,7},{7,6},{8,9},{9,8},{10,11... | collective-permute-start | bytes 393224 | tf_op jit(solution)/shard_map/ppermute | solution.py:49
  55.2 8.1 %collective-permute-start.24 = (bf16[288,128]{1,0:T(8,128)(2,1)S(1)}, bf16[288,128]{1,0:T(8,128)(2,1)S(1)}, u32[]{:S(2)}, u32[]{:S(2)}) collective-permute-start(bf16[288,128]{1,0:T(8,128)(2,1)S(1)} %pad_maximum_fusion.1.refs_4_), channel_id=1, source_target_pairs={{0,4},{4,0},{8,12},{12,8},{16,20},{20,16},{24,28},{28,24},{1,5},{5... | collective-permute-start | bytes 221192 | tf_op jit(solution)/shard_map/ppermute | solution.py:49
  63.1 26.1 %collective-permute-start.33 = (bf16[512,1024]{1,0:T(8,128)(2,1)S(1)}, bf16[512,1024]{1,0:T(8,128)(2,1)}, u32[]{:S(2)}, u32[]{:S(2)}) collective-permute-start(bf16[512,1024]{1,0:T(8,128)(2,1)S(1)} %collective-permute-done.32.refs_10_), channel_id=1, source_target_pairs={{0,1},{1,0},{2,3},{3,2},{4,5},{5,4},{6,7},{7,6},{8,9},{9,8},{10,11... | collective-permute-start | bytes 3145736 | tf_op jit(solution)/shard_map/ppermute | solution.py:49
  64.6 12.9 %collective-permute-start.13 = (bf16[128,1536]{1,0:T(8,128)(2,1)S(1)}, bf16[128,1536]{1,0:T(8,128)(2,1)S(1)}, u32[]{:S(2)}, u32[]{:S(2)}) collective-permute-start(bf16[128,1536]{1,0:T(8,128)(2,1)S(1)} %pad_maximum_fusion.refs_0_), channel_id=1, source_target_pairs={{0,24},{4,28},{8,16},{12,20},{16,8},{20,12},{24,0},{28,4},{1,25},{... | collective-permute-start | bytes 1179656 | tf_op jit(solution)/shard_map/ppermute | solution.py:49
  67.1 18.4 %collective-permute-start.12 = (bf16[128,1536]{1,0:T(8,128)(2,1)S(1)}, bf16[128,1536]{1,0:T(8,128)(2,1)}, u32[]{:S(2)}, u32[]{:S(2)}) collective-permute-start(bf16[128,1536]{1,0:T(8,128)(2,1)S(1)} %pad_maximum_fusion.refs_0_), channel_id=1, source_target_pairs={{0,16},{4,20},{8,24},{12,28},{16,0},{20,4},{24,8},{28,12},{1,17},{... | collective-permute-start | bytes 1179656 | tf_op jit(solution)/shard_map/ppermute | solution.py:49
  67.6 17.9 %collective-permute-start.11 = (bf16[128,1536]{1,0:T(8,128)(2,1)S(1)}, bf16[128,1536]{1,0:T(8,128)(2,1)}, u32[]{:S(2)}, u32[]{:S(2)}) collective-permute-start(bf16[128,1536]{1,0:T(8,128)(2,1)S(1)} %pad_maximum_fusion.refs_0_), channel_id=1, source_target_pairs={{0,8},{4,12},{8,0},{12,4},{16,24},{20,28},{24,16},{28,20},{1,9},{5... | collective-permute-start | bytes 1179656 | tf_op jit(solution)/shard_map/ppermute | solution.py:49
  102.4 6.7 %collective-permute-start.36 = (bf16[144,512]{1,0:T(8,128)(2,1)S(1)}, bf16[144,512]{1,0:T(8,128)(2,1)S(1)}, u32[]{:S(2)}, u32[]{:S(2)}) collective-permute-start(bf16[144,512]{1,0:T(8,128)(2,1)S(1)} %add_convert_fusion.2), channel_id=1, source_target_pairs={{0,8},{4,12},{8,0},{12,4},{16,24},{20,28},{24,16},{28,20},{1,9},{5... | collective-permute-start | bytes 442376 | tf_op jit(solution)/shard_map/ppermute | solution.py:49
  103.9 8.8 %collective-permute-start.38 = (bf16[144,512]{1,0:T(8,128)(2,1)S(1)}, bf16[144,512]{1,0:T(8,128)(2,1)S(1)}, u32[]{:S(2)}, u32[]{:S(2)}) collective-permute-start(bf16[144,512]{1,0:T(8,128)(2,1)S(1)} %add_convert_fusion.1), channel_id=1, source_target_pairs={{0,16},{4,20},{8,24},{12,28},{16,0},{20,4},{24,8},{28,12},{1,17},{... | collective-permute-start | bytes 442376 | tf_op jit(solution)/shard_map/ppermute | solution.py:49
  104.6 9.1 %collective-permute-start.40 = (bf16[144,512]{1,0:T(8,128)(2,1)S(1)}, bf16[144,512]{1,0:T(8,128)(2,1)S(1)}, u32[]{:S(2)}, u32[]{:S(2)}) collective-permute-start(bf16[144,512]{1,0:T(8,128)(2,1)S(1)} %add_convert_fusion), channel_id=1, source_target_pairs={{0,24},{4,28},{8,16},{12,20},{16,8},{20,12},{24,0},{28,4},{1,25},{... | collective-permute-start | bytes 442376 | tf_op jit(solution)/shard_map/ppermute | solution.py:49
  105.9 12.3 %collective-permute-start.44 = (bf16[128,512]{1,0:T(8,128)(2,1)S(1)}, bf16[128,512]{1,0:T(8,128)(2,1)S(1)}, u32[]{:S(2)}, u32[]{:S(2)}) collective-permute-start(bf16[128,512]{1,0:T(8,128)(2,1)S(1)} %get-tuple-element.112), channel_id=1, source_target_pairs={{0,4},{4,0},{8,12},{12,8},{16,20},{20,16},{24,28},{28,24},{1,5},{5... | collective-permute-start | bytes 393224 | tf_op jit(solution)/shard_map/ppermute | solution.py:49
  107.4 9.6 %collective-permute-start.49 = (bf16[128,512]{1,0:T(8,128)(2,1)S(1)}, bf16[128,512]{1,0:T(8,128)(2,1)S(1)}, u32[]{:S(2)}, u32[]{:S(2)}) collective-permute-start(bf16[128,512]{1,0:T(8,128)(2,1)S(1)} %get-tuple-element.124), channel_id=1, source_target_pairs={{0,4},{4,0},{8,12},{12,8},{16,20},{20,16},{24,28},{28,24},{1,5},{5... | collective-permute-start | bytes 393224 | tf_op jit(solution)/shard_map/ppermute | solution.py:49
  109.1 16.4 %collective-permute-start.46 = (bf16[128,512]{1,0:T(8,128)(2,1)S(1)}, bf16[128,512]{1,0:T(8,128)(2,1)S(1)}, u32[]{:S(2)}, u32[]{:S(2)}) collective-permute-start(bf16[128,512]{1,0:T(8,128)(2,1)S(1)} %add_convert_fusion.6), channel_id=1, source_target_pairs={{0,8},{4,12},{8,0},{12,4},{16,24},{20,28},{24,16},{28,20},{1,9},{5... | collective-permute-start | bytes 393224 | tf_op jit(solution)/shard_map/ppermute | solution.py:49
  112.6 12.9 %collective-permute-start.48 = (bf16[128,512]{1,0:T(8,128)(2,1)S(1)}, bf16[128,512]{1,0:T(8,128)(2,1)S(1)}, u32[]{:S(2)}, u32[]{:S(2)}) collective-permute-start(bf16[128,512]{1,0:T(8,128)(2,1)S(1)} %add_convert_fusion.5), channel_id=1, source_target_pairs={{0,16},{4,20},{8,24},{12,28},{16,0},{20,4},{24,8},{28,12},{1,17},{... | collective-permute-start | bytes 393224 | tf_op jit(solution)/shard_map/ppermute | solution.py:49
  114.4 6.8 %collective-permute-start.43 = (bf16[288,128]{1,0:T(8,128)(2,1)S(1)}, bf16[288,128]{1,0:T(8,128)(2,1)S(1)}, u32[]{:S(2)}, u32[]{:S(2)}) collective-permute-start(bf16[288,128]{1,0:T(8,128)(2,1)S(1)} %get-tuple-element.108.refs_0_), channel_id=1, source_target_pairs={{0,3},{1,2},{2,1},{3,0},{4,7},{5,6},{6,5},{7,4},{8,11},{9,10},{10,... | collective-permute-start | bytes 221192 | tf_op jit(solution)/shard_map/ppermute | solution.py:49
  117.0 8.5 %collective-permute-start.50 = (bf16[128,512]{1,0:T(8,128)(2,1)S(1)}, bf16[128,512]{1,0:T(8,128)(2,1)S(1)}, u32[]{:S(2)}, u32[]{:S(2)}) collective-permute-start(bf16[128,512]{1,0:T(8,128)(2,1)S(1)} %add_convert_fusion.4), channel_id=1, source_target_pairs={{0,24},{4,28},{8,16},{12,20},{16,8},{20,12},{24,0},{28,4},{1,25},{... | collective-permute-start | bytes 393224 | tf_op jit(solution)/shard_map/ppermute | solution.py:49
  118.1 6.0 %collective-permute-start.42 = (bf16[288,128]{1,0:T(8,128)(2,1)S(1)}, bf16[288,128]{1,0:T(8,128)(2,1)S(1)}, u32[]{:S(2)}, u32[]{:S(2)}) collective-permute-start(bf16[288,128]{1,0:T(8,128)(2,1)S(1)} %get-tuple-element.108.refs_0_), channel_id=1, source_target_pairs={{0,2},{1,3},{2,0},{3,1},{4,6},{5,7},{6,4},{7,5},{8,10},{9,11},{10,... | collective-permute-start | bytes 221192 | tf_op jit(solution)/shard_map/ppermute | solution.py:49
  127.2 6.0 %collective-permute-start.56 = (bf16[544,128]{1,0:T(8,128)(2,1)S(1)}, bf16[544,128]{1,0:T(8,128)(2,1)S(1)}, u32[]{:S(2)}, u32[]{:S(2)}) collective-permute-start(bf16[544,128]{1,0:T(8,128)(2,1)S(1)} %get-tuple-element.130), channel_id=1, source_target_pairs={{0,24},{4,28},{8,16},{12,20},{16,8},{20,12},{24,0},{28,4},{1,25},{... | collective-permute-start | bytes 417800 | tf_op jit(solution)/shard_map/ppermute | solution.py:49
  (47 other events, 473.6 us)
